TPU v7x, 32 devices: a whole 2x2x4 slice. The times are simulated.
32 devices in a mesh: rep: 2 (over x), blk: 16 (over z, y, core).
Axes of the slice: x: 2, y: 2, z: 4, core: 2. Of those that a mesh axis runs over, the one named last changes fastest.
Arguments:
- amplitudes: bfloat16 [96, 1024, 1024], P('blk', 'rep'), may hold values from -6 to 6
- integrals: bfloat16 [96, 1024, 1024], P('blk', 'rep'), may hold values from -0.0017089844 to 0.0017089844
- fock_matrix: bfloat16 [1024, 1024], P('blk'), may hold values from -0.5 to 0.5
- hole_ladder: float32 [96, 96], P('blk'), may hold values from -1.75 to 1.75
- virt_irrep: int32 [1024], replicated, may hold values from 0 to 7
- occ_irrep: int32 [128], replicated, may hold values from 0 to 7
- pair_index: int32 [96, 2], replicated, may hold values from 0 to 127
- eps_occ: float32 [128], replicated, may hold values from -2 to -0.5
- eps_virt: float32 [1024], replicated, may hold values from 0.3 to 3
Outputs:
- update: bfloat16 [96, 1024, 1024], P('blk', 'rep')
All inputs are finite; a program needn't handle non-finite values.
Results may differ from a plain program's by a relative error of at most 0.0075.
Values may be sent and summed in bfloat16 or wider, within the bound.
No kernel may reach another device: no remote copies, remote signals or barrier semaphores. Data moves between devices by JAX's collectives and lax.ppermute only.
A program may use at most 128 MiB of HBM per device.

v0:
```python
import jax
import jax.numpy as jnp
from jax import lax
from jax.sharding import PartitionSpec as P


def table_lookup(index_col, table):
    iota_rows = jnp.arange(table.shape[0], dtype=jnp.int32)
    equal = index_col[:, None] == iota_rows[None, :]
    return jnp.sum(jnp.where(equal, table[None, :], jnp.zeros_like(table)[None, :]), axis=1)


def shards(
    amplitudes,
    integrals,
    fock_matrix,
    hole_ladder,
    virt_irrep,
    occ_irrep,
    pair_index,
    eps_occ,
    eps_virt,
):
    pair_dev = amplitudes.shape[0]
    virt_rows = amplitudes.shape[1]
    virt_all = amplitudes.shape[2]
    blk_count = lax.axis_size("blk")
    rows_each = virt_rows // blk_count
    pair_total = pair_dev * blk_count
    blk_id = lax.axis_index("blk")
    rep_id = lax.axis_index("rep")
    piece = lax.all_gather(fock_matrix, "blk", axis=0, tiled=True)
    kept = jnp.where(virt_irrep[:, None] == virt_irrep[None, :], piece, jnp.zeros_like(piece))
    fock_term = jnp.einsum(
        "pac,bc->pab", amplitudes, kept, preferred_element_type=jnp.float32
    ).astype(jnp.bfloat16)
    amp_virt, int_virt = (
        lax.all_to_all(amplitudes, "blk", split_axis=1, concat_axis=0, tiled=True),
        lax.all_to_all(integrals, "blk", split_axis=1, concat_axis=0, tiled=True),
    )
    amp_flat = amp_virt.reshape(pair_total, rows_each * virt_all)
    int_flat = int_virt.reshape(pair_total, rows_each * virt_all)
    partial_sums = jnp.dot(amp_flat, int_flat.T, preferred_element_type=jnp.float32)
    pair_irrep = jnp.bitwise_xor(
        table_lookup(pair_index[:, 0], occ_irrep), table_lookup(pair_index[:, 1], occ_irrep)
    )
    pair_energy = table_lookup(pair_index[:, 0], eps_occ) + table_lookup(pair_index[:, 1], eps_occ)
    summed = lax.psum(partial_sums, ("rep", "blk"))
    hole_all = lax.all_gather(hole_ladder, "blk", axis=0, tiled=True)
    same_pair = pair_irrep[:, None] == pair_irrep[None, :]
    ladder = jnp.where(same_pair, hole_all + summed, jnp.zeros_like(summed)).astype(jnp.bfloat16)
    ladder_virt = jnp.dot(ladder, amp_flat, preferred_element_type=jnp.float32)
    ladder_virt = ladder_virt.reshape(pair_total, rows_each, virt_all).astype(jnp.bfloat16)
    fock_virt = lax.all_to_all(fock_term, "blk", split_axis=1, concat_axis=0, tiled=True)
    row_energy = lax.dynamic_slice_in_dim(
        eps_virt, rep_id * virt_rows + blk_id * rows_each, rows_each
    )
    denom = pair_energy[:, None, None] - row_energy[None, :, None] - eps_virt[None, None, :]
    total = fock_virt.astype(jnp.float32) + ladder_virt.astype(jnp.float32)
    scaled = (total / denom).astype(jnp.bfloat16)
    return lax.all_to_all(scaled, "blk", split_axis=0, concat_axis=1, tiled=True)


def solution(mesh):
    return jax.shard_map(
        shards,
        mesh=mesh,
        in_specs=(
            P("blk", "rep", None),
            P("blk", "rep", None),
            P("blk", None),
            P("blk", None),
            P(),
            P(),
            P(),
            P(),
            P(),
        ),
        out_specs=P("blk", "rep", None),
        check_vma=False,
    )
```

profile of v0, /device:TPU:0, one launch (start us, length us, event | category | flops | bytes accessed | tf_op | source)
XLA Modules:
  0.0 885.7 jit_solution(12535383395865876245)
XLA Ops:
  6.5 9.7 %copy.41 = bf16[6,512,1024]{2,0,1:T(8,128)(2,1)} copy(bf16[6,512,1024]{2,1,0:T(8,128)(2,1)} %param.9) | data formatting | bytes 12582912 | tf_op args[0]
  16.3 7.4 all-to-all-start.1
  23.7 9.7 %copy.43 = bf16[6,512,1024]{2,0,1:T(8,128)(2,1)} copy(bf16[6,512,1024]{2,1,0:T(8,128)(2,1)} %param.10) | data formatting | bytes 12582912 | tf_op args[1]
  33.4 141.0 %all-to-all-done.1 = bf16[6,512,1024]{2,0,1:T(8,128)(2,1)} async-done(((bf16[6,512,1024]{2,0,1:T(8,128)(2,1)}), bf16[6,512,1024]{2,0,1:T(8,128)(2,1)}, u32[]{:S(2)}, u32[]{:S(2)}) %all-to-all-start.1) | async-done | bytes 6291488 | tf_op jit(solution)/shard_map/all_to_all | solution.py:38
  174.4 36.5 %all-to-all-start.2 = ((bf16[6,512,1024]{2,0,1:T(8,128)(2,1)}), bf16[6,512,1024]{2,0,1:T(8,128)(2,1)}, u32[]{:S(2)}, u32[]{:S(2)}) async-start(bf16[6,512,1024]{2,0,1:T(8,128)(2,1)} %copy.43), calls=%async_computation.2 | async-start | bytes 16777216 | tf_op jit(solution)/shard_map/all_to_all | solution.py:39
  211.7 135.0 %all-gather.3.cloned.1.call-done = bf16[1024,1024]{1,0:T(8,128)(2,1)} async-done(((bf16[64,1024]{1,0:T(8,128)(2,1)}), bf16[1024,1024]{1,0:T(8,128)(2,1)}) %all-gather.3.cloned.1.call-update) | async-done | bytes 2097168 | tf_op jit(solution)/shard_map/all_gather | solution.py:32
  346.7 11.2 %convert_bitcast_fusion.1 = bf16[6,512,1024]{1,2,0:T(8,128)(2,1)} fusion(bf16[6,512,1024]{2,1,0:T(8,128)(2,1)} %param.9, bf16[1024,1024]{1,0:T(8,128)(2,1)} %all-gather.3.cloned.1.call-done, s32[1024]{0:T(1024)S(1)} %copy-done.5), kind=kOutput, calls=%fused_computation.7 | convolution fusion | flops 6447693824 | bytes 14684160 | tf_op jit(solution)/shard_map/pac,bc->pab/dot_general | solution.py:34
  357.8 12.1 %copy.38 = bf16[6,512,1024]{2,0,1:T(8,128)(2,1)} copy(bf16[6,512,1024]{1,2,0:T(8,128)(2,1)} %convert_bitcast_fusion.1) | data formatting | bytes 12582912 | tf_op jit(solution)/shard_map/convert_element_type | solution.py:36
  370.0 4.4 all-to-all-done.2
  374.3 36.5 %all-to-all-start = ((bf16[6,512,1024]{2,0,1:T(8,128)(2,1)}), bf16[6,512,1024]{2,0,1:T(8,128)(2,1)}, u32[]{:S(2)}, u32[]{:S(2)}) async-start(bf16[6,512,1024]{2,0,1:T(8,128)(2,1)} %copy.38), calls=%async_computation | async-start | bytes 16777216 | tf_op jit(solution)/shard_map/all_to_all | solution.py:54
  410.8 151.9 %all-gather = f32[16,6,96]{2,1,0:T(8,128)S(1)} all-gather(f32[1,6,96]{2,1,0:T(8,128)S(1)} %bitcast.56), channel_id=1, replica_groups=mesh['rep'=2,'blk'=16] {'blk'}, dimensions={0}, use_global_device_ids=true | all-gather | bytes 39168 | tf_op jit(solution)/shard_map/all_gather | solution.py:49
  563.3 7.6 copy.42
  570.9 4.3 copy.50
  575.2 20.6 %copy.44 = bf16[6,16,32,1024]{3,2,0,1:T(8,128)(2,1)} copy(bf16[6,16,32,1024]{3,0,2,1:T(8,128)(2,1)} %bitcast.10) | data formatting | bytes 12582912 | tf_op jit(solution)/shard_map/all_to_all | solution.py:39
  595.8 6.8 copy.51
  602.6 1.8 fusion.19
  604.4 80.8 %psum.7 = f32[96,96]{1,0:T(8,128)S(1)} all-reduce(f32[96,96]{1,0:T(8,128)S(1)} %fusion.19), channel_id=1, replica_groups=mesh['rep'=2,'blk'=16] {'rep','blk'}, use_global_device_ids=true, to_apply=%region_2.3 | all-reduce | flops 9216 | bytes 73728 | tf_op jit(solution)/shard_map/psum | solution.py:48
  685.3 6.9 copy.39
  692.2 6.1 convert_bitcast_fusion
  698.3 12.1 %copy.40 = f32[16,6,32,1024]{3,2,1,0:T(8,128)} copy(f32[16,6,32,1024]{3,2,0,1:T(8,128)} %convert_bitcast_fusion) | data formatting | bytes 25165824 | tf_op jit(solution)/shard_map/convert_element_type | solution.py:59
  710.4 18.7 %fusion.1 = bf16[96,32,1024]{2,0,1:T(8,128)(2,1)S(1)} fusion(f32[96,32,1024]{2,1,0:T(8,128)} %bitcast.55, f32[1024]{0:T(1024)S(1)} %copy-done.6, f32[96,32]{0,1:T(8,128)S(1)} %broadcast_subtract_fusion, f32[96,96]{1,0:T(8,128)S(1)} %reshape.70, f32[96,96]{1,0:T(8,128)S(1)} %psum.7, s32[96]{0:T(128)S(1)} %xor.11, bf16[12,8,32,1024]{3,2,1,0:T(8,128)(2,1)S(1)} %bitcast.49), kind=kOutput, calls=%fused_computation.3 | convolution fusion | flops 622891008 | bytes 25256320 | tf_op jit(solution)/shard_map/dot_general | solution.py:52
  729.1 3.5 copy.47
  732.7 142.4 %all_to_all.57 = bf16[96,32,1024]{2,1,0:T(8,128)(2,1)S(1)} all-to-all(bf16[96,32,1024]{2,1,0:T(8,128)(2,1)S(1)} %copy.47), channel_id=1, replica_groups=mesh['rep'=2,'blk'=16] {'blk'}, dimensions={0} | all-to-all | bytes 12582912 | tf_op jit(solution)/shard_map/all_to_all | solution.py:61
  875.1 3.4 copy.48
  (30 shorter events, 1.3 us)
Async XLA Ops:
  16.3 158.2 %all-to-all-start.1 = ((bf16[6,512,1024]{2,0,1:T(8,128)(2,1)}), bf16[6,512,1024]{2,0,1:T(8,128)(2,1)}, u32[]{:S(2)}, u32[]{:S(2)}) async-start(bf16[6,512,1024]{2,0,1:T(8,128)(2,1)} %copy.41), calls=%async_computation.1 | async-start | bytes 16777216 | tf_op jit(solution)/shard_map/all_to_all | solution.py:38
  33.4 313.2 %copy-start.5 = (s32[1024]{0:T(1024)S(1)}, s32[1024]{0:T(1024)}, u32[]{:S(2)}) copy-start(s32[1024]{0:T(1024)} %param.13) | copy-start | bytes 12292
  174.4 199.9 %all-to-all-start.2 = ((bf16[6,512,1024]{2,0,1:T(8,128)(2,1)}), bf16[6,512,1024]{2,0,1:T(8,128)(2,1)}, u32[]{:S(2)}, u32[]{:S(2)}) async-start(bf16[6,512,1024]{2,0,1:T(8,128)(2,1)} %copy.43), calls=%async_computation.2 | async-start | bytes 16777216 | tf_op jit(solution)/shard_map/all_to_all | solution.py:39
  211.0 135.7 %all-gather.3.cloned.1.call-start = ((), (), s32[]{:S(2)}) async-start(), calls=%async_computation.4 | async-start | bytes 2228224 | tf_op jit(solution)/shard_map/all_gather | solution.py:32
  369.9 40.9 %copy-start.1 = (f32[6,96]{1,0:T(8,128)S(1)}, f32[6,96]{1,0:T(8,128)}, u32[]{:S(2)}) copy-start(f32[6,96]{1,0:T(8,128)} %param.12) | copy-start | bytes 6916
  369.9 192.8 %copy-start.6 = (f32[1024]{0:T(1024)S(1)}, f32[1024]{0:T(1024)}, u32[]{:S(2)}) copy-start(f32[1024]{0:T(1024)} %param.17) | copy-start | bytes 12292
  369.9 192.9 %copy-start.2 = (s32[96,2]{0,1:T(2,128)S(1)}, s32[96,2]{0,1:T(2,128)}, u32[]{:S(2)}) copy-start(s32[96,2]{0,1:T(2,128)} %param.15) | copy-start | bytes 2308
  369.9 192.9 %copy-start.3 = (f32[128]{0:T(128)S(1)}, f32[128]{0:T(128)}, u32[]{:S(2)}) copy-start(f32[128]{0:T(128)} %param.16) | copy-start | bytes 1540
  370.0 193.1 %copy-start.4 = (s32[128]{0:T(128)S(1)}, s32[128]{0:T(128)}, u32[]{:S(2)}) copy-start(s32[128]{0:T(128)} %param.14) | copy-start | bytes 1540
  374.3 310.9 %all-to-all-start = ((bf16[6,512,1024]{2,0,1:T(8,128)(2,1)}), bf16[6,512,1024]{2,0,1:T(8,128)(2,1)}, u32[]{:S(2)}, u32[]{:S(2)}) async-start(bf16[6,512,1024]{2,0,1:T(8,128)(2,1)} %copy.38), calls=%async_computation | async-start | bytes 16777216 | tf_op jit(solution)/shard_map/all_to_all | solution.py:54
  570.9 4.3 copy-start
  692.1 18.2 %slice-start = ((s8[6291456]{0:T(1024)(128)(4,1)}), s8[4194304]{0:T(1024)(128)(4,1)S(1)}, s32[]{:S(2)}) async-start(s8[6291456]{0:T(1024)(128)(4,1)} %bitcast.47), calls=%async_computation.5 | async-start | bytes 8388608
  698.3 12.1 %slice-start.1 = ((s8[6291456]{0:T(1024)(128)(4,1)}), s8[2097152]{0:T(1024)(128)(4,1)S(1)}, s32[]{:S(2)}) async-start(s8[6291456]{0:T(1024)(128)(4,1)} %bitcast.47), calls=%async_computation.6 | async-start | bytes 4194304
Sparse Core Ops, SparseCore 0:
  214.0 132.6 all-gather.2
where the time goes:
time: 895 us; the launch traced here: 886 us
  blocking collectives  375 us (42%)
  waiting for transfers between devices  281 us (31%)
  local copies, waits for them, and re-layouts  96.9 us (11%)
  starting transfers between devices  80.5 us (9%)
  matrix products  31.7 us (4%)
  between operations  13.9 us (2%)
    all_gather x1, blocking collectives, shards(): hole_all = lax.all_gather(hole_ladder, 'blk', axis=0, tiled=True)  152 us
    all_to_all x1, blocking collectives, shards(): lax.all_to_all(scaled, 'blk', split_axis=0, concat_axis=1, tiled=True)  142 us
    all_to_all x1, waiting for transfers between devices, shards(): lax.all_to_all(amplitudes, 'blk', split_axis=1, concat_axis=0, tiled=True)  141 us
    all_gather x1, waiting for transfers between devices, shards(): piece = lax.all_gather(fock_matrix, 'blk', axis=0, tiled=True)  135 us
    psum x1, blocking collectives, shards(): summed = lax.psum(partial_sums, ('rep', 'blk'))  80.8 us
    all_to_all x1, starting transfers between devices, shards(): lax.all_to_all(integrals, 'blk', split_axis=1, concat_axis=0, tiled=True)  36.5 us
    all_to_all x1, starting transfers between devices, shards(): lax.all_to_all(fock_term, 'blk', split_axis=1, concat_axis=0, tiled=True)  36.5 us
    unnamed x23, local copies, waits for them, and re-layouts  30.6 us
  transfers between devices with their start and end apart: 4, of which 3 were waited for; matrix products, arithmetic and copies ran while one was open for 8% of the time, Pallas kernels for 0%

commit v1 on v0

--- a/solution.py
+++ b/solution.py
@@ -51,14 +51,12 @@
     ladder = jnp.where(same_pair, hole_all + summed, jnp.zeros_like(summed)).astype(jnp.bfloat16)
     ladder_virt = jnp.dot(ladder, amp_flat, preferred_element_type=jnp.float32)
     ladder_virt = ladder_virt.reshape(pair_total, rows_each, virt_all).astype(jnp.bfloat16)
-    fock_virt = lax.all_to_all(fock_term, "blk", split_axis=1, concat_axis=0, tiled=True)
-    row_energy = lax.dynamic_slice_in_dim(
-        eps_virt, rep_id * virt_rows + blk_id * rows_each, rows_each
-    )
-    denom = pair_energy[:, None, None] - row_energy[None, :, None] - eps_virt[None, None, :]
-    total = fock_virt.astype(jnp.float32) + ladder_virt.astype(jnp.float32)
-    scaled = (total / denom).astype(jnp.bfloat16)
-    return lax.all_to_all(scaled, "blk", split_axis=0, concat_axis=1, tiled=True)
+    ladder_term = lax.all_to_all(ladder_virt, "blk", split_axis=0, concat_axis=1, tiled=True)
+    row_energy = lax.dynamic_slice_in_dim(eps_virt, rep_id * virt_rows, virt_rows)
+    own_energy = lax.dynamic_slice_in_dim(pair_energy, blk_id * pair_dev, pair_dev)
+    denom = own_energy[:, None, None] - row_energy[None, :, None] - eps_virt[None, None, :]
+    total = fock_term.astype(jnp.float32) + ladder_term.astype(jnp.float32)
+    return (total / denom).astype(jnp.bfloat16)
 
 
 def solution(mesh):

time: 895 us -> 720 us (0.80)
  the two profiles are of different devices: /device:TPU:0 before, /device:TPU:15 now
where the time goes in v1:
time: 720 us; the launch traced here: 713 us
  waiting for transfers between devices  322 us (45%)
  blocking collectives  230 us (32%)
  local copies, waits for them, and re-layouts  88.5 us (12%)
  matrix products  29.1 us (4%)
  starting transfers between devices  19.6 us (3%)
  between operations  13.7 us (2%)
  other arithmetic  9.45 us (1%)
    all_gather x1, blocking collectives, shards(): hole_all = lax.all_gather(hole_ladder, 'blk', axis=0, tiled=True)  192 us
    all_to_all x1, waiting for transfers between devices, shards(): lax.all_to_all(integrals, 'blk', split_axis=1, concat_axis=0, tiled=True)  173 us
    all_to_all x1, waiting for transfers between devices, shards(): lax.all_to_all(ladder_virt, 'blk', split_axis=0, concat_axis=1, tiled=True)  149 us
    psum x1, blocking collectives, shards(): summed = lax.psum(partial_sums, ('rep', 'blk'))  38.5 us
    unnamed x21, local copies, waits for them, and re-layouts  33.4 us
    convert_element_type x2, local copies, waits for them, and re-layouts, shards(): total = fock_term.astype(jnp.float32) + ladder_term.astype(jnp.float32)  24.4 us
  transfers between devices with their start and end apart: 4, of which 2 were waited for; matrix products, arithmetic and copies ran while one was open for 8% of the time, Pallas kernels for 0%

profile of v1, /device:TPU:15, one launch (start us, length us, event | category | flops | bytes accessed | tf_op | source)
XLA Modules:
  0.0 713.0 jit_solution(2578415629179384418)
XLA Ops:
  6.5 9.7 %copy.30 = bf16[6,512,1024]{2,0,1:T(8,128)(2,1)} copy(bf16[6,512,1024]{2,1,0:T(8,128)(2,1)} %param.10) | data formatting | bytes 12582912 | tf_op args[1]
  16.2 6.6 all-to-all-start.1
  22.8 9.7 %copy.28 = bf16[6,512,1024]{2,0,1:T(8,128)(2,1)} copy(bf16[6,512,1024]{2,1,0:T(8,128)(2,1)} %param.9) | data formatting | bytes 12582912 | tf_op args[0]
  32.5 172.6 %all-to-all-done.1 = bf16[6,512,1024]{2,0,1:T(8,128)(2,1)} async-done(((bf16[6,512,1024]{2,0,1:T(8,128)(2,1)}), bf16[6,512,1024]{2,0,1:T(8,128)(2,1)}, u32[]{:S(2)}, u32[]{:S(2)}) %all-to-all-start.1) | async-done | bytes 6291488 | tf_op jit(solution)/shard_map/all_to_all | solution.py:39
  205.1 4.9 all-to-all-start
  210.1 191.9 %all-gather = f32[16,6,96]{2,1,0:T(8,128)S(1)} all-gather(f32[1,6,96]{2,1,0:T(8,128)S(1)} %bitcast.52), channel_id=1, replica_groups=mesh['rep'=2,'blk'=16] {'blk'}, dimensions={0}, use_global_device_ids=true | all-gather | bytes 39168 | tf_op jit(solution)/shard_map/all_gather | solution.py:49
  402.0 0.2 select_reduce_fusion.2
  402.2 7.6 %copy.31 = bf16[6,16,32,1024]{3,2,0,1:T(8,128)(2,1)S(1)} copy(bf16[6,16,32,1024]{3,0,2,1:T(8,128)(2,1)} %bitcast.7) | data formatting | bytes 12582912 | tf_op jit(solution)/shard_map/all_to_all | solution.py:39
  409.7 6.9 copy.39
  416.7 8.1 %copy.29 = bf16[6,16,32,1024]{3,2,0,1:T(8,128)(2,1)S(1)} copy(bf16[6,16,32,1024]{3,0,2,1:T(8,128)(2,1)} %bitcast.5) | data formatting | bytes 12582912 | tf_op jit(solution)/shard_map/all_to_all | solution.py:38
  424.7 7.0 copy.38
  431.8 4.6 fusion.20
  436.3 38.5 %psum.7 = f32[96,96]{1,0:T(8,128)S(1)} all-reduce(f32[96,96]{1,0:T(8,128)S(1)} %fusion.20), channel_id=1, replica_groups=mesh['rep'=2,'blk'=16] {'rep','blk'}, use_global_device_ids=true, to_apply=%region_2.3 | all-reduce | flops 9216 | bytes 73728 | tf_op jit(solution)/shard_map/psum | solution.py:48
  474.8 10.6 %fusion.5 = bf16[96,32,1024]{2,0,1:T(8,128)(2,1)S(1)} fusion(f32[96,96]{1,0:T(8,128)S(1)} %reshape.66, f32[96,96]{1,0:T(8,128)S(1)} %psum.7, s32[96]{0:T(128)S(1)} %xor.11, bf16[12,8,32,1024]{3,2,1,0:T(8,128)(2,1)} %bitcast.47), kind=kOutput, calls=%fused_computation.8 | convolution fusion | flops 607162368 | bytes 12657024 | tf_op jit(solution)/shard_map/dot_general | solution.py:52
  485.5 6.2 copy.33
  491.7 8.1 %all-to-all-start.2 = ((bf16[96,32,1024]{2,1,0:T(8,128)(2,1)}), bf16[96,32,1024]{2,1,0:T(8,128)(2,1)}, u32[]{:S(2)}, u32[]{:S(2)}) async-start(bf16[96,32,1024]{2,1,0:T(8,128)(2,1)} %copy.33), calls=%async_computation.2 | async-start | bytes 12582912 | tf_op jit(solution)/shard_map/all_to_all | solution.py:54
  499.9 0.7 all-gather.3.cloned.1.call-update
  500.6 0.2 select_reduce_fusion
  501.0 148.9 %all-to-all-done.2 = bf16[96,32,1024]{2,1,0:T(8,128)(2,1)} async-done(((bf16[96,32,1024]{2,1,0:T(8,128)(2,1)}), bf16[96,32,1024]{2,1,0:T(8,128)(2,1)}, u32[]{:S(2)}, u32[]{:S(2)}) %all-to-all-start.2) | async-done | bytes 6291488 | tf_op jit(solution)/shard_map/all_to_all | solution.py:54
  650.0 9.0 %convert_bitcast_fusion = f32[6,16,32,1024]{3,2,0,1:T(8,128)} fusion(bf16[16,6,32,1024]{3,2,1,0:T(8,128)(2,1)} %bitcast.14), kind=kLoop, calls=%fused_computation | loop fusion | flops 3145728 | bytes 18874368 | tf_op jit(solution)/shard_map/convert_element_type | solution.py:58
  659.0 11.8 %copy.34 = f32[6,16,32,1024]{3,2,1,0:T(8,128)} copy(f32[6,16,32,1024]{3,2,0,1:T(8,128)} %convert_bitcast_fusion) | data formatting | bytes 25165824 | tf_op jit(solution)/shard_map/convert_element_type | solution.py:58
  670.8 12.6 %copy.35 = f32[6,512,1024]{1,2,0:T(8,128)} copy(f32[6,512,1024]{2,1,0:T(8,128)} %bitcast.48) | data formatting | bytes 25165824 | tf_op jit(solution)/shard_map/convert_element_type | solution.py:58
  683.4 13.9 %fusion.1 = bf16[6,512,1024]{1,2,0:T(8,128)(2,1)} fusion(f32[6,512,1024]{1,2,0:T(8,128)} %copy.35, f32[1024]{0:T(1024)S(1)} %copy-done.3, f32[6,512]{1,0:T(8,128)S(1)} %broadcast_subtract_fusion, bf16[6,512,1024]{2,1,0:T(8,128)(2,1)} %param.9, bf16[1024,1024]{1,0:T(8,128)(2,1)} %all-gather.3.cloned.1.call-done, s32[1024]{0:T(1024)S(1)} %copy-done.7), kind=kOutput, calls=%fused_computation.3 | convolution fusion | flops 6463422464 | bytes 27283456 | tf_op jit(solution)/shard_map/pac,bc->pab/dot_general | solution.py:34
  697.4 8.6 %copy.36 = bf16[6,512,1024]{2,1,0:T(8,128)(2,1)} copy(bf16[6,512,1024]{1,2,0:T(8,128)(2,1)} %fusion.1) | data formatting | bytes 12582912 | tf_op jit(solution)/shard_map/convert_element_type | solution.py:59
  (26 shorter events, 0.3 us)
Async XLA Ops:
  16.2 188.9 %all-to-all-start.1 = ((bf16[6,512,1024]{2,0,1:T(8,128)(2,1)}), bf16[6,512,1024]{2,0,1:T(8,128)(2,1)}, u32[]{:S(2)}, u32[]{:S(2)}) async-start(bf16[6,512,1024]{2,0,1:T(8,128)(2,1)} %copy.30), calls=%async_computation.1 | async-start | bytes 16777216 | tf_op jit(solution)/shard_map/all_to_all | solution.py:39
  32.5 177.5 %copy-start.2 = (f32[6,96]{1,0:T(8,128)S(1)}, f32[6,96]{1,0:T(8,128)}, u32[]{:S(2)}) copy-start(f32[6,96]{1,0:T(8,128)} %param.12) | copy-start | bytes 6916
  32.5 369.4 %copy-start.4 = (s32[96,2]{0,1:T(2,128)S(1)}, s32[96,2]{0,1:T(2,128)}, u32[]{:S(2)}) copy-start(s32[96,2]{0,1:T(2,128)} %param.15) | copy-start | bytes 2308
  32.5 369.4 %copy-start.5 = (s32[128]{0:T(128)S(1)}, s32[128]{0:T(128)}, u32[]{:S(2)}) copy-start(s32[128]{0:T(128)} %param.14) | copy-start | bytes 1540
  205.1 211.5 %all-to-all-start = ((bf16[6,512,1024]{2,0,1:T(8,128)(2,1)}), bf16[6,512,1024]{2,0,1:T(8,128)(2,1)}, u32[]{:S(2)}, u32[]{:S(2)}) async-start(bf16[6,512,1024]{2,0,1:T(8,128)(2,1)} %copy.28), calls=%async_computation | async-start | bytes 16777216 | tf_op jit(solution)/shard_map/all_to_all | solution.py:38
  424.7 7.0 copy-start
  424.7 7.0 copy-start.1
  491.7 8.9 %copy-start.6 = (f32[128]{0:T(128)S(1)}, f32[128]{0:T(128)}, u32[]{:S(2)}) copy-start(f32[128]{0:T(128)} %param.16) | copy-start | bytes 1540
  491.7 9.2 %copy-start.3 = (f32[1024]{0:T(1024)S(1)}, f32[1024]{0:T(1024)}, u32[]{:S(2)}) copy-start(f32[1024]{0:T(1024)} %param.17) | copy-start | bytes 12292
  491.7 158.2 %all-to-all-start.2 = ((bf16[96,32,1024]{2,1,0:T(8,128)(2,1)}), bf16[96,32,1024]{2,1,0:T(8,128)(2,1)}, u32[]{:S(2)}, u32[]{:S(2)}) async-start(bf16[96,32,1024]{2,1,0:T(8,128)(2,1)} %copy.33), calls=%async_computation.2 | async-start | bytes 12582912 | tf_op jit(solution)/shard_map/all_to_all | solution.py:54
  499.9 183.5 %all-gather.3.cloned.1.call-start = ((), (), s32[]{:S(2)}) async-start(), calls=%async_computation.3 | async-start | bytes 2228224 | tf_op jit(solution)/shard_map/all_gather | solution.py:32
  670.8 12.6 %copy-start.7 = (s32[1024]{0:T(1024)S(1)}, s32[1024]{0:T(1024)}, u32[]{:S(2)}) copy-start(s32[1024]{0:T(1024)} %param.13) | copy-start | bytes 12292
Sparse Core Ops, SparseCore 0:
  502.9 113.3 all-gather.2

commit v2 on v1

--- a/solution.py
+++ b/solution.py
@@ -1,7 +1,19 @@
+import functools
+
 import jax
 import jax.numpy as jnp
 from jax import lax
+from jax.experimental import pallas as pl
+from jax.experimental.pallas import tpu as pltpu
 from jax.sharding import PartitionSpec as P
+
+PLANES = 4
+INNER = 4
+CHUNK = 16
+CHUNKS = 8
+WIDE = 5
+LANES = 128
+VMEM_BYTES = 56 * 1024 * 1024
 
 
 def table_lookup(index_col, table):
@@ -10,7 +22,7 @@
     return jnp.sum(jnp.where(equal, table[None, :], jnp.zeros_like(table)[None, :]), axis=1)
 
 
-def shards(
+def spread_plan(
     amplitudes,
     integrals,
     fock_matrix,
@@ -59,9 +71,424 @@
     return (total / denom).astype(jnp.bfloat16)
 
 
+def plane_perm(step, first, last):
+    return [
+        (plane * INNER + at, (plane + step) * INNER + at)
+        for plane in range(first, last + 1)
+        for at in range(INNER)
+    ]
+
+
+def inner_perm(flip, planes=range(PLANES)):
+    return [(p * INNER + at, p * INNER + (at ^ flip)) for p in planes for at in range(INNER)]
+
+
+def outward_perm(flip):
+    return [
+        (p * INNER + at, q * INNER + (at ^ flip)) for p, q in ((1, 0), (2, 3)) for at in range(INNER)
+    ]
+
+
+def sixth(index):
+    return sum((index >= edge).astype(jnp.int32) for edge in (6, 12, 18))
+
+
+def pair_at(index, me, pair_dev):
+    group = sixth(index)
+    return pair_dev * (me ^ group) + index - pair_dev * group
+
+
+def place_sources(plane, own, plus, minus, chunk):
+    wide = chunk < WIDE
+    table = {
+        1: {0: plus[chunk], 1: own, 2: minus[chunk], 3: minus[CHUNKS + chunk]},
+        2: {0: plus[CHUNKS + chunk], 1: plus[chunk], 2: own, 3: minus[chunk]},
+    }
+    if wide:
+        table[0] = {0: own, 1: minus[chunk], 2: minus[WIDE + chunk], 3: minus[2 * WIDE + chunk]}
+        table[3] = {0: plus[2 * WIDE + chunk], 1: plus[WIDE + chunk], 2: plus[chunk], 3: own}
+    return table
+
+
+def source_steps(chunk):
+    steps = [chunk, CHUNKS + chunk]
+    if chunk < WIDE:
+        steps += [WIDE + chunk, 2 * WIDE + chunk]
+    return sorted(set(steps))
+
+
+def chunk_refs(chunk, own, plus, minus):
+    steps = source_steps(chunk)
+    return [own[chunk]] + [plus[s] for s in steps] + [minus[s] for s in steps]
+
+
+def ref_table(chunk, refs):
+    steps = source_steps(chunk)
+    count = len(steps)
+    plus = dict(zip(steps, refs[1 : 1 + count]))
+    minus = dict(zip(steps, refs[1 + count : 1 + 2 * count]))
+    return place_sources(None, refs[0], plus, minus, chunk)
+
+
+def here():
+    blk = lax.axis_index("blk")
+    return lax.div(blk, INNER), lax.rem(blk, INNER)
+
+
+def blocked_sum(left, right):
+    rows, depth = left.shape[0], left.shape[1]
+    cols = right.shape[0]
+    gram = lax.dot_general(
+        left.reshape(rows * depth, -1),
+        right.reshape(cols * depth, -1),
+        (((1,), (1,)), ((), ())),
+        preferred_element_type=jnp.float32,
+    )
+    row_id = lax.broadcasted_iota(jnp.int32, gram.shape, 0)
+    col_id = lax.broadcasted_iota(jnp.int32, gram.shape, 1)
+    same = (row_id & (depth - 1)) == (col_id & (depth - 1))
+    return jnp.where(same, gram, 0.0).reshape(rows, depth, cols * depth).sum(axis=1)
+
+
+def exact_dot(left, right):
+    return jnp.dot(left, right, preferred_element_type=jnp.float32, precision=lax.Precision.HIGHEST)
+
+
+def pad_rows(array):
+    extra = LANES - array.shape[0]
+    return jnp.concatenate([array, jnp.zeros((extra, array.shape[1]), array.dtype)], axis=0)
+
+
+def pair_kernel(chunk, last, pair_dev, *refs):
+    wide = chunk < WIDE
+    count = 1 + 2 * len(source_steps(chunk))
+    table = ref_table(chunk, refs[:count])
+    refs = refs[count:]
+    if wide:
+        (int_own,), refs = refs[:1], refs[1:]
+        int_near = None
+    else:
+        (int_own, int_plus, int_minus), refs = refs[:3], refs[3:]
+        int_near = {1: int_plus, 2: int_minus}
+    acc_in, refs = refs[0], refs[1:]
+    if last:
+        hole_ref, refs = refs[0], refs[1:]
+    out_ref, amp, ints, total, sems = refs
+    plane, me = here()
+    rows = amp.shape[1]
+    total[...] = acc_in[...]
+    for z, sources in table.items():
+
+        @pl.when(plane == z)
+        def _():
+            copies = [pltpu.make_async_copy(int_own, ints.at[0], sems.at[PLANES])]
+            if int_near is not None:
+                copies.append(pltpu.make_async_copy(int_near[z], ints.at[1], sems.at[PLANES + 1]))
+            for p in range(PLANES):
+                copies.append(pltpu.make_async_copy(sources[p], amp.at[p], sems.at[p]))
+            for copy in copies:
+                copy.start()
+            for copy in copies:
+                copy.wait()
+            for p in range(PLANES):
+                for side in range(1 if wide else 2):
+                    total[side, p * rows : (p + 1) * rows] += blocked_sum(amp[p], ints[side])
+
+    if not last:
+        out_ref[...] = total[...]
+        return
+    lanes = total.shape[2]
+    placed = hole_ref[...]
+    summed = jnp.zeros((total.shape[1], LANES), jnp.float32)
+    near = jnp.where(plane < 2, 0, PLANES - 1)
+    row_id = lax.broadcasted_iota(jnp.int32, (lanes, LANES), 0) // CHUNK
+    col_id = lax.broadcasted_iota(jnp.int32, (lanes, LANES), 1)
+    pair_id = pair_at(row_id, me, pair_dev)
+    for side, at in ((0, plane), (1, near)):
+        chosen = (col_id == pair_id + at * rows).astype(jnp.float32)
+        summed += exact_dot(total[side], chosen)
+    out_id = lax.broadcasted_iota(jnp.int32, (total.shape[1], LANES), 0)
+    in_id = lax.broadcasted_iota(jnp.int32, (total.shape[1], LANES), 1)
+    in_plane = sum((in_id >= p * rows).astype(jnp.int32) for p in range(1, PLANES))
+    in_pair = pair_at(in_id - in_plane * rows, me, pair_dev) + in_plane * rows
+    chosen = (out_id == in_pair).astype(jnp.float32)
+    out_ref[...] = placed + exact_dot(chosen, pad_rows(summed))
+
+
+def add_pair_sums(chunk, own, plus, minus, int_own, acc, hole, pair_dev):
+    last = hole is not None
+    rows, depth, width = own[chunk].shape
+    operands = chunk_refs(chunk, own, plus, minus) + [int_own[chunk]]
+    if chunk >= WIDE:
+        operands += [plus[CHUNKS + chunk - WIDE], minus[CHUNKS + chunk - WIDE]]
+    far = len(operands)
+    operands.append(acc)
+    if last:
+        operands.append(hole)
+    shape = (PLANES * rows, LANES) if last else acc.shape
+    flops = 2 * PLANES * (rows * depth) ** 2 * width * (1 if chunk < WIDE else 2)
+    return pl.pallas_call(
+        functools.partial(pair_kernel, chunk, last, pair_dev),
+        out_shape=jax.ShapeDtypeStruct(shape, jnp.float32),
+        in_specs=[pl.BlockSpec(memory_space=pl.ANY)] * far
+        + [pl.BlockSpec(memory_space=pltpu.VMEM)] * (len(operands) - far),
+        out_specs=pl.BlockSpec(memory_space=pltpu.VMEM),
+        scratch_shapes=[
+            pltpu.VMEM((PLANES, rows, depth, width), jnp.bfloat16),
+            pltpu.VMEM((2, rows, depth, width), jnp.bfloat16),
+            pltpu.VMEM(acc.shape, jnp.float32),
+            pltpu.SemaphoreType.DMA((PLANES + 2,)),
+        ],
+        compiler_params=pltpu.CompilerParams(vmem_limit_bytes=VMEM_BYTES),
+        cost_estimate=pl.CostEstimate(flops=flops, bytes_accessed=5 * rows * depth * width * 2, transcendentals=0),
+        name=f"pair_sums_{chunk}",
+    )(*operands)
+
+
+def ladder_kernel(chunks, pair_dev, *refs):
+    wide = chunks[0] < WIDE
+    tables = []
+    for chunk in chunks:
+        count = 1 + 2 * len(source_steps(chunk))
+        tables.append(ref_table(chunk, refs[:count]))
+        refs = refs[count:]
+    sum_ref, mask_ref = refs[:2]
+    outs = refs[2 : 2 + (INNER if wide else 2 * INNER)]
+    amp, spread, sems = refs[2 + len(outs) :]
+    plane, me = here()
+    rows, depth, width = amp.shape[2:]
+    block = rows * depth
+
+    def work(z):
+        copies = [
+            [pltpu.make_async_copy(table[z][p], amp.at[n, p], sems.at[n, p]) for p in range(PLANES)]
+            for n, table in enumerate(tables)
+        ]
+        for group in copies:
+            for copy in group:
+                copy.start()
+        ladder = jnp.where(mask_ref[...] > 0, sum_ref[...], 0.0).astype(jnp.bfloat16)
+        ladder = pad_rows(ladder)
+        near = 0 if z < 2 else PLANES - 1
+        col = lax.broadcasted_iota(jnp.int32, (LANES, PLANES * block), 1) // depth
+        col_plane = sum((col >= p * rows).astype(jnp.int32) for p in range(1, PLANES))
+        col_pair = pair_at(col - col_plane * rows, me, pair_dev) + col_plane * rows
+        col_one = (lax.broadcasted_iota(jnp.int32, col.shape, 0) == col_pair).astype(jnp.bfloat16)
+        row = lax.broadcasted_iota(jnp.int32, (block, LANES), 0) // depth
+        row_pair = pair_at(row, me, pair_dev)
+        for side, at in enumerate((z,) if wide else (z, near)):
+            row_one = (lax.broadcasted_iota(jnp.int32, row.shape, 1) == row_pair + at * rows).astype(jnp.bfloat16)
+            picked = jnp.dot(row_one, ladder, preferred_element_type=jnp.float32).astype(jnp.bfloat16)
+            full = jnp.dot(picked, col_one, preferred_element_type=jnp.float32)
+            left = lax.broadcasted_iota(jnp.int32, full.shape, 0) & (depth - 1)
+            right = lax.broadcasted_iota(jnp.int32, full.shape, 1) & (depth - 1)
+            spread[side] = jnp.where(left == right, full, 0.0).astype(jnp.bfloat16)
+        for n, group in enumerate(copies):
+            for copy in group:
+                copy.wait()
+            columns = amp[n].reshape(PLANES * block, width)
+            for side in range(1 if wide else 2):
+                term = jnp.dot(spread[side], columns, preferred_element_type=jnp.float32).astype(jnp.bfloat16)
+                term = term.reshape(INNER, pair_dev, depth, width)
+                for flip in range(INNER):
+                    outs[side * INNER + flip][:, n * depth : (n + 1) * depth, :] = term[flip]
+
+    for z in tables[0]:
+        pl.when(plane == z)(functools.partial(work, z))
+
+
+def ladder_terms(chunks, own, plus, minus, summed, mask, pair_dev):
+    rows, depth, width = own[chunks[0]].shape
+    wide = chunks[0] < WIDE
+    operands = [ref for chunk in chunks for ref in chunk_refs(chunk, own, plus, minus)]
+    far = len(operands)
+    operands += [summed, mask]
+    sides = 1 if wide else 2
+    block = rows * depth
+    return pl.pallas_call(
+        functools.partial(ladder_kernel, chunks, pair_dev),
+        out_shape=[jax.ShapeDtypeStruct((pair_dev, len(chunks) * depth, width), jnp.bfloat16)] * (sides * INNER),
+        in_specs=[pl.BlockSpec(memory_space=pl.ANY)] * far + [pl.BlockSpec(memory_space=pltpu.VMEM)] * 2,
+        out_specs=[pl.BlockSpec(memory_space=pltpu.VMEM)] * (sides * INNER),
+        scratch_shapes=[
+            pltpu.VMEM((len(chunks), PLANES, rows, depth, width), jnp.bfloat16),
+            pltpu.VMEM((sides, block, PLANES * block), jnp.bfloat16),
+            pltpu.SemaphoreType.DMA((len(chunks), PLANES)),
+        ],
+        compiler_params=pltpu.CompilerParams(vmem_limit_bytes=VMEM_BYTES),
+        cost_estimate=pl.CostEstimate(
+            flops=2 * PLANES * block * block * width * sides * len(chunks),
+            bytes_accessed=(PLANES + sides) * block * width * 2 * len(chunks),
+            transcendentals=0,
+        ),
+        name=f"ladder_{chunks[0]}",
+    )(*operands)
+
+
+def scale_kernel(pick, base_ref, energy_ref, *refs):
+    if pick:
+        fock, inside, outside, row_energy, col_energy, out = refs
+        plane, _ = here()
+        middle = (plane == 1) | (plane == 2)
+    else:
+        fock, inside, row_energy, col_energy, out = refs
+    for p in range(fock.shape[0]):
+        ladder = inside[p]
+        if pick:
+            ladder = jnp.where(middle, ladder, outside[p])
+        denom = energy_ref[p] - row_energy[...] - col_energy[...]
+        total = fock[p].astype(jnp.float32) + ladder.astype(jnp.float32)
+        out[p] = (total / denom).astype(out.dtype)
+
+
+def add_and_scale(buffer, pieces, base, own_energy, row_energy, col_energy):
+    pair_dev, _, width = buffer.shape
+    steps = pieces[0].shape[1] // CHUNK
+    place = pl.BlockSpec((pair_dev, CHUNK, width), lambda i, b, e: (0, b[0] + i, 0))
+    piece = pl.BlockSpec((pair_dev, CHUNK, width), lambda i, b, e: (0, i, 0))
+    return pl.pallas_call(
+        functools.partial(scale_kernel, len(pieces) > 1),
+        out_shape=jax.ShapeDtypeStruct(buffer.shape, buffer.dtype),
+        grid_spec=pltpu.PrefetchScalarGridSpec(
+            num_scalar_prefetch=2,
+            grid=(steps,),
+            in_specs=[place]
+            + [piece] * len(pieces)
+            + [
+                pl.BlockSpec((CHUNK, 1), lambda i, b, e: (b[0] + i, 0)),
+                pl.BlockSpec((1, width), lambda i, b, e: (0, 0)),
+            ],
+            out_specs=place,
+        ),
+        input_output_aliases={2: 0},
+        compiler_params=pltpu.CompilerParams(vmem_limit_bytes=VMEM_BYTES),
+        cost_estimate=pl.CostEstimate(
+            flops=5 * steps * CHUNK * pair_dev * width,
+            bytes_accessed=(2 + len(pieces)) * steps * CHUNK * pair_dev * width * 2,
+            transcendentals=0,
+        ),
+        name="add_and_scale",
+    )(base, own_energy, buffer, *pieces, row_energy, col_energy)
+
+
+def exchange_inner(array, groups, me):
+    found = {}
+    for first, end in groups:
+        parts = []
+        for flip in range(INNER):
+            part = lax.dynamic_slice_in_dim(array[:, :, first:end], me ^ flip, 1, axis=1)[:, 0]
+            if flip:
+                part = lax.ppermute(part, "blk", inner_perm(flip))
+            parts.append(part)
+        for chunk in range(first, end):
+            found[chunk] = jnp.concatenate([part[:, chunk - first] for part in parts], axis=0)
+    return found
+
+
+def line_plan(
+    amplitudes,
+    integrals,
+    fock_matrix,
+    hole_ladder,
+    virt_irrep,
+    occ_irrep,
+    pair_index,
+    eps_occ,
+    eps_virt,
+):
+    pair_dev, virt_rows, virt_all = amplitudes.shape
+    pair_total = pair_dev * PLANES * INNER
+    blk_id = lax.axis_index("blk")
+    rep_id = lax.axis_index("rep")
+    plane, me = here()
+    split = (pair_dev, INNER, CHUNKS, CHUNK, virt_all)
+    own = exchange_inner(amplitudes.reshape(split), ((0, 1), (1, 3), (3, CHUNKS)), me)
+    int_own = exchange_inner(integrals.reshape(split), ((WIDE, CHUNKS), (0, WIDE)), me)
+
+    piece = lax.all_gather(fock_matrix, "blk", axis=0, tiled=True)
+    kept = jnp.where(virt_irrep[:, None] == virt_irrep[None, :], piece, jnp.zeros_like(piece))
+    fock_term = jnp.einsum(
+        "pac,bc->pab", amplitudes, kept, preferred_element_type=jnp.float32
+    ).astype(jnp.bfloat16)
+
+    narrow = CHUNKS - WIDE
+    got = {1: {}, -1: {}}
+    for step in range(2 * CHUNKS):
+        for way in (1, -1):
+            far = plane if way == 1 else PLANES - 1 - plane
+            have = got[way]
+            first, last = 0, 2
+            if step < WIDE:
+                send = own[step]
+            elif step < CHUNKS:
+                send = jnp.where(far == 2, have[step - WIDE], own[step])
+            else:
+                send = have[step - CHUNKS]
+                if step < 2 * WIDE:
+                    send = jnp.where(far == 2, have[step - WIDE], send)
+                elif step < 3 * WIDE:
+                    send = jnp.where(far == 2, have[step - 2 * WIDE + CHUNKS], send)
+                else:
+                    last = 1
+                if step < CHUNKS + narrow:
+                    send = jnp.where(far == 0, int_own[WIDE + step - CHUNKS], send)
+                else:
+                    first = 1
+            if way == 1:
+                perm = plane_perm(1, first, last)
+            else:
+                perm = plane_perm(-1, PLANES - 1 - last, PLANES - 1 - first)
+            have[step] = lax.ppermute(send, "blk", perm)
+    plus, minus = got[1], got[-1]
+
+    hole = jnp.zeros((pair_total, LANES), jnp.float32)
+    hole_rows = jnp.pad(hole_ladder, ((0, 0), (0, LANES - pair_total)))
+    hole = lax.dynamic_update_slice_in_dim(hole, hole_rows, blk_id * pair_dev, axis=0)
+    hole = jnp.where(rep_id == 0, hole, jnp.zeros_like(hole))
+    acc = jnp.zeros((2, pair_total, pair_dev * INNER * CHUNK), jnp.float32)
+    order = sorted(range(CHUNKS), key=lambda c: (2 * WIDE if c < WIDE else CHUNKS) + c)
+    for chunk in order:
+        extra = hole if chunk == order[-1] else None
+        acc = add_pair_sums(chunk, own, plus, minus, int_own, acc, extra, pair_dev)
+    summed = acc + lax.ppermute(acc, "blk", inner_perm(1))
+    summed = summed + lax.ppermute(summed, "rep", [(0, 1), (1, 0)])
+    for flip in (2, 4, 8):
+        summed = summed + lax.ppermute(summed, "blk", [(i, i ^ flip) for i in range(PLANES * INNER)])
+
+    pair_irrep = jnp.bitwise_xor(
+        table_lookup(pair_index[:, 0], occ_irrep), table_lookup(pair_index[:, 1], occ_irrep)
+    )
+    pair_energy = table_lookup(pair_index[:, 0], eps_occ) + table_lookup(pair_index[:, 1], eps_occ)
+    mask = (pair_irrep[:, None] == pair_irrep[None, :]).astype(jnp.float32)
+    mask = jnp.pad(mask, ((0, 0), (0, LANES - pair_total)))
+    own_energy = lax.dynamic_slice_in_dim(pair_energy, blk_id * pair_dev, pair_dev)
+    row_energy = lax.dynamic_slice_in_dim(eps_virt, rep_id * virt_rows, virt_rows)[:, None]
+    col_energy = eps_virt[None, :]
+
+    narrow_terms = ladder_terms(tuple(range(WIDE, CHUNKS)), own, plus, minus, summed, mask, pair_dev)
+    wide_terms = ladder_terms(tuple(range(WIDE)), own, plus, minus, summed, mask, pair_dev)
+    outside, inside, every = {}, {}, {}
+    for flip in (2, 3, 1, 0):
+        outside[flip] = lax.ppermute(narrow_terms[INNER + flip], "blk", outward_perm(flip))
+    for flip in (2, 3, 1, 0):
+        every[flip], inside[flip] = wide_terms[flip], narrow_terms[flip]
+        if flip:
+            inside[flip] = lax.ppermute(inside[flip], "blk", inner_perm(flip, (1, 2)))
+            every[flip] = lax.ppermute(every[flip], "blk", inner_perm(flip))
+    update = fock_term
+    for flip in range(INNER):
+        base = jnp.reshape((me ^ flip) * CHUNKS, (1,)).astype(jnp.int32)
+        update = add_and_scale(update, [every[flip]], base, own_energy, row_energy, col_energy)
+        update = add_and_scale(
+            update, [inside[flip], outside[flip]], base + WIDE, own_energy, row_energy, col_energy
+        )
+    return update
+
+
 def solution(mesh):
+    fits = mesh.shape["blk"] == PLANES * INNER and mesh.shape["rep"] == 2
     return jax.shard_map(
-        shards,
+        line_plan if fits else spread_plan,
         mesh=mesh,
         in_specs=(
             P("blk", "rep", None),

time: 720 us -> 565 us (0.78)
  the two profiles are of different devices: /device:TPU:15 before, /device:TPU:0 now
where the time goes in v2:
time: 565 us; the launch traced here: 554 us
  waiting for transfers between devices  224 us (40%)
  starting transfers between devices  129 us (23%)
  Pallas kernels  92.2 us (16%)
  local copies, waits for them, and re-layouts  53.4 us (9%)
  other arithmetic  28.3 us (5%)
  between operations  15.3 us (3%)
  matrix products  11.4 us (2%)
    ppermute x32, waiting for transfers between devices, line_plan(): have[step] = lax.ppermute(send, 'blk', perm)  116 us
    ppermute x32, starting transfers between devices, line_plan(): have[step] = lax.ppermute(send, 'blk', perm)  73.6 us
    ppermute x15, waiting for transfers between devices, exchange_inner(): part = lax.ppermute(part, 'blk', inner_perm(flip))  63.1 us
    pallas_call x8, Pallas kernels, add_and_scale(): pl.pallas_call(functools.partial(scale_kernel, len(pieces) > 1), out_shap...  36.5 us
    pallas_call x8, Pallas kernels, add_pair_sums(): pl.pallas_call(functools.partial(pair_kernel, chunk, last, pair_dev), out...  35.5 us
    ppermute x4, waiting for transfers between devices, line_plan(): lax.ppermute(narrow_terms[INNER + flip], 'blk', outward_perm(flip))  32.9 us
    ppermute x3, starting transfers between devices, line_plan(): lax.ppermute(summed, 'blk', [(i, i ^ flip) for i in range(PLANES * INNER)])  31 us
    unnamed x178, local copies, waits for them, and re-layouts  21.9 us
  transfers between devices with their start and end apart: 63, of which 24 were waited for; matrix products, arithmetic and copies ran while one was open for 15% of the time, Pallas kernels for 16%

profile of v2, /device:TPU:0, one launch (start us, length us, event | category | flops | bytes accessed | tf_op | source)
XLA Modules:
  0.0 553.6 jit_solution(4701027795914497807)
XLA Ops:
  47.1 50.9 %collective-permute-done.15 = bf16[6,2,16,1024]{3,2,0,1:T(8,128)(2,1)S(1)} collective-permute-done((bf16[6,2,16,1024]{3,2,0,1:T(8,128)(2,1)}, bf16[6,2,16,1024]{3,2,0,1:T(8,128)(2,1)S(1)}, u32[]{:S(2)}, u32[]{:S(2)}) %collective-permute-start.15) | collective-permute-done | bytes 393248 | tf_op jit(solution)/shard_map/ppermute | solution.py:381
  118.7 7.9 %collective-permute-done.10 = bf16[6,3,16,1024]{3,2,0,1:T(8,128)(2,1)S(1)} collective-permute-done((bf16[6,3,16,1024]{3,2,0,1:T(8,128)(2,1)}, bf16[6,3,16,1024]{3,2,0,1:T(8,128)(2,1)S(1)}, u32[]{:S(2)}, u32[]{:S(2)}) %collective-permute-start.10) | collective-permute-done | bytes 589856 | tf_op jit(solution)/shard_map/ppermute | solution.py:381
  133.3 10.8 %collective-permute-done.31.refs_5_.refs_41_ = bf16[24,16,1024]{2,1,0:T(8,128)(2,1)S(1)} collective-permute-done((bf16[24,16,1024]{2,1,0:T(8,128)(2,1)}, bf16[24,16,1024]{2,1,0:T(8,128)(2,1)S(1)}, u32[]{:S(2)}, u32[]{:S(2)}) %collective-permute-start.31) | collective-permute-done | bytes 786464 | tf_op jit(solution)/shard_map/ppermute | solution.py:441
  180.1 14.2 %collective-permute-done.32.refs_7_.refs_6_.refs_16_.refs_42_ = bf16[24,16,1024]{2,1,0:T(8,128)(2,1)S(1)} collective-permute-done((bf16[24,16,1024]{2,1,0:T(8,128)(2,1)}, bf16[24,16,1024]{2,1,0:T(8,128)(2,1)S(1)}, u32[]{:S(2)}, u32[]{:S(2)}) %collective-permute-start.32) | collective-permute-done | bytes 786464 | tf_op jit(solution)/shard_map/ppermute | solution.py:441
  203.4 9.7 %collective-permute-done.27.refs_3_.refs_2_.refs_6_.refs_12_.refs_38_ = bf16[24,16,1024]{2,1,0:T(8,128)(2,1)S(1)} collective-permute-done((bf16[24,16,1024]{2,1,0:T(8,128)(2,1)S(1)}, bf16[24,16,1024]{2,1,0:T(8,128)(2,1)S(1)}, u32[]{:S(2)}, u32[]{:S(2)}) %collective-permute-start.27) | collective-permute-done | bytes 786464 | tf_op jit(solution)/shard_map/ppermute | solution.py:441
  226.7 9.8 %collective-permute-done.21.refs_7_.refs_6_.refs_33_ = bf16[24,16,1024]{2,1,0:T(8,128)(2,1)S(1)} collective-permute-done((bf16[24,16,1024]{2,1,0:T(8,128)(2,1)S(1)}, bf16[24,16,1024]{2,1,0:T(8,128)(2,1)S(1)}, u32[]{:S(2)}, u32[]{:S(2)}) %collective-permute-start.21) | collective-permute-done | bytes 786464 | tf_op jit(solution)/shard_map/ppermute | solution.py:441
  239.3 7.4 %collective-permute-done.12.refs_3_.refs_2_.refs_6_.refs_29_ = bf16[24,16,1024]{2,1,0:T(8,128)(2,1)S(1)} collective-permute-done((bf16[24,16,1024]{2,1,0:T(8,128)(2,1)S(1)}, bf16[24,16,1024]{2,1,0:T(8,128)(2,1)S(1)}, u32[]{:S(2)}, u32[]{:S(2)}) %collective-permute-start.12) | collective-permute-done | bytes 786464 | tf_op jit(solution)/shard_map/ppermute | solution.py:441
  258.2 12.1 %collective-permute-done.23.refs_8_.refs_7_.refs_25_ = bf16[24,16,1024]{2,1,0:T(8,128)(2,1)S(1)} collective-permute-done((bf16[24,16,1024]{2,1,0:T(8,128)(2,1)S(1)}, bf16[24,16,1024]{2,1,0:T(8,128)(2,1)S(1)}, u32[]{:S(2)}, u32[]{:S(2)}) %collective-permute-start.23) | collective-permute-done | bytes 786464 | tf_op jit(solution)/shard_map/ppermute | solution.py:441
  272.6 6.4 %collective-permute-start.25 = (bf16[24,16,1024]{2,1,0:T(8,128)(2,1)S(1)}, bf16[24,16,1024]{2,1,0:T(8,128)(2,1)S(1)}, u32[]{:S(2)}, u32[]{:S(2)}) collective-permute-start(bf16[24,16,1024]{2,1,0:T(8,128)(2,1)S(1)} %get-tuple-element.99), channel_id=1, source_target_pairs={{0,4},{1,5},{2,6},{3,7},{4,8},{5,9},{6,10},{7,11},{8,12},{9,13},{1... | collective-permute-start | bytes 2359304 | tf_op jit(solution)/shard_map/ppermute | solution.py:441
  280.5 6.7 %collective-permute-done.33.refs_8_.refs_7_.refs_17_.refs_34_ = bf16[24,16,1024]{2,1,0:T(8,128)(2,1)S(1)} collective-permute-done((bf16[24,16,1024]{2,1,0:T(8,128)(2,1)S(1)}, bf16[24,16,1024]{2,1,0:T(8,128)(2,1)S(1)}, u32[]{:S(2)}, u32[]{:S(2)}) %collective-permute-start.33) | collective-permute-done | bytes 786464 | tf_op jit(solution)/shard_map/ppermute | solution.py:441
  291.1 12.9 %collective-permute-done.30.refs_6_.refs_3_.refs_15_.refs_8_ = bf16[24,16,1024]{2,1,0:T(8,128)(2,1)S(1)} collective-permute-done((bf16[24,16,1024]{2,1,0:T(8,128)(2,1)S(1)}, bf16[24,16,1024]{2,1,0:T(8,128)(2,1)S(1)}, u32[]{:S(2)}, u32[]{:S(2)}) %collective-permute-start.30) | collective-permute-done | bytes 786464 | tf_op jit(solution)/shard_map/ppermute | solution.py:441
  308.9 12.0 %collective-permute-done.37.refs_8_.refs_7_.refs_26_.refs_43_ = bf16[24,16,1024]{2,1,0:T(8,128)(2,1)S(1)} collective-permute-done((bf16[24,16,1024]{2,1,0:T(8,128)(2,1)S(1)}, bf16[24,16,1024]{2,1,0:T(8,128)(2,1)S(1)}, u32[]{:S(2)}, u32[]{:S(2)}) %collective-permute-start.37) | collective-permute-done | bytes 786464 | tf_op jit(solution)/shard_map/ppermute | solution.py:441
  324.8 12.9 %collective-permute-done.36.refs_6_.refs_3_.refs_24_.refs_13_ = bf16[24,16,1024]{2,1,0:T(8,128)(2,1)S(1)} collective-permute-done((bf16[24,16,1024]{2,1,0:T(8,128)(2,1)S(1)}, bf16[24,16,1024]{2,1,0:T(8,128)(2,1)S(1)}, u32[]{:S(2)}, u32[]{:S(2)}) %collective-permute-start.36) | collective-permute-done | bytes 786464 | tf_op jit(solution)/shard_map/ppermute | solution.py:441
  341.0 5.7 %pair_sums_0.1.refs_10_ = f32[2,96,384]{2,1,0:T(8,128)} custom-call(bf16[24,16,1024]{2,1,0:T(8,128)(2,1)} %copy-done.17, bf16[24,16,1024]{2,1,0:T(8,128)(2,1)} %copy-done.22, bf16[24,16,1024]{2,1,0:T(8,128)(2,1)} %copy-done.14, bf16[24,16,1024]{2,1,0:T(8,128)(2,1)} %copy-done.9, bf16[24,16,1024]{2,1,0:T(8,128)(2,1)} %copy-done.1, ...), custom_call_target="tpu_custom_call" | custom-call | flops 1207959552 | bytes 3932160 | tf_op jit(solution)/shard_map/pair_sums_0/pallas_call | solution.py:230
  346.7 6.1 %pair_sums_1.1.refs_10_ = f32[2,96,384]{2,1,0:T(8,128)} custom-call(bf16[24,16,1024]{2,1,0:T(8,128)(2,1)} %copy-done.18, bf16[24,16,1024]{2,1,0:T(8,128)(2,1)} %copy-done.21, bf16[24,16,1024]{2,1,0:T(8,128)(2,1)} %copy-done.16, bf16[24,16,1024]{2,1,0:T(8,128)(2,1)} %copy-done.7, bf16[24,16,1024]{2,1,0:T(8,128)(2,1)} %copy-done.3, ...), custom_call_target="tpu_custom_call" | custom-call | flops 1207959552 | bytes 3932160 | tf_op jit(solution)/shard_map/pair_sums_1/pallas_call | solution.py:230
  355.3 5.7 %pair_sums_2.1.refs_10_ = f32[2,96,384]{2,1,0:T(8,128)} custom-call(bf16[24,16,1024]{2,1,0:T(8,128)(2,1)} %copy-done.19, bf16[24,16,1024]{2,1,0:T(8,128)(2,1)} %copy-done.25, bf16[24,16,1024]{2,1,0:T(8,128)(2,1)} %copy-done.27, bf16[24,16,1024]{2,1,0:T(8,128)(2,1)} %copy-done.1, bf16[24,16,1024]{2,1,0:T(8,128)(2,1)} %copy-done.5, ...), custom_call_target="tpu_custom_call" | custom-call | flops 1207959552 | bytes 3932160 | tf_op jit(solution)/shard_map/pair_sums_2/pallas_call | solution.py:230
  361.9 5.9 %pair_sums_3.1.refs_8_ = f32[2,96,384]{2,1,0:T(8,128)} custom-call(bf16[24,16,1024]{2,1,0:T(8,128)(2,1)} %pad_maximum_fusion.3.refs_0_.refs_27_, bf16[24,16,1024]{2,1,0:T(8,128)(2,1)} %copy-done.23, bf16[24,16,1024]{2,1,0:T(8,128)(2,1)} %copy-done.9, bf16[24,16,1024]{2,1,0:T(8,128)(2,1)} %copy-done.3, bf16[24,16,1024]{2,1,0:T(8,128)(2,1)} %copy-done.29, ...), custom_call_target="tpu_custom_call" | custom-call | flops 1207959552 | bytes 3932160 | tf_op jit(solution)/shard_map/pair_sums_3/pallas_call | solution.py:230
  370.9 5.9 %pair_sums_4.1.refs_8_ = f32[2,96,384]{2,1,0:T(8,128)} custom-call(bf16[24,16,1024]{2,1,0:T(8,128)(2,1)} %pad_maximum_fusion.9.refs_0_.refs_36_, bf16[24,16,1024]{2,1,0:T(8,128)(2,1)} %copy-done.11, bf16[24,16,1024]{2,1,0:T(8,128)(2,1)} %copy-done.7, bf16[24,16,1024]{2,1,0:T(8,128)(2,1)} %copy-done.5, ...), custom_call_target="tpu_custom_call" | custom-call | flops 1207959552 | bytes 3932160 | tf_op jit(solution)/shard_map/pair_sums_4/pallas_call | solution.py:230
  393.0 25.3 %collective-permute-start.50 = (f32[96,128]{1,0:T(8,128)S(1)}, f32[96,128]{1,0:T(8,128)S(1)}, u32[]{:S(2)}, u32[]{:S(2)}) collective-permute-start(f32[96,128]{1,0:T(8,128)S(1)} %add.79), channel_id=1, source_target_pairs={{0,4},{1,5},{2,6},{3,7},{4,0},{5,1},{6,2},{7,3},{8,12},{9,13},{10,... | collective-permute-start | bytes 147464 | tf_op jit(solution)/shard_map/ppermute | solution.py:456
  427.1 12.2 %ladder_0.1 = (bf16[6,80,1024]{2,1,0:T(8,128)(2,1)}, bf16[6,80,1024]{2,1,0:T(8,128)(2,1)}, bf16[6,80,1024]{2,1,0:T(8,128)(2,1)}, bf16[6,80,1024]{2,1,0:T(8,128)(2,1)}) custom-call(bf16[24,16,1024]{2,1,0:T(8,128)(2,1)} %copy-done.17, bf16[24,16,1024]{2,1,0:T(8,128)(2,1)} %copy-done.22, bf16[24,16,1024]{2,1,0:T(8,128)(2,1)} %copy-done.14, ...), custom_call_target="tpu_custom_call" | custom-call | flops 6039797760 | bytes 19660800 | tf_op jit(solution)/shard_map/ladder_0/pallas_call | solution.py:308
  439.7 7.9 %ladder_5.1 = (bf16[6,48,1024]{2,1,0:T(8,128)(2,1)}, bf16[6,48,1024]{2,1,0:T(8,128)(2,1)}, bf16[6,48,1024]{2,1,0:T(8,128)(2,1)}, bf16[6,48,1024]{2,1,0:T(8,128)(...) custom-call(bf16[24,16,1024]{2,1,0:T(8,128)(2,1)} %get-tuple-element, ...), custom_call_target="tpu_custom_call" | custom-call | flops 7247757312 | bytes 14155776 | tf_op jit(solution)/shard_map/ladder_5/pallas_call | solution.py:308
  452.6 23.9 %collective-permute-done.52.refs_2_ = bf16[6,48,1024]{2,1,0:T(8,128)(2,1)} collective-permute-done((bf16[6,48,1024]{2,1,0:T(8,128)(2,1)}, bf16[6,48,1024]{2,1,0:T(8,128)(2,1)}, u32[]{:S(2)}, u32[]{:S(2)}) %collective-permute-start.52) | collective-permute-done | bytes 589856 | tf_op jit(solution)/shard_map/ppermute | solution.py:472
  479.3 9.1 %collective-permute-done.55.refs_2_ = bf16[6,48,1024]{2,1,0:T(8,128)(2,1)S(1)} collective-permute-done((bf16[6,48,1024]{2,1,0:T(8,128)(2,1)}, bf16[6,48,1024]{2,1,0:T(8,128)(2,1)S(1)}, u32[]{:S(2)}, u32[]{:S(2)}) %collective-permute-start.55) | collective-permute-done | bytes 589856 | tf_op jit(solution)/shard_map/ppermute | solution.py:472
  494.4 11.4 %convert_bitcast_fusion.refs_0_ = bf16[6,512,1024]{2,1,0:T(8,128)(2,1)} fusion(bf16[6,512,1024]{2,1,0:T(8,128)(2,1)} %param.9, bf16[1024,1024]{1,0:T(8,128)(2,1)} %all-gather.2.cloned.1.call-done, s32[1024]{0:T(1024)S(1)} %copy-done.78), kind=kOutput, calls=%fused_computation | convolution fusion | flops 6447693824 | bytes 14684160 | tf_op jit(solution)/shard_map/pac,bc->pab/dot_general | solution.py:410
  (367 shorter events, 245.6 us)
Async XLA Ops:
  6.5 487.8 %all-gather.2.cloned.1.call-start = ((), (), s32[]{:S(2)}) async-start(), calls=%async_computation | async-start | bytes 2228224 | tf_op jit(solution)/shard_map/all_gather | solution.py:408
  31.7 68.6 %collective-permute-start.4 = (bf16[6,5,16,1024]{3,2,0,1:T(8,128)(2,1)}, bf16[6,5,16,1024]{3,2,0,1:T(8,128)(2,1)}, u32[]{:S(2)}, u32[]{:S(2)}) collective-permute-start(bf16[6,5,16,1024]{3,2,0,1:T(8,128)(2,1)} %bitcast.219), channel_id=1, source_target_pairs={{0,1},{1,0},{2,3},{3,2},{4,5},{5,4},{6,7},{7,6},{8,9},{9,8},{10,11... | collective-permute-start | bytes 2949128 | tf_op jit(solution)/shard_map/ppermute | solution.py:381
  40.0 64.2 %collective-permute-start.5 = (bf16[6,5,16,1024]{3,2,0,1:T(8,128)(2,1)}, bf16[6,5,16,1024]{3,2,0,1:T(8,128)(2,1)S(1)}, u32[]{:S(2)}, u32[]{:S(2)}) collective-permute-start(bf16[6,5,16,1024]{3,2,0,1:T(8,128)(2,1)} %bitcast.194), channel_id=1, source_target_pairs={{0,2},{1,3},{2,0},{3,1},{4,6},{5,7},{6,4},{7,5},{8,10},{9,11},{10,... | collective-permute-start | bytes 2949128 | tf_op jit(solution)/shard_map/ppermute | solution.py:381
  40.2 64.8 %collective-permute-start.6 = (bf16[6,5,16,1024]{3,2,0,1:T(8,128)(2,1)S(1)}, bf16[6,5,16,1024]{3,2,0,1:T(8,128)(2,1)S(1)}, u32[]{:S(2)}, u32[]{:S(2)}) collective-permute-start(bf16[6,5,16,1024]{3,2,0,1:T(8,128)(2,1)S(1)} %bitcast.218), channel_id=1, source_target_pairs={{0,3},{1,2},{2,1},{3,0},{4,7},{5,6},{6,5},{7,4},{8,11},{9,10},{10,... | collective-permute-start | bytes 2949128 | tf_op jit(solution)/shard_map/ppermute | solution.py:381
  42.6 55.4 %collective-permute-start.15 = (bf16[6,2,16,1024]{3,2,0,1:T(8,128)(2,1)}, bf16[6,2,16,1024]{3,2,0,1:T(8,128)(2,1)S(1)}, u32[]{:S(2)}, u32[]{:S(2)}) collective-permute-start(bf16[6,2,16,1024]{3,2,0,1:T(8,128)(2,1)} %bitcast.223), channel_id=1, source_target_pairs={{0,3},{1,2},{2,1},{3,0},{4,7},{5,6},{6,5},{7,4},{8,11},{9,10},{10,... | collective-permute-start | bytes 1179656 | tf_op jit(solution)/shard_map/ppermute | solution.py:381
  45.0 63.1 %collective-permute-start.8 = (bf16[6,3,16,1024]{3,2,0,1:T(8,128)(2,1)}, bf16[6,3,16,1024]{3,2,0,1:T(8,128)(2,1)S(1)}, u32[]{:S(2)}, u32[]{:S(2)}) collective-permute-start(bf16[6,3,16,1024]{3,2,0,1:T(8,128)(2,1)} %bitcast.222), channel_id=1, source_target_pairs={{0,1},{1,0},{2,3},{3,2},{4,5},{5,4},{6,7},{7,6},{8,9},{9,8},{10,11... | collective-permute-start | bytes 1769480 | tf_op jit(solution)/shard_map/ppermute | solution.py:381
  104.1 64.0 %collective-permute-start.44 = (bf16[6,5,16,1024]{3,2,0,1:T(8,128)(2,1)}, bf16[6,5,16,1024]{3,2,0,1:T(8,128)(2,1)}, u32[]{:S(2)}, u32[]{:S(2)}) collective-permute-start(bf16[6,5,16,1024]{3,2,0,1:T(8,128)(2,1)} %bitcast.191), channel_id=1, source_target_pairs={{0,1},{1,0},{2,3},{3,2},{4,5},{5,4},{6,7},{7,6},{8,9},{9,8},{10,11... | collective-permute-start | bytes 2949128 | tf_op jit(solution)/shard_map/ppermute | solution.py:381
  148.0 46.3 %collective-permute-start.32 = (bf16[24,16,1024]{2,1,0:T(8,128)(2,1)}, bf16[24,16,1024]{2,1,0:T(8,128)(2,1)S(1)}, u32[]{:S(2)}, u32[]{:S(2)}) collective-permute-start(bf16[24,16,1024]{2,1,0:T(8,128)(2,1)} %get-tuple-element.102), channel_id=1, source_target_pairs={{4,0},{5,1},{6,2},{7,3},{8,4},{9,5},{10,6},{11,7},{12,8},{13,9},{1... | collective-permute-start | bytes 2359304 | tf_op jit(solution)/shard_map/ppermute | solution.py:441
  155.9 41.4 %collective-permute-start.3 = (bf16[24,16,1024]{2,1,0:T(8,128)(2,1)S(1)}, bf16[24,16,1024]{2,1,0:T(8,128)(2,1)S(1)}, u32[]{:S(2)}, u32[]{:S(2)}) collective-permute-start(bf16[24,16,1024]{2,1,0:T(8,128)(2,1)S(1)} %pad_maximum_fusion.refs_0_), channel_id=1, source_target_pairs={{0,4},{1,5},{2,6},{3,7},{4,8},{5,9},{6,10},{7,11},{8,12},{9,13},{1... | collective-permute-start | bytes 2359304 | tf_op jit(solution)/shard_map/ppermute | solution.py:441
  168.2 44.9 %collective-permute-start.27 = (bf16[24,16,1024]{2,1,0:T(8,128)(2,1)S(1)}, bf16[24,16,1024]{2,1,0:T(8,128)(2,1)S(1)}, u32[]{:S(2)}, u32[]{:S(2)}) collective-permute-start(bf16[24,16,1024]{2,1,0:T(8,128)(2,1)S(1)} %get-tuple-element.98), channel_id=1, source_target_pairs={{0,4},{1,5},{2,6},{3,7},{4,8},{5,9},{6,10},{7,11},{8,12},{9,13},{1... | collective-permute-start | bytes 2359304 | tf_op jit(solution)/shard_map/ppermute | solution.py:441
  220.8 50.3 %collective-permute-start.19 = (bf16[24,16,1024]{2,1,0:T(8,128)(2,1)S(1)}, bf16[24,16,1024]{2,1,0:T(8,128)(2,1)S(1)}, u32[]{:S(2)}, u32[]{:S(2)}) collective-permute-start(bf16[24,16,1024]{2,1,0:T(8,128)(2,1)S(1)} %get-tuple-element.94), channel_id=1, source_target_pairs={{4,0},{5,1},{6,2},{7,3},{8,4},{9,5},{10,6},{11,7},{12,8},{13,9},{1... | collective-permute-start | bytes 2359304 | tf_op jit(solution)/shard_map/ppermute | solution.py:441
  222.1 50.4 %collective-permute-start.7 = (bf16[24,16,1024]{2,1,0:T(8,128)(2,1)S(1)}, bf16[24,16,1024]{2,1,0:T(8,128)(2,1)S(1)}, u32[]{:S(2)}, u32[]{:S(2)}) collective-permute-start(bf16[24,16,1024]{2,1,0:T(8,128)(2,1)S(1)} %get-tuple-element.92), channel_id=1, source_target_pairs={{0,4},{1,5},{2,6},{3,7},{4,8},{5,9},{6,10},{7,11},{8,12},{9,13},{1... | collective-permute-start | bytes 2359304 | tf_op jit(solution)/shard_map/ppermute | solution.py:441
  279.1 41.8 %collective-permute-start.37 = (bf16[24,16,1024]{2,1,0:T(8,128)(2,1)S(1)}, bf16[24,16,1024]{2,1,0:T(8,128)(2,1)S(1)}, u32[]{:S(2)}, u32[]{:S(2)}) collective-permute-start(bf16[24,16,1024]{2,1,0:T(8,128)(2,1)S(1)} %broadcast_select_fusion.2), channel_id=1, source_target_pairs={{4,0},{5,1},{6,2},{7,3},{8,4},{9,5},{10,6},{11,7},{20,16},{21,17},... | collective-permute-start | bytes 2359304 | tf_op jit(solution)/shard_map/ppermute | solution.py:441
  288.8 48.9 %collective-permute-start.36 = (bf16[24,16,1024]{2,1,0:T(8,128)(2,1)S(1)}, bf16[24,16,1024]{2,1,0:T(8,128)(2,1)S(1)}, u32[]{:S(2)}, u32[]{:S(2)}) collective-permute-start(bf16[24,16,1024]{2,1,0:T(8,128)(2,1)S(1)} %get-tuple-element.107), channel_id=1, source_target_pairs={{4,0},{5,1},{6,2},{7,3},{8,4},{9,5},{10,6},{11,7},{12,8},{13,9},{1... | collective-permute-start | bytes 2359304 | tf_op jit(solution)/shard_map/ppermute | solution.py:441
  304.0 48.9 %collective-permute-start.34 = (bf16[24,16,1024]{2,1,0:T(8,128)(2,1)}, bf16[24,16,1024]{2,1,0:T(8,128)(2,1)S(1)}, u32[]{:S(2)}, u32[]{:S(2)}) collective-permute-start(bf16[24,16,1024]{2,1,0:T(8,128)(2,1)} %get-tuple-element.105), channel_id=1, source_target_pairs={{0,4},{1,5},{2,6},{3,7},{4,8},{5,9},{6,10},{7,11},{8,12},{9,13},{1... | collective-permute-start | bytes 2359304 | tf_op jit(solution)/shard_map/ppermute | solution.py:441
  307.6 47.0 %collective-permute-start.39 = (bf16[24,16,1024]{2,1,0:T(8,128)(2,1)}, bf16[24,16,1024]{2,1,0:T(8,128)(2,1)S(1)}, u32[]{:S(2)}, u32[]{:S(2)}) collective-permute-start(bf16[24,16,1024]{2,1,0:T(8,128)(2,1)} %broadcast_select_fusion.1), channel_id=1, source_target_pairs={{4,0},{5,1},{6,2},{7,3},{8,4},{9,5},{10,6},{11,7},{20,16},{21,17},... | collective-permute-start | bytes 2359304 | tf_op jit(solution)/shard_map/ppermute | solution.py:441
  322.5 48.3 %collective-permute-start.41 = (bf16[24,16,1024]{2,1,0:T(8,128)(2,1)}, bf16[24,16,1024]{2,1,0:T(8,128)(2,1)}, u32[]{:S(2)}, u32[]{:S(2)}) collective-permute-start(bf16[24,16,1024]{2,1,0:T(8,128)(2,1)} %broadcast_select_fusion), channel_id=1, source_target_pairs={{4,0},{5,1},{6,2},{7,3},{8,4},{9,5},{10,6},{11,7},{20,16},{21,17},... | collective-permute-start | bytes 2359304 | tf_op jit(solution)/shard_map/ppermute | solution.py:441
  439.3 52.2 %collective-permute-start.53 = (bf16[6,80,1024]{2,1,0:T(8,128)(2,1)}, bf16[6,80,1024]{2,1,0:T(8,128)(2,1)S(1)}, u32[]{:S(2)}, u32[]{:S(2)}) collective-permute-start(bf16[6,80,1024]{2,1,0:T(8,128)(2,1)} %get-tuple-element.20), channel_id=1, source_target_pairs={{0,1},{1,0},{2,3},{3,2},{4,5},{5,4},{6,7},{7,6},{8,9},{9,8},{10,11... | collective-permute-start | bytes 2949128 | tf_op jit(solution)/shard_map/ppermute | solution.py:477
  439.4 53.6 %collective-permute-start.56 = (bf16[6,80,1024]{2,1,0:T(8,128)(2,1)}, bf16[6,80,1024]{2,1,0:T(8,128)(2,1)S(1)}, u32[]{:S(2)}, u32[]{:S(2)}) collective-permute-start(bf16[6,80,1024]{2,1,0:T(8,128)(2,1)} %get-tuple-element.23), channel_id=1, source_target_pairs={{0,2},{1,3},{2,0},{3,1},{4,6},{5,7},{6,4},{7,5},{8,10},{9,11},{10,... | collective-permute-start | bytes 2949128 | tf_op jit(solution)/shard_map/ppermute | solution.py:477
  476.5 52.6 %collective-permute-start.57 = (bf16[6,48,1024]{2,1,0:T(8,128)(2,1)}, bf16[6,48,1024]{2,1,0:T(8,128)(2,1)}, u32[]{:S(2)}, u32[]{:S(2)}) collective-permute-start(bf16[6,48,1024]{2,1,0:T(8,128)(2,1)} %get-tuple-element.24), channel_id=1, source_target_pairs={{4,6},{5,7},{6,4},{7,5},{8,10},{9,11},{10,8},{11,9},{20,22},{21,23... | collective-permute-start | bytes 1769480 | tf_op jit(solution)/shard_map/ppermute | solution.py:476
  478.0 51.1 %collective-permute-start.58 = (bf16[6,48,1024]{2,1,0:T(8,128)(2,1)}, bf16[6,48,1024]{2,1,0:T(8,128)(2,1)}, u32[]{:S(2)}, u32[]{:S(2)}) collective-permute-start(bf16[6,48,1024]{2,1,0:T(8,128)(2,1)} %get-tuple-element.25), channel_id=1, source_target_pairs={{4,2},{5,3},{6,0},{7,1},{8,14},{9,15},{10,12},{11,13},{20,18},{21,... | collective-permute-start | bytes 1769480 | tf_op jit(solution)/shard_map/ppermute | solution.py:472
  489.2 47.0 %collective-permute-start.59 = (bf16[6,80,1024]{2,1,0:T(8,128)(2,1)}, bf16[6,80,1024]{2,1,0:T(8,128)(2,1)S(1)}, u32[]{:S(2)}, u32[]{:S(2)}) collective-permute-start(bf16[6,80,1024]{2,1,0:T(8,128)(2,1)} %get-tuple-element.26), channel_id=1, source_target_pairs={{0,3},{1,2},{2,1},{3,0},{4,7},{5,6},{6,5},{7,4},{8,11},{9,10},{10,... | collective-permute-start | bytes 2949128 | tf_op jit(solution)/shard_map/ppermute | solution.py:477
  491.5 50.8 %collective-permute-start.60 = (bf16[6,48,1024]{2,1,0:T(8,128)(2,1)}, bf16[6,48,1024]{2,1,0:T(8,128)(2,1)}, u32[]{:S(2)}, u32[]{:S(2)}) collective-permute-start(bf16[6,48,1024]{2,1,0:T(8,128)(2,1)} %get-tuple-element.27), channel_id=1, source_target_pairs={{4,7},{5,6},{6,5},{7,4},{8,11},{9,10},{10,9},{11,8},{20,23},{21,22... | collective-permute-start | bytes 1769480 | tf_op jit(solution)/shard_map/ppermute | solution.py:476
  493.0 49.3 %collective-permute-start.61 = (bf16[6,48,1024]{2,1,0:T(8,128)(2,1)}, bf16[6,48,1024]{2,1,0:T(8,128)(2,1)}, u32[]{:S(2)}, u32[]{:S(2)}) collective-permute-start(bf16[6,48,1024]{2,1,0:T(8,128)(2,1)} %get-tuple-element.28), channel_id=1, source_target_pairs={{4,3},{5,2},{6,1},{7,0},{8,15},{9,14},{10,13},{11,12},{20,19},{21,... | collective-permute-start | bytes 1769480 | tf_op jit(solution)/shard_map/ppermute | solution.py:472
  (120 other events, 3673.7 us)
Sparse Core Ops, SparseCore 0:
  17.8 47.4 all-gather.1

commit v3 on v1

--- a/solution.py
+++ b/solution.py
@@ -1,7 +1,19 @@
+import functools
+
 import jax
 import jax.numpy as jnp
 from jax import lax
+from jax.experimental import pallas as pl
+from jax.experimental.pallas import tpu as pltpu
 from jax.sharding import PartitionSpec as P
+
+PLANES = 4
+INNER = 4
+CHUNK = 16
+CHUNKS = 8
+WIDE = 5
+LANES = 128
+VMEM_BYTES = 63 * 1024 * 1024
 
 
 def table_lookup(index_col, table):
@@ -10,7 +22,7 @@
     return jnp.sum(jnp.where(equal, table[None, :], jnp.zeros_like(table)[None, :]), axis=1)
 
 
-def shards(
+def spread_plan(
     amplitudes,
     integrals,
     fock_matrix,
@@ -59,9 +71,680 @@
     return (total / denom).astype(jnp.bfloat16)
 
 
+def plane_perm(step, first, last):
+    return [
+        (plane * INNER + at, (plane + step) * INNER + at)
+        for plane in range(first, last + 1)
+        for at in range(INNER)
+    ]
+
+
+def inner_perm(flip, planes=range(PLANES)):
+    return [(p * INNER + at, p * INNER + (at ^ flip)) for p in planes for at in range(INNER)]
+
+
+def outward_perm(flip):
+    return [
+        (p * INNER + at, q * INNER + (at ^ flip)) for p, q in ((1, 0), (2, 3)) for at in range(INNER)
+    ]
+
+
+def sixth(index):
+    return sum((index >= edge).astype(jnp.int32) for edge in (6, 12, 18))
+
+
+def pair_at(index, me, pair_dev):
+    group = sixth(index)
+    return pair_dev * (me ^ group) + index - pair_dev * group
+
+
+def place_sources(own, plus, minus, chunk):
+    table = {
+        1: {0: plus.get(chunk), 1: own, 2: minus.get(chunk), 3: minus.get(CHUNKS + chunk)},
+        2: {0: plus.get(CHUNKS + chunk), 1: plus.get(chunk), 2: own, 3: minus.get(chunk)},
+    }
+    if chunk < WIDE:
+        table[0] = {0: own, 1: minus.get(chunk), 2: minus.get(WIDE + chunk), 3: minus.get(2 * WIDE + chunk)}
+        table[3] = {0: plus.get(2 * WIDE + chunk), 1: plus.get(WIDE + chunk), 2: plus.get(chunk), 3: own}
+    return table
+
+
+def late_plane(plane):
+    return PLANES - 1 if plane < 2 else 0
+
+
+def numbered(arrays, chosen):
+    numbers = []
+    for array in chosen:
+        found = [n for n, other in enumerate(arrays) if other is array]
+        if not found:
+            found = [len(arrays)]
+            arrays.append(array)
+        numbers.append(found[0])
+    return numbers
+
+
+def here():
+    blk = lax.axis_index("blk")
+    return lax.div(blk, INNER), lax.rem(blk, INNER)
+
+
+def kept_sum(gram, depth):
+    row_id = lax.broadcasted_iota(jnp.int32, gram.shape, 0)
+    col_id = lax.broadcasted_iota(jnp.int32, gram.shape, 1)
+    same = (row_id & (depth - 1)) == (col_id & (depth - 1))
+    return jnp.where(same, gram, 0.0).reshape(-1, depth, gram.shape[1]).sum(axis=1)
+
+
+def exact_dot(left, right):
+    return jnp.dot(left, right, preferred_element_type=jnp.float32, precision=lax.Precision.HIGHEST)
+
+
+def pad_rows(array):
+    extra = LANES - array.shape[0]
+    return jnp.concatenate([array, jnp.zeros((extra, array.shape[1]), array.dtype)], axis=0)
+
+
+def pair_kernel(table, near_too, own_too, parts, late, last, pair_dev, *refs):
+    acc_in, out_ref, amp, ints, turned, total, sems = refs[-7:]
+    plane, me = here()
+    chunks, _, rows, depth, width = amp.shape
+    sides = ints.shape[1]
+    total[...] = acc_in[...]
+    for z, (amp_from, int_from) in table.items():
+
+        @pl.when(plane == z)
+        def _():
+            for c in range(chunks):
+                for n in range(sides):
+                    pltpu.make_async_copy(refs[int_from[c][n]], ints.at[c, n], sems.at[c, len(parts) + n]).start()
+                for n in range(len(parts)):
+                    pltpu.make_async_copy(refs[amp_from[c][n]], amp.at[c, n], sems.at[c, n]).start()
+
+    def add_all():
+        for c in range(chunks):
+            for n in range(sides):
+                pltpu.make_async_copy(refs[0], ints.at[c, n], sems.at[c, len(parts) + n]).wait()
+                turned[c, n] = ints[c, n].reshape(rows * depth, width).T
+            for n in range(len(parts)):
+                pltpu.make_async_copy(refs[0], amp.at[c, n], sems.at[c, n]).wait()
+
+        def add_part(n, carry):
+            if late:
+                p = jnp.where(plane < 2, PLANES - 1, 0)
+            else:
+                p = jnp.where(plane < 2, n + parts[0], n + parts[0] + 1)
+            place = pl.ds(pl.multiple_of(p * rows, 8), rows)
+            for side in range(sides):
+                gram = jnp.zeros((rows * depth, rows * depth), jnp.float32)
+                for c in range(chunks):
+                    left = amp[c, n].reshape(rows * depth, width)
+                    gram += jnp.dot(left, turned[c, side], preferred_element_type=jnp.float32)
+                total[side + (0 if own_too else 1), place] += kept_sum(gram, depth)
+            return carry
+
+        lax.fori_loop(0, len(parts), add_part, 0)
+
+    if len(table) == PLANES:
+        add_all()
+    else:
+        pl.when((plane == 1) | (plane == 2))(add_all)
+    if not last:
+        out_ref[...] = total[...]
+        return
+    hole_ref = refs[-8]
+    lanes = total.shape[2]
+    summed = jnp.zeros((total.shape[1], LANES), jnp.float32)
+    near = jnp.where(plane < 2, 0, PLANES - 1)
+    row_id = lax.broadcasted_iota(jnp.int32, (lanes, LANES), 0) // CHUNK
+    col_id = lax.broadcasted_iota(jnp.int32, (lanes, LANES), 1)
+    pair_id = pair_at(row_id, me, pair_dev)
+    for side, at in ((0, plane), (1, near)):
+        chosen = (col_id == pair_id + at * rows).astype(jnp.float32)
+        summed += exact_dot(total[side], chosen)
+    out_id = lax.broadcasted_iota(jnp.int32, (total.shape[1], LANES), 0)
+    in_id = lax.broadcasted_iota(jnp.int32, (total.shape[1], LANES), 1)
+    in_plane = sum((in_id >= p * rows).astype(jnp.int32) for p in range(1, PLANES))
+    in_pair = pair_at(in_id - in_plane * rows, me, pair_dev) + in_plane * rows
+    chosen = (out_id == in_pair).astype(jnp.float32)
+    out_ref[...] = hole_ref[...] + exact_dot(chosen, pad_rows(summed))
+
+
+def add_pair_sums(chunks, parts, own_too, near_too, own, got, int_own, acc, hole=None, after=()):
+    late, last = parts is None, hole is not None
+    parts = (0,) if late else parts
+    rows, depth, width = own[chunks[0]].shape
+    arrays, table = [], {}
+    for chunk in chunks:
+        for z, sources in place_sources(own[chunk], got[0], got[1], chunk).items():
+            early = [sources[p] for p in range(PLANES) if p != late_plane(z)]
+            amp_from = [sources[late_plane(z)]] if late else [early[n] for n in parts]
+            int_from = [int_own[chunk]] if own_too else []
+            if near_too:
+                int_from.append(got[z - 1][CHUNKS + chunk - WIDE])
+            entry = table.setdefault(z, ([], []))
+            entry[0].append(numbered(arrays, amp_from))
+            entry[1].append(numbered(arrays, int_from))
+    sides = own_too + near_too
+    operands = arrays + list(after)
+    far = len(operands)
+    if last:
+        operands.append(hole)
+    operands.append(acc)
+    shape = (PLANES * rows, LANES) if last else acc.shape
+    block = rows * depth
+    return pl.pallas_call(
+        functools.partial(pair_kernel, table, near_too, own_too, parts, late, last, rows // INNER),
+        out_shape=jax.ShapeDtypeStruct(shape, jnp.float32),
+        in_specs=[pl.BlockSpec(memory_space=pl.ANY)] * far
+        + [pl.BlockSpec(memory_space=pltpu.VMEM)] * (len(operands) - far),
+        out_specs=pl.BlockSpec(memory_space=pltpu.VMEM),
+        scratch_shapes=[
+            pltpu.VMEM((len(chunks), len(parts), rows, depth, width), jnp.bfloat16),
+            pltpu.VMEM((len(chunks), sides, rows, depth, width), jnp.bfloat16),
+            pltpu.VMEM((len(chunks), sides, width, block), jnp.bfloat16),
+            pltpu.VMEM(acc.shape, jnp.float32),
+            pltpu.SemaphoreType.DMA((len(chunks), len(parts) + sides)),
+        ],
+        compiler_params=pltpu.CompilerParams(vmem_limit_bytes=VMEM_BYTES),
+        cost_estimate=pl.CostEstimate(
+            flops=2 * len(chunks) * len(parts) * sides * block**2 * width,
+            bytes_accessed=len(chunks) * (len(parts) + sides) * block * width * 2,
+            transcendentals=0,
+        ),
+        name=f"pair_sums_{chunks[0]}_{'late' if late else parts[0]}",
+    )(*operands)
+
+
+def places_kernel(pair_dev, col_ref, row_ref, keep_ref):
+    plane, me = here()
+    rows, depth = INNER * pair_dev, CHUNK
+    block = rows * depth
+    col = lax.broadcasted_iota(jnp.int32, (LANES, PLANES * block), 1) // depth
+    col_plane = sum((col >= p * rows).astype(jnp.int32) for p in range(1, PLANES))
+    col_pair = pair_at(col - col_plane * rows, me, pair_dev) + col_plane * rows
+    col_ref[...] = (lax.broadcasted_iota(jnp.int32, col.shape, 0) == col_pair).astype(jnp.bfloat16)
+    row = lax.broadcasted_iota(jnp.int32, (block, LANES), 0) // depth
+    row_pair = pair_at(row, me, pair_dev)
+    for side, at in enumerate((plane, jnp.where(plane < 2, 0, PLANES - 1))):
+        chosen = lax.broadcasted_iota(jnp.int32, row.shape, 1) == row_pair + at * rows
+        row_ref[side] = chosen.astype(jnp.bfloat16)
+    left = lax.broadcasted_iota(jnp.int32, (block, PLANES * block), 0) & (depth - 1)
+    right = lax.broadcasted_iota(jnp.int32, (block, PLANES * block), 1) & (depth - 1)
+    keep_ref[...] = (left == right).astype(jnp.bfloat16)
+
+
+def ladder_places(pair_dev):
+    block = INNER * pair_dev * CHUNK
+    shapes = [(LANES, PLANES * block), (2, block, LANES), (block, PLANES * block)]
+    return pl.pallas_call(
+        functools.partial(places_kernel, pair_dev),
+        out_shape=[jax.ShapeDtypeStruct(shape, jnp.bfloat16) for shape in shapes],
+        out_specs=[pl.BlockSpec(memory_space=pltpu.VMEM)] * 3,
+        compiler_params=pltpu.CompilerParams(vmem_limit_bytes=VMEM_BYTES),
+        name="ladder_places",
+    )()
+
+
+def ladder_kernel(table_of, wide, pair_dev, *refs):
+    sides = 1 if wide else 2
+    own = refs[0]
+    count = sides * INNER
+    sum_ref, mask_ref, col_ref, row_ref, keep_ref = refs[-8 - count : -3 - count]
+    outs = refs[-3 - count : -3]
+    amp, spread, sems = refs[-3:]
+    plane, _ = here()
+    rows, depth, width = amp.shape[2:]
+    block = rows * depth
+    for z, table in table_of.items():
+
+        @pl.when(plane == z)
+        def _():
+            for n, sources in enumerate(table):
+                for p in range(PLANES):
+                    pltpu.make_async_copy(refs[sources[p]], amp.at[n, p], sems.at[n, p]).start()
+
+    def work():
+        ladder = jnp.where(mask_ref[...] > 0, sum_ref[...], 0.0).astype(jnp.bfloat16)
+        ladder = pad_rows(ladder)
+        for side in range(sides):
+            picked = jnp.dot(row_ref[side], ladder, preferred_element_type=jnp.float32).astype(jnp.bfloat16)
+            full = jnp.dot(picked, col_ref[...], preferred_element_type=jnp.float32).astype(jnp.bfloat16)
+            spread[side] = jnp.where(keep_ref[...] > 0, full, jnp.zeros_like(full))
+
+        def one_chunk(n, carry):
+            for p in range(PLANES):
+                pltpu.make_async_copy(own, amp.at[n, p], sems.at[n, p]).wait()
+            columns = amp[n].reshape(PLANES * block, width)
+            place = pl.ds(pl.multiple_of(n * depth, depth), depth)
+            for side in range(sides):
+                term = jnp.dot(spread[side], columns, preferred_element_type=jnp.float32).astype(jnp.bfloat16)
+                term = term.reshape(INNER, pair_dev, depth, width)
+                for flip in range(INNER):
+                    outs[side * INNER + flip][:, place, :] = term[flip]
+            return carry
+
+        lax.fori_loop(0, amp.shape[0], one_chunk, 0)
+
+    if wide:
+        work()
+    else:
+        pl.when((plane == 1) | (plane == 2))(work)
+
+
+def ladder_terms(chunks, own, plus, minus, summed, mask, places, after=()):
+    rows, depth, width = own[chunks[0]].shape
+    pair_dev = rows // INNER
+    wide = chunks[0] < WIDE
+    arrays, table = [], {}
+    for chunk in chunks:
+        for z, sources in place_sources(own[chunk], plus, minus, chunk).items():
+            table.setdefault(z, []).append(numbered(arrays, [sources[p] for p in range(PLANES)]))
+    operands = arrays + list(after)
+    far = len(operands)
+    operands += [summed, mask, *places]
+    sides = 1 if wide else 2
+    block = rows * depth
+    return pl.pallas_call(
+        functools.partial(ladder_kernel, table, wide, pair_dev),
+        out_shape=[jax.ShapeDtypeStruct((pair_dev, len(chunks) * depth, width), jnp.bfloat16)] * (sides * INNER),
+        in_specs=[pl.BlockSpec(memory_space=pl.ANY)] * far
+        + [pl.BlockSpec(memory_space=pltpu.VMEM)] * (len(operands) - far),
+        out_specs=[pl.BlockSpec(memory_space=pltpu.VMEM)] * (sides * INNER),
+        scratch_shapes=[
+            pltpu.VMEM((len(chunks), PLANES, rows, depth, width), jnp.bfloat16),
+            pltpu.VMEM((sides, block, PLANES * block), jnp.bfloat16),
+            pltpu.SemaphoreType.DMA((len(chunks), PLANES)),
+        ],
+        compiler_params=pltpu.CompilerParams(vmem_limit_bytes=VMEM_BYTES),
+        cost_estimate=pl.CostEstimate(
+            flops=2 * PLANES * block * block * width * sides * len(chunks),
+            bytes_accessed=(PLANES + sides) * block * width * 2 * len(chunks),
+            transcendentals=0,
+        ),
+        name=f"ladder_{chunks[0]}",
+    )(*operands)
+
+
+def scale_kernel(flip, first, count, fock_ref, inverse_ref, *refs):
+    pieces, (out_ref, fock, inverse, ladder, sems) = refs[:count], refs[count:]
+    plane, me = here()
+    pair_dev, rows, _ = fock.shape
+    start = pl.multiple_of((me ^ flip) * (CHUNK * CHUNKS) + first * CHUNK, CHUNK)
+    place = pl.ds(start, rows)
+
+    def load(p):
+        return (
+            pltpu.make_async_copy(fock_ref.at[p, place], fock.at[p], sems.at[p, 0]),
+            pltpu.make_async_copy(inverse_ref.at[p, place], inverse.at[p], sems.at[p, 1]),
+        )
+
+    def piece(p, source):
+        return pltpu.make_async_copy(source.at[p], ladder.at[p], sems.at[p, 2])
+
+    def store(p):
+        return pltpu.make_async_copy(fock.at[p], out_ref.at[p, place], sems.at[p, 3])
+
+    middle = (plane == 1) | (plane == 2)
+    for p in range(pair_dev):
+        for copy in load(p):
+            copy.start()
+        if count == 1:
+            piece(p, pieces[0]).start()
+        else:
+            pl.when(middle)(piece(p, pieces[0]).start)
+            pl.when(jnp.logical_not(middle))(piece(p, pieces[1]).start)
+
+    def one_pair(p, carry):
+        for copy in (*load(p), piece(p, pieces[0])):
+            copy.wait()
+        total = fock[p].astype(jnp.float32) + ladder[p].astype(jnp.float32)
+        fock[p] = (total * inverse[p]).astype(fock.dtype)
+        store(p).start()
+        return carry
+
+    lax.fori_loop(0, pair_dev, one_pair, 0)
+    for p in range(pair_dev):
+        store(p).wait()
+
+
+def add_and_scale(buffer, inverse, pieces, flip, first):
+    shape = pieces[0].shape
+    size = shape[0] * shape[1] * shape[2]
+    return pl.pallas_call(
+        functools.partial(scale_kernel, flip, first, len(pieces)),
+        out_shape=jax.ShapeDtypeStruct(buffer.shape, buffer.dtype),
+        in_specs=[pl.BlockSpec(memory_space=pl.ANY)] * (2 + len(pieces)),
+        out_specs=pl.BlockSpec(memory_space=pl.ANY),
+        scratch_shapes=[
+            pltpu.VMEM(shape, buffer.dtype),
+            pltpu.VMEM(shape, jnp.float32),
+            pltpu.VMEM(shape, buffer.dtype),
+            pltpu.SemaphoreType.DMA((shape[0], 4)),
+        ],
+        input_output_aliases={0: 0},
+        compiler_params=pltpu.CompilerParams(vmem_limit_bytes=VMEM_BYTES),
+        cost_estimate=pl.CostEstimate(
+            flops=2 * size, bytes_accessed=(8 + 2 * len(pieces)) * size, transcendentals=0
+        ),
+        name="add_and_scale",
+    )(buffer, inverse, *pieces)
+
+
+def move_kernel(moves, count, *refs):
+    outs, sems = refs[count:-1], refs[-1]
+    _, me = here()
+    copies = []
+    for n, (source, flip, at, target, place) in enumerate(moves):
+        ref = refs[source]
+        if flip is None:
+            ref = ref.at[at]
+        else:
+            start = pl.multiple_of((me ^ flip) * (CHUNK * CHUNKS) + at.start, CHUNK)
+            ref = ref.at[:, pl.ds(start, at.stop - at.start), :]
+        copies.append(pltpu.make_async_copy(ref, outs[target].at[place], sems.at[n]))
+    for copy in copies:
+        copy.start()
+    for copy in copies:
+        copy.wait()
+
+
+def move(operands, shapes, moves, name):
+    moved = 2 * sum(2 * shape[0] * shape[-2] * shape[-1] for shape in shapes)
+    call = pl.pallas_call(
+        functools.partial(move_kernel, moves, len(operands)),
+        out_shape=[jax.ShapeDtypeStruct(shape, jnp.bfloat16) for shape in shapes],
+        in_specs=[pl.BlockSpec(memory_space=pl.ANY)] * len(operands),
+        out_specs=[pl.BlockSpec(memory_space=pltpu.VMEM)] * len(shapes),
+        scratch_shapes=[pltpu.SemaphoreType.DMA((len(moves),))],
+        compiler_params=pltpu.CompilerParams(vmem_limit_bytes=VMEM_BYTES),
+        cost_estimate=pl.CostEstimate(flops=0, bytes_accessed=moved, transcendentals=0),
+        name=name,
+    )
+    return list(call(*operands))
+
+
+def rows_of(chunk, first=0):
+    return slice((chunk - first) * CHUNK, (chunk - first + 1) * CHUNK)
+
+
+def core_moves(source, group, target):
+    rows = slice(group[0] * CHUNK, group[1] * CHUNK)
+    return [(source, 1 + 2 * side, rows, target, (slice(None), side)) for side in range(2)]
+
+
+def across_moves(source, core, first, group, pair_dev, target):
+    rows = slice(group[0] * CHUNK, group[1] * CHUNK)
+    near = slice((group[0] - first) * CHUNK, (group[1] - first) * CHUNK)
+    return [
+        (source, 2, rows, target, slice(0, pair_dev)),
+        (core, None, (slice(None), 1, near), target, slice(pair_dev, 2 * pair_dev)),
+    ]
+
+
+def own_moves(source, core, first, across, group, pair_dev, target):
+    moves = []
+    for n, chunk in enumerate(range(*group)):
+        moves += [
+            (source, 0, rows_of(chunk), target + n, slice(0, pair_dev)),
+            (core, None, (slice(None), 0, rows_of(chunk, first)), target + n, slice(pair_dev, 2 * pair_dev)),
+            (across, None, (slice(None), rows_of(chunk, group[0])), target + n, slice(2 * pair_dev, 4 * pair_dev)),
+        ]
+    return moves
+
+
+def pick_kernel(choices, *refs):
+    outs, sems = refs[-3:-1], refs[-1]
+    plane, _ = here()
+
+    def each(do):
+        for n, table in enumerate(choices):
+            for far, source in table.items():
+                at = far if n == 0 else PLANES - 1 - far
+                copy = pltpu.make_async_copy(refs[source], outs[n], sems.at[n])
+                pl.when(plane == at)(getattr(copy, do))
+
+    each("start")
+    each("wait")
+
+
+def pick(choices, name, after=()):
+    arrays = []
+    tables = [dict(zip(table, numbered(arrays, table.values()))) for table in choices]
+    example = arrays[0]
+    arrays += after
+    size = example.size
+    return pl.pallas_call(
+        functools.partial(pick_kernel, tables),
+        out_shape=[jax.ShapeDtypeStruct(example.shape, example.dtype)] * 2,
+        in_specs=[pl.BlockSpec(memory_space=pl.ANY)] * len(arrays),
+        out_specs=[pl.BlockSpec(memory_space=pltpu.VMEM)] * 2,
+        scratch_shapes=[pltpu.SemaphoreType.DMA((2,))],
+        compiler_params=pltpu.CompilerParams(vmem_limit_bytes=VMEM_BYTES),
+        cost_estimate=pl.CostEstimate(flops=0, bytes_accessed=8 * size, transcendentals=0),
+        name=name,
+    )(*arrays)
+
+
+def line_round(step, own, int_own, got, after, done_with):
+    narrow = CHUNKS - WIDE
+    first, last = 0, 2
+    choices = []
+    for have in got:
+        if step < WIDE:
+            table = {far: own[step] for far in range(3)}
+        elif step < CHUNKS:
+            table = {0: own[step], 1: own[step], 2: have[step - WIDE]}
+        else:
+            table = {1: have[step - CHUNKS]}
+            if step < CHUNKS + narrow:
+                table[0] = int_own[WIDE + step - CHUNKS]
+            else:
+                first = 1
+            if step < 2 * WIDE:
+                table[2] = have[step - WIDE]
+            elif step < 3 * WIDE:
+                table[2] = have[step - 2 * WIDE + CHUNKS]
+            else:
+                last = 1
+        choices.append(table)
+    if not after and (step < WIDE or first == last):
+        sends = [table[1] for table in choices]
+    else:
+        sends = done_with(list(pick(choices, f"pick_{step}", after)))
+    got[0][step] = lax.ppermute(sends[0], "blk", plane_perm(1, first, last))
+    got[1][step] = lax.ppermute(sends[1], "blk", plane_perm(-1, PLANES - 1 - last, PLANES - 1 - first))
+
+
+def line_exchanges(amplitudes, integrals, hole, beside, beside_later):
+    pair_dev, _, width = amplitudes.shape
+    rows = INNER * pair_dev
+    full = (rows, CHUNK, width)
+    own, int_own, got = {}, {}, ({}, {})
+
+    def across_shape(group):
+        return (2 * pair_dev, (group[1] - group[0]) * CHUNK, width)
+
+    last = []
+
+    def in_turn(operands):
+        return list(operands) + last
+
+    def done_with(found):
+        last[:] = found[:1]
+        return found
+
+    def arrived(step):
+        return [have[step] for have in got]
+
+    def rounds(*steps, after=()):
+        for step in steps:
+            before = arrived(step - 2) if step >= 2 else []
+            line_round(step, own, int_own, got, in_turn(before + list(after)) if step >= 2 else [], done_with)
+
+    groups = ((0, 1), (1, 2), (2, 4), (4, 6), (6, CHUNKS))
+    core_groups = ((0, 2), (2, CHUNKS))
+    cores = move(
+        [amplitudes],
+        [(pair_dev, 2, (end - first) * CHUNK, width) for first, end in core_groups],
+        [one for n, group in enumerate(core_groups) for one in core_moves(0, group, n)],
+        "move_core",
+    )
+    cores = [lax.ppermute(core, "blk", inner_perm(1)) for core in cores]
+    (across,) = move(
+        [amplitudes, cores[0]],
+        [across_shape(groups[0])],
+        across_moves(0, 1, 0, groups[0], pair_dev, 0),
+        "move_across",
+    )
+    waits = ((), (), (0,), (2,), (4,))
+    int_groups = ((WIDE, CHUNKS), (0, WIDE))
+    for n, group in enumerate(groups):
+        across = lax.ppermute(across, "blk", inner_perm(2))
+        size = group[1] - group[0]
+        mine = int(group[0] >= core_groups[1][0])
+        moves = own_moves(0, 1, core_groups[mine][0], 2, group, pair_dev, 0)
+        shapes = [full] * size
+        operands = [amplitudes, cores[mine], across]
+        if n + 1 < len(groups):
+            then = int(groups[n + 1][0] >= core_groups[1][0])
+            moves += across_moves(0, 3, core_groups[then][0], groups[n + 1], pair_dev, size)
+            shapes.append(across_shape(groups[n + 1]))
+            operands.append(cores[then])
+        else:
+            moves += across_moves(3, 4, 0, int_groups[0], pair_dev, size)
+            shapes.append(across_shape(int_groups[0]))
+            operands += [integrals, int_core]
+        if n == 3:
+            moves += core_moves(4, (0, CHUNKS), size + 1)
+            shapes.append((pair_dev, 2, CHUNKS * CHUNK, width))
+            operands.append(integrals)
+        if n == 2:
+            operands += beside
+        for step in waits[n]:
+            operands += arrived(step)
+        found = done_with(move(in_turn(operands), shapes, moves, f"move_own_{group[0]}"))
+        own.update(zip(range(*group), found))
+        across = found[size]
+        if n == 3:
+            int_core = lax.ppermute(found[size + 1], "blk", inner_perm(1))
+        rounds(*((0,), (1,), (2, 3), (4, 5), (6,))[n])
+    rounds(7, after=beside_later[1:])
+
+    def own_integrals(n, across):
+        group = int_groups[n]
+        across = lax.ppermute(across, "blk", inner_perm(2))
+        size = group[1] - group[0]
+        moves = own_moves(0, 1, 0, 2, group, pair_dev, 0)
+        shapes = [full] * size
+        if n + 1 < len(int_groups):
+            moves += across_moves(0, 1, 0, int_groups[n + 1], pair_dev, size)
+            shapes.append(across_shape(int_groups[n + 1]))
+        found = done_with(move(in_turn([integrals, int_core, across]), shapes, moves, f"move_ints_{group[0]}"))
+        int_own.update(zip(range(*group), found))
+        return found[-1]
+
+    wide, narrow = tuple(range(WIDE)), tuple(range(WIDE, CHUNKS))
+    acc = jnp.zeros((2, PLANES * rows, rows * CHUNK), jnp.float32)
+
+    def add(*what, acc, **more):
+        return done_with([add_pair_sums(*what, own, got, int_own, acc, after=in_turn([]), **more)])[0]
+
+    across = own_integrals(0, across)
+    rounds(8)
+    acc = add(narrow, (0, 1, 2), True, False, acc=acc)
+    rounds(9)
+    rounds(10, after=beside_later[:1])
+    rounds(11)
+    own_integrals(1, across)
+    for part in range(3):
+        acc = add(wide, (part,), True, False, acc=acc)
+        rounds(12 + part)
+    acc = add(narrow, (0, 1, 2), False, True, acc=acc)
+    rounds(15)
+    acc = add(wide[:3], None, True, False, acc=acc)
+    acc = add(wide[3:], None, True, False, acc=acc)
+    acc = add(narrow[:-1], None, True, True, acc=acc)
+    acc = add(narrow[-1:], None, True, True, acc=acc, hole=hole)
+    return own, *got, acc
+
+
+def line_plan(
+    amplitudes,
+    integrals,
+    fock_matrix,
+    hole_ladder,
+    virt_irrep,
+    occ_irrep,
+    pair_index,
+    eps_occ,
+    eps_virt,
+):
+    pair_dev, virt_rows, virt_all = amplitudes.shape
+    pair_total = pair_dev * PLANES * INNER
+    blk_id = lax.axis_index("blk")
+    rep_id = lax.axis_index("rep")
+    plane, me = here()
+    half = virt_all // 2
+    piece = lax.dynamic_slice_in_dim(fock_matrix, rep_id * half, half, axis=1)
+    piece = lax.all_gather(piece, "blk", axis=0, tiled=True)
+    fock_all = lax.all_gather(piece, "rep", axis=1, tiled=True)
+    kept = jnp.where(virt_irrep[:, None] == virt_irrep[None, :], fock_all, jnp.zeros_like(fock_all))
+    fock_term = jnp.einsum(
+        "pac,bc->pab", amplitudes, kept, preferred_element_type=jnp.float32
+    ).astype(jnp.bfloat16)
+
+    pair_irrep = jnp.bitwise_xor(
+        table_lookup(pair_index[:, 0], occ_irrep), table_lookup(pair_index[:, 1], occ_irrep)
+    )
+    pair_energy = table_lookup(pair_index[:, 0], eps_occ) + table_lookup(pair_index[:, 1], eps_occ)
+    mask = (pair_irrep[:, None] == pair_irrep[None, :]).astype(jnp.float32)
+    mask = jnp.pad(mask, ((0, 0), (0, LANES - pair_total)))
+    own_energy = lax.dynamic_slice_in_dim(pair_energy, blk_id * pair_dev, pair_dev)
+    row_energy = lax.dynamic_slice_in_dim(eps_virt, rep_id * virt_rows, virt_rows)
+    inverse = 1.0 / (own_energy[:, None, None] - row_energy[None, :, None] - eps_virt[None, None, :])
+
+    hole = jnp.zeros((pair_total, LANES), jnp.float32)
+    hole_rows = jnp.pad(hole_ladder, ((0, 0), (0, LANES - pair_total)))
+    hole = lax.dynamic_update_slice_in_dim(hole, hole_rows, blk_id * pair_dev, axis=0)
+    hole = jnp.where(rep_id == 0, hole, jnp.zeros_like(hole))
+    places = ladder_places(pair_dev)
+    own, plus, minus, acc = line_exchanges(
+        amplitudes, integrals, hole, [piece], [fock_term, inverse, mask, places[2]]
+    )
+    summed = acc + lax.ppermute(acc, "blk", inner_perm(1))
+    summed = summed + lax.ppermute(summed, "rep", [(0, 1), (1, 0)])
+    for flip in (2, 4, 8):
+        summed = summed + lax.ppermute(summed, "blk", [(i, i ^ flip) for i in range(PLANES * INNER)])
+
+    terms = functools.partial(ladder_terms, own=own, plus=plus, minus=minus, summed=summed, mask=mask, places=places)
+    ladder_groups = (tuple(range(WIDE, CHUNKS)), tuple(range(2)), tuple(range(2, WIDE)))
+    outside, inside = {}, {}
+    narrow = terms(ladder_groups[0])
+    for flip in (2, 3):
+        inside[0, flip] = lax.ppermute(narrow[flip], "blk", inner_perm(flip, (1, 2)))
+        outside[flip] = lax.ppermute(narrow[INNER + flip], "blk", outward_perm(flip))
+    for flip in (0, 1):
+        outside[flip] = lax.ppermute(narrow[INNER + flip], "blk", outward_perm(flip))
+    inside[0, 1] = lax.ppermute(narrow[1], "blk", inner_perm(1, (1, 2)))
+    inside[0, 0] = narrow[0]
+    for n in (1, 2):
+        wide = terms(ladder_groups[n], after=[inside[0, 2], outside[2]] if n == 2 else [narrow[0]])
+        inside[n, 0] = wide[0]
+        for flip in (2, 3, 1):
+            inside[n, flip] = lax.ppermute(wide[flip], "blk", inner_perm(flip))
+    update = fock_term
+    order = ((1, 0), (1, 1), (2, 0), (2, 1), (0, 2), (0, 3), (0, 1), (0, 0), (1, 2), (1, 3), (2, 2), (2, 3))
+    for n, flip in order:
+        pieces = [inside[n, flip]] + ([outside[flip]] if n == 0 else [])
+        update = add_and_scale(update, inverse, pieces, flip, ladder_groups[n][0])
+    return update
+
+
 def solution(mesh):
+    fits = mesh.shape["blk"] == PLANES * INNER and mesh.shape["rep"] == 2
     return jax.shard_map(
-        shards,
+        line_plan if fits else spread_plan,
         mesh=mesh,
         in_specs=(
             P("blk", "rep", None),

time: 720 us -> 492 us (0.68)
  the two profiles are of different devices: /device:TPU:15 before, /device:TPU:0 now
where the time goes in v3:
time: 492 us; the launch traced here: 489 us
  waiting for transfers between devices  160 us (33%)
  Pallas kernels  149 us (30%)
  starting transfers between devices  140 us (28%)
  between operations  14.4 us (3%)
  matrix products  11.3 us (2%)
  other arithmetic  7.92 us (2%)
  local copies, waits for them, and re-layouts  6.84 us (1%)
    ppermute x16, starting transfers between devices, line_round(): got[0][step] = lax.ppermute(sends[0], 'blk', plane_perm(1, first, last))  67.9 us
    pallas_call x9, Pallas kernels, add_pair_sums(): pl.pallas_call(functools.partial(pair_kernel, table, near_too, own_too, p...  39.8 us
    ppermute x16, waiting for transfers between devices, line_round(): lax.ppermute(sends[1], 'blk', plane_perm(-1, PLANES - 1 - last, PLANES -...  35.2 us
    pallas_call x9, Pallas kernels, move(): return list(call(*operands))  30.8 us
    pallas_call x12, Pallas kernels, add_and_scale(): pl.pallas_call(functools.partial(scale_kernel, flip, first, len(pieces)),...  30 us
    ppermute x16, waiting for transfers between devices, line_round(): got[0][step] = lax.ppermute(sends[0], 'blk', plane_perm(1, first, last))  27.5 us
    pallas_call x14, Pallas kernels, pick(): pl.pallas_call(functools.partial(pick_kernel, tables), out_shape=[jax.Sha...  27 us
    ppermute x4, waiting for transfers between devices, line_plan(): lax.ppermute(narrow[INNER + flip], 'blk', outward_perm(flip))  26.1 us
  transfers between devices with their start and end apart: 62, of which 29 were waited for; matrix products, arithmetic and copies ran while one was open for 4% of the time, Pallas kernels for 27%

profile of v3, /device:TPU:0, one launch (start us, length us, event | category | flops | bytes accessed | tf_op | source)
XLA Modules:
  0.0 489.0 jit_solution(6667296945933582687)
XLA Ops:
  21.4 10.6 %collective-permute-done.1.refs_2_ = bf16[12,16,1024]{2,1,0:T(8,128)(2,1)S(1)} collective-permute-done((bf16[12,16,1024]{2,1,0:T(8,128)(2,1)}, bf16[12,16,1024]{2,1,0:T(8,128)(2,1)S(1)}, u32[]{:S(2)}, u32[]{:S(2)}) %collective-permute-start.1) | collective-permute-done | bytes 393248 | tf_op jit(solution)/shard_map/ppermute | solution.py:603
  41.7 7.4 %collective-permute-done.5.refs_2_ = bf16[12,16,1024]{2,1,0:T(8,128)(2,1)} collective-permute-done((bf16[12,16,1024]{2,1,0:T(8,128)(2,1)}, bf16[12,16,1024]{2,1,0:T(8,128)(2,1)}, u32[]{:S(2)}, u32[]{:S(2)}) %collective-permute-start.5) | collective-permute-done | bytes 393248 | tf_op jit(solution)/shard_map/ppermute | solution.py:603
  84.8 10.0 %collective-permute-done.8.refs_5_.refs_1_.refs_0_.refs_8_.refs_11_ = bf16[24,16,1024]{2,1,0:T(8,128)(2,1)S(1)} collective-permute-done((bf16[24,16,1024]{2,1,0:T(8,128)(2,1)}, bf16[24,16,1024]{2,1,0:T(8,128)(2,1)S(1)}, u32[]{:S(2)}, u32[]{:S(2)}) %collective-permute-start.8) | collective-permute-done | bytes 786464 | tf_op jit(solution)/shard_map/ppermute | solution.py:555
  119.2 7.0 %collective-permute-done.16.refs_3_.refs_2_.refs_0_.refs_12_.refs_15_.refs_9_ = bf16[24,16,1024]{2,1,0:T(8,128)(2,1)} collective-permute-done((bf16[24,16,1024]{2,1,0:T(8,128)(2,1)}, bf16[24,16,1024]{2,1,0:T(8,128)(2,1)}, u32[]{:S(2)}, u32[]{:S(2)}) %collective-permute-start.16) | collective-permute-done | bytes 786464 | tf_op jit(solution)/shard_map/ppermute | solution.py:555
  137.7 5.4 %collective-permute-done.14.refs_5_.refs_3_.refs_2_.refs_16_.refs_0_.refs_19_.refs_18_ = bf16[24,16,1024]{2,1,0:T(8,128)(2,1)S(1)} collective-permute-done((bf16[24,16,1024]{2,1,0:T(8,128)(2,1)}, bf16[24,16,1024]{2,1,0:T(8,128)(2,1)S(1)}, u32[]{:S(2)}, u32[]{:S(2)}) %collective-permute-start.14) | collective-permute-done | bytes 786464 | tf_op jit(solution)/shard_map/ppermute | solution.py:555
  144.3 5.3 %subtract_divide_fusion.refs_5_.inverse_ref = f32[6,512,1024]{2,1,0:T(8,128)} fusion(f32[1024]{0:T(1024)S(1)} %copy-done.15, f32[6,512]{1,0:T(8,128)S(1)} %broadcast_subtract_fusion), kind=kLoop, calls=%fused_computation | loop fusion | flops 6291456 | bytes 12599296 | tf_op jit(solution)/shard_map/div | solution.py:705
  168.3 5.7 %collective-permute-start.25 = (bf16[24,16,1024]{2,1,0:T(8,128)(2,1)}, bf16[24,16,1024]{2,1,0:T(8,128)(2,1)}, u32[]{:S(2)}, u32[]{:S(2)}) collective-permute-start(bf16[24,16,1024]{2,1,0:T(8,128)(2,1)} %get-tuple-element.103.refs_3_), channel_id=1, source_target_pairs={{0,4},{1,5},{2,6},{3,7},{4,8},{5,9},{6,10},{7,11},{8,12},{9,13},{1... | collective-permute-start | bytes 2359304 | tf_op jit(solution)/shard_map/ppermute | solution.py:555
  175.3 5.4 %collective-permute-done.18.refs_2_ = bf16[12,48,1024]{2,1,0:T(8,128)(2,1)} collective-permute-done((bf16[12,48,1024]{2,1,0:T(8,128)(2,1)}, bf16[12,48,1024]{2,1,0:T(8,128)(2,1)}, u32[]{:S(2)}, u32[]{:S(2)}) %collective-permute-start.18) | collective-permute-done | bytes 1179680 | tf_op jit(solution)/shard_map/ppermute | solution.py:636
  190.9 6.0 %collective-permute-start.24 = (bf16[24,16,1024]{2,1,0:T(8,128)(2,1)}, bf16[24,16,1024]{2,1,0:T(8,128)(2,1)}, u32[]{:S(2)}, u32[]{:S(2)}) collective-permute-start(bf16[24,16,1024]{2,1,0:T(8,128)(2,1)} %get-tuple-element.107.refs_12_), channel_id=1, source_target_pairs={{0,4},{1,5},{2,6},{3,7},{4,8},{5,9},{6,10},{7,11},{8,12},{9,13},{1... | collective-permute-start | bytes 2359304 | tf_op jit(solution)/shard_map/ppermute | solution.py:555
  210.4 13.9 %collective-permute-start.30 = (bf16[24,16,1024]{2,1,0:T(8,128)(2,1)}, bf16[24,16,1024]{2,1,0:T(8,128)(2,1)}, u32[]{:S(2)}, u32[]{:S(2)}) collective-permute-start(bf16[24,16,1024]{2,1,0:T(8,128)(2,1)} %get-tuple-element.111.refs_8_), channel_id=1, source_target_pairs={{0,4},{1,5},{2,6},{3,7},{4,8},{5,9},{6,10},{7,11},{8,12},{9,13},{1... | collective-permute-start | bytes 2359304 | tf_op jit(solution)/shard_map/ppermute | solution.py:555
  224.6 11.3 %convert_bitcast_fusion.refs_7_.fock_ref = bf16[6,512,1024]{2,1,0:T(8,128)(2,1)} fusion(bf16[6,512,1024]{2,1,0:T(8,128)(2,1)} %refs_0_.15, bf16[1024,1024]{1,0:T(8,128)(2,1)} %all-gather.5.cloned.1.call-done, s32[1024]{0:T(1024)S(1)} %copy-done.20), kind=kOutput, calls=%fused_computation.1 | convolution fusion | flops 6447693824 | bytes 14684160 | tf_op jit(solution)/shard_map/pac,bc->pab/dot_general | solution.py:693
  240.5 5.4 %collective-permute-start.28 = (bf16[24,16,1024]{2,1,0:T(8,128)(2,1)}, bf16[24,16,1024]{2,1,0:T(8,128)(2,1)}, u32[]{:S(2)}, u32[]{:S(2)}) collective-permute-start(bf16[24,16,1024]{2,1,0:T(8,128)(2,1)} %get-tuple-element.113.refs_6_), channel_id=1, source_target_pairs={{0,4},{1,5},{2,6},{3,7},{4,8},{5,9},{6,10},{7,11},{8,12},{9,13},{1... | collective-permute-start | bytes 2359304 | tf_op jit(solution)/shard_map/ppermute | solution.py:555
  250.0 14.8 %collective-permute-done.33.refs_2_ = bf16[12,80,1024]{2,1,0:T(8,128)(2,1)} collective-permute-done((bf16[12,80,1024]{2,1,0:T(8,128)(2,1)}, bf16[12,80,1024]{2,1,0:T(8,128)(2,1)}, u32[]{:S(2)}, u32[]{:S(2)}) %collective-permute-start.33) | collective-permute-done | bytes 1966112 | tf_op jit(solution)/shard_map/ppermute | solution.py:636
  269.0 7.3 %pair_sums_0_0.1.refs_6_.refs_21_ = f32[2,96,384]{2,1,0:T(8,128)} custom-call(bf16[24,16,1024]{2,1,0:T(8,128)(2,1)} %copy-done.4, bf16[24,16,1024]{2,1,0:T(8,128)(2,1)} %get-tuple-element.118.refs_1_.refs_20_, bf16[24,16,1024]{2,1,0:T(8,128)(2,1)} %get-tuple-element.78.refs_4_.refs_2_.refs_0_.refs_3_.refs_1_, ...), custom_call_target="tpu_custom_call" | custom-call | flops 1509949440 | bytes 7864320 | tf_op jit(solution)/shard_map/pair_sums_0_0/pallas_call | solution.py:236
  280.4 7.3 %pair_sums_0_1.1.refs_6_.refs_21_ = f32[2,96,384]{2,1,0:T(8,128)} custom-call(bf16[24,16,1024]{2,1,0:T(8,128)(2,1)} %get-tuple-element.78.refs_4_.refs_2_.refs_0_.refs_3_.refs_1_, bf16[24,16,1024]{2,1,0:T(8,128)(2,1)} %get-tuple-element.118.refs_1_.refs_20_, bf16[24,16,1024]{2,1,0:T(8,128)(2,1)} %collective-permute-done.3.refs_6_.refs_2_.refs_3_.refs_0_, ...), custom_call_target="tpu_custom_call" | custom-call | flops 1509949440 | bytes 7864320 | tf_op jit(solution)/shard_map/pair_sums_0_1/pallas_call | solution.py:236
  291.8 7.3 %pair_sums_0_2.1.refs_6_.refs_16_ = f32[2,96,384]{2,1,0:T(8,128)} custom-call(bf16[24,16,1024]{2,1,0:T(8,128)(2,1)} %collective-permute-done.3.refs_6_.refs_2_.refs_3_.refs_0_, bf16[24,16,1024]{2,1,0:T(8,128)(2,1)} %get-tuple-element.118.refs_1_.refs_20_, bf16[24,16,1024]{2,1,0:T(8,128)(2,1)} %collective-permute-done.20.refs_4_.refs_2_.refs_5_, ...), custom_call_target="tpu_custom_call" | custom-call | flops 1509949440 | bytes 7864320 | tf_op jit(solution)/shard_map/pair_sums_0_2/pallas_call | solution.py:236
  309.1 9.8 %collective-permute-done.34.refs_3_.refs_0_.refs_15_ = bf16[24,16,1024]{2,1,0:T(8,128)(2,1)} collective-permute-done((bf16[24,16,1024]{2,1,0:T(8,128)(2,1)}, bf16[24,16,1024]{2,1,0:T(8,128)(2,1)}, u32[]{:S(2)}, u32[]{:S(2)}) %collective-permute-start.34) | collective-permute-done | bytes 786464 | tf_op jit(solution)/shard_map/ppermute | solution.py:556
  323.4 5.5 %pair_sums_0_late.1.refs_10_.refs_11_ = f32[2,96,384]{2,1,0:T(8,128)} custom-call(bf16[24,16,1024]{2,1,0:T(8,128)(2,1)} %copy-done.2, bf16[24,16,1024]{2,1,0:T(8,128)(2,1)} %get-tuple-element.118.refs_1_.refs_20_, bf16[24,16,1024]{2,1,0:T(8,128)(2,1)} %collective-permute-done.24.refs_2_.refs_5_.refs_15_.refs_3_.refs_4_.refs_17_, ...), custom_call_target="tpu_custom_call" | custom-call | flops 905969664 | bytes 4718592 | tf_op jit(solution)/shard_map/pair_sums_0_late/pallas_call | solution.py:236
  352.1 22.6 %collective-permute-start.45 = (f32[96,128]{1,0:T(8,128)S(1)}, f32[96,128]{1,0:T(8,128)S(1)}, u32[]{:S(2)}, u32[]{:S(2)}) collective-permute-start(f32[96,128]{1,0:T(8,128)S(1)} %add.33), channel_id=1, source_target_pairs={{0,4},{1,5},{2,6},{3,7},{4,0},{5,1},{6,2},{7,3},{8,12},{9,13},{10,... | collective-permute-start | bytes 147464 | tf_op jit(solution)/shard_map/ppermute | solution.py:718
  388.3 7.4 %ladder_0.1 = (bf16[6,32,1024]{2,1,0:T(8,128)(2,1)}, bf16[6,32,1024]{2,1,0:T(8,128)(2,1)}, bf16[6,32,1024]{2,1,0:T(8,128)(2,1)}, bf16[6,32,1024]{2,1,0:T(8,128)(2,1)}) custom-call(bf16[24,16,1024]{2,1,0:T(8,128)(2,1)} %copy-done.4, bf16[24,16,1024]{2,1,0:T(8,128)(2,1)} %get-tuple-element.78.refs_4_.refs_2_.refs_0_.refs_3_.refs_1_, ...), custom_call_target="tpu_custom_call" | custom-call | flops 2415919104 | bytes 7864320 | tf_op jit(solution)/shard_map/ladder_0/pallas_call | solution.py:348
  400.1 11.6 %collective-permute-done.49.refs_26_.refs_1_ = bf16[6,48,1024]{2,1,0:T(8,128)(2,1)} collective-permute-done((bf16[6,48,1024]{2,1,0:T(8,128)(2,1)}, bf16[6,48,1024]{2,1,0:T(8,128)(2,1)}, u32[]{:S(2)}, u32[]{:S(2)}) %collective-permute-start.49) | collective-permute-done | bytes 589856 | tf_op jit(solution)/shard_map/ppermute | solution.py:726
  413.3 9.2 %ladder_2.1 = (bf16[6,48,1024]{2,1,0:T(8,128)(2,1)}, bf16[6,48,1024]{2,1,0:T(8,128)(2,1)}, bf16[6,48,1024]{2,1,0:T(8,128)(2,1)}, bf16[6,48,1024]{2,1,0:T(8,128)(2,1)}) custom-call(bf16[24,16,1024]{2,1,0:T(8,128)(2,1)} %copy-done.3, bf16[24,16,1024]{2,1,0:T(8,128)(2,1)} %get-tuple-element.84.refs_0_.refs_3_.refs_10_.refs_8_.refs_11_.refs_1_, ...), custom_call_target="tpu_custom_call" | custom-call | flops 3623878656 | bytes 11796480 | tf_op jit(solution)/shard_map/ladder_2/pallas_call | solution.py:348
  430.2 10.5 %collective-permute-done.54.refs_1_ = bf16[6,48,1024]{2,1,0:T(8,128)(2,1)} collective-permute-done((bf16[6,48,1024]{2,1,0:T(8,128)(2,1)}, bf16[6,48,1024]{2,1,0:T(8,128)(2,1)}, u32[]{:S(2)}, u32[]{:S(2)}) %collective-permute-start.54) | collective-permute-done | bytes 589856 | tf_op jit(solution)/shard_map/ppermute | solution.py:728
  467.8 6.0 %collective-permute-done.57.refs_0_ = bf16[6,32,1024]{2,1,0:T(8,128)(2,1)} collective-permute-done((bf16[6,32,1024]{2,1,0:T(8,128)(2,1)}, bf16[6,32,1024]{2,1,0:T(8,128)(2,1)}, u32[]{:S(2)}, u32[]{:S(2)}) %collective-permute-start.57) | collective-permute-done | bytes 393248 | tf_op jit(solution)/shard_map/ppermute | solution.py:735
  (214 shorter events, 261.9 us)
Async XLA Ops:
  6.5 58.7 %all-gather.3.cloned.1.call-start = ((), (), s32[]{:S(2)}) async-start(), calls=%async_computation | async-start | bytes 1114112 | tf_op jit(solution)/shard_map/all_gather | solution.py:690
  10.1 39.0 %collective-permute-start.4 = (bf16[6,2,96,1024]{3,2,1,0:T(8,128)(2,1)}, bf16[6,2,96,1024]{3,2,1,0:T(8,128)(2,1)}, u32[]{:S(2)}, u32[]{:S(2)}) collective-permute-start(bf16[6,2,96,1024]{3,2,1,0:T(8,128)(2,1)} %get-tuple-element.79), channel_id=1, source_target_pairs={{0,1},{1,0},{2,3},{3,2},{4,5},{5,4},{6,7},{7,6},{8,9},{9,8},{10,11... | collective-permute-start | bytes 7077896 | tf_op jit(solution)/shard_map/ppermute | solution.py:593
  11.4 213.2 %all-gather.5.cloned.1.call-start = ((), (), s32[]{:S(2)}) async-start(), calls=%async_computation.1 | async-start | bytes 3145728 | tf_op jit(solution)/shard_map/all_gather | solution.py:691
  104.2 45.5 %collective-permute-start.12 = (bf16[6,2,128,1024]{3,2,1,0:T(8,128)(2,1)}, bf16[6,2,128,1024]{3,2,1,0:T(8,128)(2,1)}, u32[]{:S(2)}, u32[]{:S(2)}) collective-permute-start(bf16[6,2,128,1024]{3,2,1,0:T(8,128)(2,1)} %get-tuple-element.89), channel_id=1, source_target_pairs={{0,1},{1,0},{2,3},{3,2},{4,5},{5,4},{6,7},{7,6},{8,9},{9,8},{10,11... | collective-permute-start | bytes 9437192 | tf_op jit(solution)/shard_map/ppermute | solution.py:630
  112.5 30.5 %collective-permute-start.14 = (bf16[24,16,1024]{2,1,0:T(8,128)(2,1)}, bf16[24,16,1024]{2,1,0:T(8,128)(2,1)S(1)}, u32[]{:S(2)}, u32[]{:S(2)}) collective-permute-start(bf16[24,16,1024]{2,1,0:T(8,128)(2,1)} %get-tuple-element.92.refs_5_), channel_id=1, source_target_pairs={{0,4},{1,5},{2,6},{3,7},{4,8},{5,9},{6,10},{7,11},{8,12},{9,13},{1... | collective-permute-start | bytes 2359304 | tf_op jit(solution)/shard_map/ppermute | solution.py:555
  117.9 31.8 %collective-permute-start.15 = (bf16[24,16,1024]{2,1,0:T(8,128)(2,1)}, bf16[24,16,1024]{2,1,0:T(8,128)(2,1)}, u32[]{:S(2)}, u32[]{:S(2)}) collective-permute-start(bf16[24,16,1024]{2,1,0:T(8,128)(2,1)} %get-tuple-element.93), channel_id=1, source_target_pairs={{4,0},{5,1},{6,2},{7,3},{8,4},{9,5},{10,6},{11,7},{12,8},{13,9},{1... | collective-permute-start | bytes 2359304 | tf_op jit(solution)/shard_map/ppermute | solution.py:556
  133.8 32.1 %collective-permute-start.19 = (bf16[24,16,1024]{2,1,0:T(8,128)(2,1)}, bf16[24,16,1024]{2,1,0:T(8,128)(2,1)}, u32[]{:S(2)}, u32[]{:S(2)}) collective-permute-start(bf16[24,16,1024]{2,1,0:T(8,128)(2,1)} %get-tuple-element.96.refs_7_), channel_id=1, source_target_pairs={{0,4},{1,5},{2,6},{3,7},{4,8},{5,9},{6,10},{7,11},{8,12},{9,13},{1... | collective-permute-start | bytes 2359304 | tf_op jit(solution)/shard_map/ppermute | solution.py:555
  168.3 31.4 %collective-permute-start.25 = (bf16[24,16,1024]{2,1,0:T(8,128)(2,1)}, bf16[24,16,1024]{2,1,0:T(8,128)(2,1)}, u32[]{:S(2)}, u32[]{:S(2)}) collective-permute-start(bf16[24,16,1024]{2,1,0:T(8,128)(2,1)} %get-tuple-element.103.refs_3_), channel_id=1, source_target_pairs={{0,4},{1,5},{2,6},{3,7},{4,8},{5,9},{6,10},{7,11},{8,12},{9,13},{1... | collective-permute-start | bytes 2359304 | tf_op jit(solution)/shard_map/ppermute | solution.py:555
  174.0 30.1 %collective-permute-start.26 = (bf16[24,16,1024]{2,1,0:T(8,128)(2,1)}, bf16[24,16,1024]{2,1,0:T(8,128)(2,1)}, u32[]{:S(2)}, u32[]{:S(2)}) collective-permute-start(bf16[24,16,1024]{2,1,0:T(8,128)(2,1)} %get-tuple-element.110), channel_id=1, source_target_pairs={{4,0},{5,1},{6,2},{7,3},{8,4},{9,5},{10,6},{11,7},{12,8},{13,9},{1... | collective-permute-start | bytes 2359304 | tf_op jit(solution)/shard_map/ppermute | solution.py:556
  189.6 46.3 %collective-permute-start.23 = (bf16[24,16,1024]{2,1,0:T(8,128)(2,1)}, bf16[24,16,1024]{2,1,0:T(8,128)(2,1)S(1)}, u32[]{:S(2)}, u32[]{:S(2)}) collective-permute-start(bf16[24,16,1024]{2,1,0:T(8,128)(2,1)} %get-tuple-element.106), channel_id=1, source_target_pairs={{4,0},{5,1},{6,2},{7,3},{8,4},{9,5},{10,6},{11,7},{12,8},{13,9},{1... | collective-permute-start | bytes 2359304 | tf_op jit(solution)/shard_map/ppermute | solution.py:556
  190.9 45.0 %collective-permute-start.24 = (bf16[24,16,1024]{2,1,0:T(8,128)(2,1)}, bf16[24,16,1024]{2,1,0:T(8,128)(2,1)}, u32[]{:S(2)}, u32[]{:S(2)}) collective-permute-start(bf16[24,16,1024]{2,1,0:T(8,128)(2,1)} %get-tuple-element.107.refs_12_), channel_id=1, source_target_pairs={{0,4},{1,5},{2,6},{3,7},{4,8},{5,9},{6,10},{7,11},{8,12},{9,13},{1... | collective-permute-start | bytes 2359304 | tf_op jit(solution)/shard_map/ppermute | solution.py:555
  209.1 36.8 %collective-permute-start.29 = (bf16[24,16,1024]{2,1,0:T(8,128)(2,1)}, bf16[24,16,1024]{2,1,0:T(8,128)(2,1)}, u32[]{:S(2)}, u32[]{:S(2)}) collective-permute-start(bf16[24,16,1024]{2,1,0:T(8,128)(2,1)} %get-tuple-element.114), channel_id=1, source_target_pairs={{4,0},{5,1},{6,2},{7,3},{8,4},{9,5},{10,6},{11,7},{12,8},{13,9},{1... | collective-permute-start | bytes 2359304 | tf_op jit(solution)/shard_map/ppermute | solution.py:556
  210.4 35.5 %collective-permute-start.30 = (bf16[24,16,1024]{2,1,0:T(8,128)(2,1)}, bf16[24,16,1024]{2,1,0:T(8,128)(2,1)}, u32[]{:S(2)}, u32[]{:S(2)}) collective-permute-start(bf16[24,16,1024]{2,1,0:T(8,128)(2,1)} %get-tuple-element.111.refs_8_), channel_id=1, source_target_pairs={{0,4},{1,5},{2,6},{3,7},{4,8},{5,9},{6,10},{7,11},{8,12},{9,13},{1... | collective-permute-start | bytes 2359304 | tf_op jit(solution)/shard_map/ppermute | solution.py:555
  224.3 40.5 %collective-permute-start.33 = (bf16[12,80,1024]{2,1,0:T(8,128)(2,1)}, bf16[12,80,1024]{2,1,0:T(8,128)(2,1)}, u32[]{:S(2)}, u32[]{:S(2)}) collective-permute-start(bf16[12,80,1024]{2,1,0:T(8,128)(2,1)} %get-tuple-element.117), channel_id=1, source_target_pairs={{0,2},{1,3},{2,0},{3,1},{4,6},{5,7},{6,4},{7,5},{8,10},{9,11},{10,... | collective-permute-start | bytes 5898248 | tf_op jit(solution)/shard_map/ppermute | solution.py:636
  239.2 37.1 %collective-permute-start.27 = (bf16[24,16,1024]{2,1,0:T(8,128)(2,1)}, bf16[24,16,1024]{2,1,0:T(8,128)(2,1)S(1)}, u32[]{:S(2)}, u32[]{:S(2)}) collective-permute-start(bf16[24,16,1024]{2,1,0:T(8,128)(2,1)} %get-tuple-element.112), channel_id=1, source_target_pairs={{4,0},{5,1},{6,2},{7,3},{8,4},{9,5},{10,6},{11,7},{12,8},{13,9},{1... | collective-permute-start | bytes 2359304 | tf_op jit(solution)/shard_map/ppermute | solution.py:556
  240.5 35.8 %collective-permute-start.28 = (bf16[24,16,1024]{2,1,0:T(8,128)(2,1)}, bf16[24,16,1024]{2,1,0:T(8,128)(2,1)}, u32[]{:S(2)}, u32[]{:S(2)}) collective-permute-start(bf16[24,16,1024]{2,1,0:T(8,128)(2,1)} %get-tuple-element.113.refs_6_), channel_id=1, source_target_pairs={{0,4},{1,5},{2,6},{3,7},{4,8},{5,9},{6,10},{7,11},{8,12},{9,13},{1... | collective-permute-start | bytes 2359304 | tf_op jit(solution)/shard_map/ppermute | solution.py:555
  247.2 40.5 %collective-permute-start.31 = (bf16[24,16,1024]{2,1,0:T(8,128)(2,1)}, bf16[24,16,1024]{2,1,0:T(8,128)(2,1)}, u32[]{:S(2)}, u32[]{:S(2)}) collective-permute-start(bf16[24,16,1024]{2,1,0:T(8,128)(2,1)} %get-tuple-element.115), channel_id=1, source_target_pairs={{4,0},{5,1},{6,2},{7,3},{8,4},{9,5},{10,6},{11,7},{20,16},{21,17},... | collective-permute-start | bytes 2359304 | tf_op jit(solution)/shard_map/ppermute | solution.py:556
  248.5 39.2 %collective-permute-start.32 = (bf16[24,16,1024]{2,1,0:T(8,128)(2,1)}, bf16[24,16,1024]{2,1,0:T(8,128)(2,1)}, u32[]{:S(2)}, u32[]{:S(2)}) collective-permute-start(bf16[24,16,1024]{2,1,0:T(8,128)(2,1)} %get-tuple-element.116.refs_3_), channel_id=1, source_target_pairs={{4,8},{5,9},{6,10},{7,11},{8,12},{9,13},{10,14},{11,15},{20,24},{2... | collective-permute-start | bytes 2359304 | tf_op jit(solution)/shard_map/ppermute | solution.py:555
  397.3 30.6 %collective-permute-start.52 = (bf16[6,48,1024]{2,1,0:T(8,128)(2,1)}, bf16[6,48,1024]{2,1,0:T(8,128)(2,1)}, u32[]{:S(2)}, u32[]{:S(2)}) collective-permute-start(bf16[6,48,1024]{2,1,0:T(8,128)(2,1)} %get-tuple-element.141), channel_id=1, source_target_pairs={{4,3},{5,2},{6,1},{7,0},{8,15},{9,14},{10,13},{11,12},{20,19},{21,... | collective-permute-start | bytes 1769480 | tf_op jit(solution)/shard_map/ppermute | solution.py:726
  398.6 30.9 %collective-permute-start.53 = (bf16[6,48,1024]{2,1,0:T(8,128)(2,1)}, bf16[6,48,1024]{2,1,0:T(8,128)(2,1)}, u32[]{:S(2)}, u32[]{:S(2)}) collective-permute-start(bf16[6,48,1024]{2,1,0:T(8,128)(2,1)} %get-tuple-element.142), channel_id=1, source_target_pairs={{4,5},{5,4},{6,7},{7,6},{8,9},{9,8},{10,11},{11,10},{20,21},{21,20... | collective-permute-start | bytes 1769480 | tf_op jit(solution)/shard_map/ppermute | solution.py:729
  422.6 38.3 %collective-permute-start.55 = (bf16[6,48,1024]{2,1,0:T(8,128)(2,1)}, bf16[6,48,1024]{2,1,0:T(8,128)(2,1)}, u32[]{:S(2)}, u32[]{:S(2)}) collective-permute-start(bf16[6,48,1024]{2,1,0:T(8,128)(2,1)} %get-tuple-element.144), channel_id=1, source_target_pairs={{4,0},{5,1},{6,2},{7,3},{8,12},{9,13},{10,14},{11,15},{20,16},{21,... | collective-permute-start | bytes 1769480 | tf_op jit(solution)/shard_map/ppermute | solution.py:728
  427.9 48.2 %collective-permute-start.58 = (bf16[6,48,1024]{2,1,0:T(8,128)(2,1)}, bf16[6,48,1024]{2,1,0:T(8,128)(2,1)S(1)}, u32[]{:S(2)}, u32[]{:S(2)}) collective-permute-start(bf16[6,48,1024]{2,1,0:T(8,128)(2,1)} %get-tuple-element.147), channel_id=1, source_target_pairs={{0,2},{1,3},{2,0},{3,1},{4,6},{5,7},{6,4},{7,5},{8,10},{9,11},{10,... | collective-permute-start | bytes 1769480 | tf_op jit(solution)/shard_map/ppermute | solution.py:735
  429.5 50.0 %collective-permute-start.59 = (bf16[6,48,1024]{2,1,0:T(8,128)(2,1)}, bf16[6,48,1024]{2,1,0:T(8,128)(2,1)}, u32[]{:S(2)}, u32[]{:S(2)}) collective-permute-start(bf16[6,48,1024]{2,1,0:T(8,128)(2,1)} %get-tuple-element.148), channel_id=1, source_target_pairs={{0,3},{1,2},{2,1},{3,0},{4,7},{5,6},{6,5},{7,4},{8,11},{9,10},{10,... | collective-permute-start | bytes 1769480 | tf_op jit(solution)/shard_map/ppermute | solution.py:735
  441.1 32.7 %collective-permute-start.57 = (bf16[6,32,1024]{2,1,0:T(8,128)(2,1)}, bf16[6,32,1024]{2,1,0:T(8,128)(2,1)}, u32[]{:S(2)}, u32[]{:S(2)}) collective-permute-start(bf16[6,32,1024]{2,1,0:T(8,128)(2,1)} %get-tuple-element.146), channel_id=1, source_target_pairs={{0,3},{1,2},{2,1},{3,0},{4,7},{5,6},{6,5},{7,4},{8,11},{9,10},{10,... | collective-permute-start | bytes 1179656 | tf_op jit(solution)/shard_map/ppermute | solution.py:735
  (59 other events, 938.0 us)
Sparse Core Ops, SparseCore 0:
  11.5 42.9 all-gather.2
  118.0 33.9 all-gather.4

commit v4 on v3

--- a/solution.py
+++ b/solution.py
@@ -10,6 +10,7 @@
 PLANES = 4
 INNER = 4
 CHUNK = 16
+HALF = 8
 CHUNKS = 8
 WIDE = 5
 LANES = 128
@@ -136,6 +137,12 @@
     return jnp.where(same, gram, 0.0).reshape(-1, depth, gram.shape[1]).sum(axis=1)
 
 
+def split_rows(block):
+    pairs, depth, width = block.shape
+    wide = block.astype(jnp.float32).reshape(pairs, depth // HALF, HALF, width)
+    return [wide[:, n].reshape(pairs * HALF, width).astype(block.dtype) for n in range(depth // HALF)]
+
+
 def exact_dot(left, right):
     return jnp.dot(left, right, preferred_element_type=jnp.float32, precision=lax.Precision.HIGHEST)
 
@@ -165,7 +172,8 @@
         for c in range(chunks):
             for n in range(sides):
                 pltpu.make_async_copy(refs[0], ints.at[c, n], sems.at[c, len(parts) + n]).wait()
-                turned[c, n] = ints[c, n].reshape(rows * depth, width).T
+                for h, half in enumerate(split_rows(ints[c, n])):
+                    turned[c, h, n * rows * HALF : (n + 1) * rows * HALF] = half
             for n in range(len(parts)):
                 pltpu.make_async_copy(refs[0], amp.at[c, n], sems.at[c, n]).wait()
 
@@ -175,12 +183,15 @@
             else:
                 p = jnp.where(plane < 2, n + parts[0], n + parts[0] + 1)
             place = pl.ds(pl.multiple_of(p * rows, 8), rows)
+            gram = jnp.zeros((rows * HALF, sides * rows * HALF), jnp.float32)
+            for c in range(chunks):
+                for h, half in enumerate(split_rows(amp[c, n])):
+                    gram += lax.dot_general(
+                        half, turned[c, h], (((1,), (1,)), ((), ())), preferred_element_type=jnp.float32
+                    )
             for side in range(sides):
-                gram = jnp.zeros((rows * depth, rows * depth), jnp.float32)
-                for c in range(chunks):
-                    left = amp[c, n].reshape(rows * depth, width)
-                    gram += jnp.dot(left, turned[c, side], preferred_element_type=jnp.float32)
-                total[side + (0 if own_too else 1), place] += kept_sum(gram, depth)
+                kept = kept_sum(gram[:, side * rows * HALF : (side + 1) * rows * HALF], HALF)
+                total[side + (0 if own_too else 1), place] += kept
             return carry
 
         lax.fori_loop(0, len(parts), add_part, 0)
@@ -196,7 +207,7 @@
     lanes = total.shape[2]
     summed = jnp.zeros((total.shape[1], LANES), jnp.float32)
     near = jnp.where(plane < 2, 0, PLANES - 1)
-    row_id = lax.broadcasted_iota(jnp.int32, (lanes, LANES), 0) // CHUNK
+    row_id = lax.broadcasted_iota(jnp.int32, (lanes, LANES), 0) // HALF
     col_id = lax.broadcasted_iota(jnp.int32, (lanes, LANES), 1)
     pair_id = pair_at(row_id, me, pair_dev)
     for side, at in ((0, plane), (1, near)):
@@ -221,7 +232,7 @@
             amp_from = [sources[late_plane(z)]] if late else [early[n] for n in parts]
             int_from = [int_own[chunk]] if own_too else []
             if near_too:
-                int_from.append(got[z - 1][CHUNKS + chunk - WIDE])
+                int_from.append(got[z - 1][CHUNKS + 1 + chunk - WIDE])
             entry = table.setdefault(z, ([], []))
             entry[0].append(numbered(arrays, amp_from))
             entry[1].append(numbered(arrays, int_from))
@@ -242,7 +253,7 @@
         scratch_shapes=[
             pltpu.VMEM((len(chunks), len(parts), rows, depth, width), jnp.bfloat16),
             pltpu.VMEM((len(chunks), sides, rows, depth, width), jnp.bfloat16),
-            pltpu.VMEM((len(chunks), sides, width, block), jnp.bfloat16),
+            pltpu.VMEM((len(chunks), depth // HALF, sides * rows * HALF, width), jnp.bfloat16),
             pltpu.VMEM(acc.shape, jnp.float32),
             pltpu.SemaphoreType.DMA((len(chunks), len(parts) + sides)),
         ],
@@ -258,7 +269,7 @@
 
 def places_kernel(pair_dev, col_ref, row_ref, keep_ref):
     plane, me = here()
-    rows, depth = INNER * pair_dev, CHUNK
+    rows, depth = INNER * pair_dev, HALF
     block = rows * depth
     col = lax.broadcasted_iota(jnp.int32, (LANES, PLANES * block), 1) // depth
     col_plane = sum((col >= p * rows).astype(jnp.int32) for p in range(1, PLANES))
@@ -275,7 +286,7 @@
 
 
 def ladder_places(pair_dev):
-    block = INNER * pair_dev * CHUNK
+    block = INNER * pair_dev * HALF
     shapes = [(LANES, PLANES * block), (2, block, LANES), (block, PLANES * block)]
     return pl.pallas_call(
         functools.partial(places_kernel, pair_dev),
@@ -286,83 +297,118 @@
     )()
 
 
-def ladder_kernel(table_of, wide, pair_dev, *refs):
-    sides = 1 if wide else 2
+def ladder_kernel(table_of, wide_count, pair_dev, *refs):
     own = refs[0]
-    count = sides * INNER
-    sum_ref, mask_ref, col_ref, row_ref, keep_ref = refs[-8 - count : -3 - count]
-    outs = refs[-3 - count : -3]
-    amp, spread, sems = refs[-3:]
+    outs = refs[-8 - 3 * INNER : -8]
+    sum_ref, mask_ref, col_ref, row_ref, keep_ref = refs[-13 - 3 * INNER : -8 - 3 * INNER]
+    amp, near_spread, wide_spread, halves, near_terms, wide_terms, in_sems, out_sems = refs[-8:]
+    chunks, _, rows, depth, width = amp.shape
+    narrow_count = chunks - wide_count
     plane, _ = here()
-    rows, depth, width = amp.shape[2:]
-    block = rows * depth
+    middle = (plane == 1) | (plane == 2)
     for z, table in table_of.items():
 
         @pl.when(plane == z)
         def _():
             for n, sources in enumerate(table):
-                for p in range(PLANES):
-                    pltpu.make_async_copy(refs[sources[p]], amp.at[n, p], sems.at[n, p]).start()
-
-    def work():
-        ladder = jnp.where(mask_ref[...] > 0, sum_ref[...], 0.0).astype(jnp.bfloat16)
-        ladder = pad_rows(ladder)
-        for side in range(sides):
-            picked = jnp.dot(row_ref[side], ladder, preferred_element_type=jnp.float32).astype(jnp.bfloat16)
-            full = jnp.dot(picked, col_ref[...], preferred_element_type=jnp.float32).astype(jnp.bfloat16)
-            spread[side] = jnp.where(keep_ref[...] > 0, full, jnp.zeros_like(full))
-
-        def one_chunk(n, carry):
-            for p in range(PLANES):
-                pltpu.make_async_copy(own, amp.at[n, p], sems.at[n, p]).wait()
-            columns = amp[n].reshape(PLANES * block, width)
-            place = pl.ds(pl.multiple_of(n * depth, depth), depth)
-            for side in range(sides):
-                term = jnp.dot(spread[side], columns, preferred_element_type=jnp.float32).astype(jnp.bfloat16)
-                term = term.reshape(INNER, pair_dev, depth, width)
-                for flip in range(INNER):
-                    outs[side * INNER + flip][:, place, :] = term[flip]
+                if sources is not None:
+                    for p in range(PLANES):
+                        pltpu.make_async_copy(refs[sources[p]], amp.at[n, p], in_sems.at[n, p]).start()
+
+    ladder = jnp.where(mask_ref[...] > 0, sum_ref[...], 0.0).astype(jnp.bfloat16)
+    ladder = pad_rows(ladder)
+
+    def spread_of(side):
+        picked = jnp.dot(row_ref[side], ladder, preferred_element_type=jnp.float32).astype(jnp.bfloat16)
+        full = jnp.dot(picked, col_ref[...], preferred_element_type=jnp.float32).astype(jnp.bfloat16)
+        return jnp.where(keep_ref[...] > 0, full, jnp.zeros_like(full))
+
+    size = rows * HALF
+    wide_spread[...] = spread_of(0)
+
+    def store(terms, first_out, n, slot, sides):
+        place = pl.ds(pl.multiple_of(n * depth, depth), depth)
+        return [
+            pltpu.make_async_copy(terms.at[slot, k], outs[first_out + k].at[:, place, :], out_sems.at[slot, k])
+            for k in range(sides * INNER)
+        ]
+
+    def work(n, spread, terms, first_out, at, slot, sides):
+        for p in range(PLANES):
+            pltpu.make_async_copy(own, amp.at[n, p], in_sems.at[n, p]).wait()
+        for p in range(PLANES):
+            for h, half in enumerate(split_rows(amp[n, p])):
+                halves[h, p * size : (p + 1) * size] = half
+        parts = [
+            jnp.dot(spread[...], halves[h], preferred_element_type=jnp.float32).reshape(-1, HALF, width)
+            for h in range(depth // HALF)
+        ]
+        term = jnp.concatenate(parts, axis=1).astype(jnp.bfloat16)
+        terms[slot] = term.reshape(sides * INNER, pair_dev, depth, width)
+        for copy in store(terms, first_out, at, slot, sides):
+            copy.start()
+
+    @pl.when(middle)
+    def _():
+        near_spread[:size] = wide_spread[...]
+        near_spread[size:] = spread_of(1)
+
+        def one(n, carry):
+            work(n, near_spread, near_terms, 0, n, n, 2)
             return carry
 
-        lax.fori_loop(0, amp.shape[0], one_chunk, 0)
-
-    if wide:
-        work()
-    else:
-        pl.when((plane == 1) | (plane == 2))(work)
-
-
-def ladder_terms(chunks, own, plus, minus, summed, mask, places, after=()):
-    rows, depth, width = own[chunks[0]].shape
+        lax.fori_loop(0, narrow_count, one, 0)
+        for n in range(narrow_count):
+            for copy in store(near_terms, 0, n, n, 2):
+                copy.wait()
+
+    def one(n, carry):
+        work(n + narrow_count, wide_spread, wide_terms, 2 * INNER, n, n, 1)
+        return carry
+
+    lax.fori_loop(0, wide_count, one, 0)
+    for n in range(wide_count):
+        for copy in store(wide_terms, 2 * INNER, n, n, 1):
+            copy.wait()
+
+
+def ladder_terms(narrow, wide, own, plus, minus, summed, mask, places):
+    rows, depth, width = own[wide[0]].shape
     pair_dev = rows // INNER
-    wide = chunks[0] < WIDE
-    arrays, table = [], {}
-    for chunk in chunks:
-        for z, sources in place_sources(own[chunk], plus, minus, chunk).items():
-            table.setdefault(z, []).append(numbered(arrays, [sources[p] for p in range(PLANES)]))
-    operands = arrays + list(after)
-    far = len(operands)
-    operands += [summed, mask, *places]
-    sides = 1 if wide else 2
-    block = rows * depth
+    arrays, table = [], {z: [] for z in range(PLANES)}
+    for chunk in narrow + wide:
+        sources = place_sources(own[chunk], plus, minus, chunk)
+        for z in range(PLANES):
+            numbers = numbered(arrays, [sources[z][p] for p in range(PLANES)]) if z in sources else None
+            table[z].append(numbers)
+    far = len(arrays)
+    operands = arrays + [summed, mask, *places]
+    size = rows * HALF
+    sems = max(len(narrow), len(wide))
+    shapes = [(pair_dev, len(group) * depth, width) for group in (narrow, narrow, wide) for _ in range(INNER)]
     return pl.pallas_call(
-        functools.partial(ladder_kernel, table, wide, pair_dev),
-        out_shape=[jax.ShapeDtypeStruct((pair_dev, len(chunks) * depth, width), jnp.bfloat16)] * (sides * INNER),
+        functools.partial(ladder_kernel, table, len(wide), pair_dev),
+        out_shape=[jax.ShapeDtypeStruct(shape, jnp.bfloat16) for shape in shapes],
         in_specs=[pl.BlockSpec(memory_space=pl.ANY)] * far
         + [pl.BlockSpec(memory_space=pltpu.VMEM)] * (len(operands) - far),
-        out_specs=[pl.BlockSpec(memory_space=pltpu.VMEM)] * (sides * INNER),
+        out_specs=[pl.BlockSpec(memory_space=pl.ANY)] * len(shapes),
         scratch_shapes=[
-            pltpu.VMEM((len(chunks), PLANES, rows, depth, width), jnp.bfloat16),
-            pltpu.VMEM((sides, block, PLANES * block), jnp.bfloat16),
-            pltpu.SemaphoreType.DMA((len(chunks), PLANES)),
+            pltpu.VMEM((len(narrow) + len(wide), PLANES, rows, depth, width), jnp.bfloat16),
+            pltpu.VMEM((2 * size, PLANES * size), jnp.bfloat16),
+            pltpu.VMEM((size, PLANES * size), jnp.bfloat16),
+            pltpu.VMEM((depth // HALF, PLANES * size, width), jnp.bfloat16),
+            pltpu.VMEM((len(narrow), 2 * INNER, pair_dev, depth, width), jnp.bfloat16),
+            pltpu.VMEM((len(wide), INNER, pair_dev, depth, width), jnp.bfloat16),
+            pltpu.SemaphoreType.DMA((len(narrow) + len(wide), PLANES)),
+            pltpu.SemaphoreType.DMA((sems, 2 * INNER)),
         ],
         compiler_params=pltpu.CompilerParams(vmem_limit_bytes=VMEM_BYTES),
         cost_estimate=pl.CostEstimate(
-            flops=2 * PLANES * block * block * width * sides * len(chunks),
-            bytes_accessed=(PLANES + sides) * block * width * 2 * len(chunks),
+            flops=2 * PLANES * size * size * width * 2 * (2 * len(narrow) + len(wide)),
+            bytes_accessed=(PLANES + 2) * rows * depth * width * 2 * (len(narrow) + len(wide)),
             transcendentals=0,
         ),
-        name=f"ladder_{chunks[0]}",
+        name="ladder",
     )(*operands)
 
 
@@ -527,8 +573,8 @@
 
 
 def line_round(step, own, int_own, got, after, done_with):
-    narrow = CHUNKS - WIDE
     first, last = 0, 2
+    int_first = CHUNKS + 1
     choices = []
     for have in got:
         if step < WIDE:
@@ -537,8 +583,8 @@
             table = {0: own[step], 1: own[step], 2: have[step - WIDE]}
         else:
             table = {1: have[step - CHUNKS]}
-            if step < CHUNKS + narrow:
-                table[0] = int_own[WIDE + step - CHUNKS]
+            if int_first <= step < int_first + CHUNKS - WIDE:
+                table[0] = int_own[WIDE + step - int_first]
             else:
                 first = 1
             if step < 2 * WIDE:
@@ -580,83 +626,77 @@
     def rounds(*steps, after=()):
         for step in steps:
             before = arrived(step - 2) if step >= 2 else []
-            line_round(step, own, int_own, got, in_turn(before + list(after)) if step >= 2 else [], done_with)
-
-    groups = ((0, 1), (1, 2), (2, 4), (4, 6), (6, CHUNKS))
-    core_groups = ((0, 2), (2, CHUNKS))
-    cores = move(
-        [amplitudes],
-        [(pair_dev, 2, (end - first) * CHUNK, width) for first, end in core_groups],
-        [one for n, group in enumerate(core_groups) for one in core_moves(0, group, n)],
-        "move_core",
-    )
-    cores = [lax.ppermute(core, "blk", inner_perm(1)) for core in cores]
-    (across,) = move(
-        [amplitudes, cores[0]],
-        [across_shape(groups[0])],
-        across_moves(0, 1, 0, groups[0], pair_dev, 0),
-        "move_across",
-    )
-    waits = ((), (), (0,), (2,), (4,))
+            line_round(step, own, int_own, got, in_turn(before + list(after)) if step not in (0, 1, 4) else [], done_with)
+
+    groups = ((2, 4), (4, CHUNKS))
+    core_first = groups[0][0]
+    flips = (2, 3, 1)
+    pieces = [
+        (0, flip, rows_of(chunk), len(flips) * chunk + n, slice(None))
+        for chunk in range(core_first)
+        for n, flip in enumerate(flips)
+    ]
+    def send_across(source, core, first, group):
+        (across,) = done_with(
+            move(
+                in_turn([source, core]),
+                [across_shape(group)],
+                across_moves(0, 1, first, group, pair_dev, 0),
+                f"move_across_{group[0]}",
+            )
+        )
+        return lax.ppermute(across, "blk", inner_perm(2))
+
+    def assemble(source, core, across, first, group, found_in, before=()):
+        operands = in_turn([source, core, across] + list(before))
+        moves = own_moves(0, 1, first, 2, group, pair_dev, 0)
+        found = done_with(move(operands, [full] * (group[1] - group[0]), moves, f"move_own_{group[0]}"))
+        found_in.update(zip(range(*group), found))
+
+    def send_core(source, first):
+        shape = (pair_dev, 2, (CHUNKS - first) * CHUNK, width)
+        (core,) = done_with(move(in_turn([source]), [shape], core_moves(0, (first, CHUNKS), 0), f"move_core_{first}"))
+        return lax.ppermute(core, "blk", inner_perm(1))
+
     int_groups = ((WIDE, CHUNKS), (0, WIDE))
-    for n, group in enumerate(groups):
-        across = lax.ppermute(across, "blk", inner_perm(2))
-        size = group[1] - group[0]
-        mine = int(group[0] >= core_groups[1][0])
-        moves = own_moves(0, 1, core_groups[mine][0], 2, group, pair_dev, 0)
-        shapes = [full] * size
-        operands = [amplitudes, cores[mine], across]
-        if n + 1 < len(groups):
-            then = int(groups[n + 1][0] >= core_groups[1][0])
-            moves += across_moves(0, 3, core_groups[then][0], groups[n + 1], pair_dev, size)
-            shapes.append(across_shape(groups[n + 1]))
-            operands.append(cores[then])
-        else:
-            moves += across_moves(3, 4, 0, int_groups[0], pair_dev, size)
-            shapes.append(across_shape(int_groups[0]))
-            operands += [integrals, int_core]
-        if n == 3:
-            moves += core_moves(4, (0, CHUNKS), size + 1)
-            shapes.append((pair_dev, 2, CHUNKS * CHUNK, width))
-            operands.append(integrals)
-        if n == 2:
-            operands += beside
-        for step in waits[n]:
-            operands += arrived(step)
-        found = done_with(move(in_turn(operands), shapes, moves, f"move_own_{group[0]}"))
-        own.update(zip(range(*group), found))
-        across = found[size]
-        if n == 3:
-            int_core = lax.ppermute(found[size + 1], "blk", inner_perm(1))
-        rounds(*((0,), (1,), (2, 3), (4, 5), (6,))[n])
-    rounds(7, after=beside_later[1:])
-
-    def own_integrals(n, across):
-        group = int_groups[n]
-        across = lax.ppermute(across, "blk", inner_perm(2))
-        size = group[1] - group[0]
-        moves = own_moves(0, 1, 0, 2, group, pair_dev, 0)
-        shapes = [full] * size
-        if n + 1 < len(int_groups):
-            moves += across_moves(0, 1, 0, int_groups[n + 1], pair_dev, size)
-            shapes.append(across_shape(int_groups[n + 1]))
-        found = done_with(move(in_turn([integrals, int_core, across]), shapes, moves, f"move_ints_{group[0]}"))
-        int_own.update(zip(range(*group), found))
-        return found[-1]
+    sent = done_with(move([amplitudes], [(pair_dev, CHUNK, width)] * len(pieces), pieces, "move_first"))
+    sent = [lax.ppermute(part, "blk", inner_perm(flips[n % len(flips)])) for n, part in enumerate(sent)]
+    core = send_core(amplitudes, core_first)
+    for chunk in range(core_first):
+        parts = sent[len(flips) * chunk : len(flips) * (chunk + 1)]
+        moves = [(0, 0, rows_of(chunk), 0, slice(0, pair_dev))]
+        for n, flip in enumerate(flips):
+            moves.append((1 + n, None, slice(None), 0, slice(flip * pair_dev, (flip + 1) * pair_dev)))
+        (own[chunk],) = done_with(move(in_turn([amplitudes] + parts), [full], moves, "move_own"))
+        rounds(chunk)
+        if chunk == 0:
+            across = send_across(amplitudes, core, core_first, groups[0])
+    int_core = send_core(integrals, 0)
+    assemble(amplitudes, core, across, core_first, groups[0], own, arrived(0))
+    across = send_across(amplitudes, core, core_first, groups[1])
+    rounds(2, after=beside)
+    rounds(3)
+    assemble(amplitudes, core, across, core_first, groups[1], own, arrived(2))
+    rounds(4)
+    across = send_across(integrals, int_core, 0, int_groups[0])
+    rounds(5)
+    rounds(6, after=beside_later[1:])
+    across_later = send_across(integrals, int_core, 0, int_groups[1])
+    rounds(7, after=beside_later[:1])
+    rounds(8)
+    assemble(integrals, int_core, across, 0, int_groups[0], int_own)
 
     wide, narrow = tuple(range(WIDE)), tuple(range(WIDE, CHUNKS))
-    acc = jnp.zeros((2, PLANES * rows, rows * CHUNK), jnp.float32)
+    acc = jnp.zeros((2, PLANES * rows, rows * HALF), jnp.float32)
 
     def add(*what, acc, **more):
         return done_with([add_pair_sums(*what, own, got, int_own, acc, after=in_turn([]), **more)])[0]
 
-    across = own_integrals(0, across)
-    rounds(8)
     acc = add(narrow, (0, 1, 2), True, False, acc=acc)
     rounds(9)
-    rounds(10, after=beside_later[:1])
+    rounds(10)
+    assemble(integrals, int_core, across_later, 0, int_groups[1], int_own)
     rounds(11)
-    own_integrals(1, across)
     for part in range(3):
         acc = add(wide, (part,), True, False, acc=acc)
         rounds(12 + part)
@@ -713,31 +753,31 @@
         amplitudes, integrals, hole, [piece], [fock_term, inverse, mask, places[2]]
     )
     summed = acc + lax.ppermute(acc, "blk", inner_perm(1))
-    summed = summed + lax.ppermute(summed, "rep", [(0, 1), (1, 0)])
-    for flip in (2, 4, 8):
-        summed = summed + lax.ppermute(summed, "blk", [(i, i ^ flip) for i in range(PLANES * INNER)])
-
-    terms = functools.partial(ladder_terms, own=own, plus=plus, minus=minus, summed=summed, mask=mask, places=places)
-    ladder_groups = (tuple(range(WIDE, CHUNKS)), tuple(range(2)), tuple(range(2, WIDE)))
-    outside, inside = {}, {}
-    narrow = terms(ladder_groups[0])
-    for flip in (2, 3):
-        inside[0, flip] = lax.ppermute(narrow[flip], "blk", inner_perm(flip, (1, 2)))
-        outside[flip] = lax.ppermute(narrow[INNER + flip], "blk", outward_perm(flip))
-    for flip in (0, 1):
-        outside[flip] = lax.ppermute(narrow[INNER + flip], "blk", outward_perm(flip))
-    inside[0, 1] = lax.ppermute(narrow[1], "blk", inner_perm(1, (1, 2)))
-    inside[0, 0] = narrow[0]
-    for n in (1, 2):
-        wide = terms(ladder_groups[n], after=[inside[0, 2], outside[2]] if n == 2 else [narrow[0]])
-        inside[n, 0] = wide[0]
-        for flip in (2, 3, 1):
-            inside[n, flip] = lax.ppermute(wide[flip], "blk", inner_perm(flip))
+    count = PLANES * INNER
+    for flips in (((1, 0), (0, 2), (1, 2)), ((0, 4), (0, 8), (0, 12))):
+        parts = [
+            lax.ppermute(
+                summed,
+                ("rep", "blk"),
+                [(r * count + i, (r ^ rep) * count + (i ^ flip)) for r in range(2) for i in range(count)],
+            )
+            for rep, flip in flips
+        ]
+        summed = (summed + parts[0]) + (parts[1] + parts[2])
+    wide, narrow = tuple(range(WIDE)), tuple(range(WIDE, CHUNKS))
+    found = ladder_terms(narrow, wide, own, plus, minus, summed, mask, places)
+    outside, inside, every = {}, {}, {}
+    for flip in (2, 3, 0, 1):
+        inside[flip] = lax.ppermute(found[flip], "blk", inner_perm(flip, (1, 2))) if flip else found[flip]
+        outside[flip] = lax.ppermute(found[INNER + flip], "blk", outward_perm(flip))
+    for flip in (2, 3, 1, 0):
+        term = found[2 * INNER + flip]
+        every[flip] = lax.ppermute(term, "blk", inner_perm(flip)) if flip else term
     update = fock_term
-    order = ((1, 0), (1, 1), (2, 0), (2, 1), (0, 2), (0, 3), (0, 1), (0, 0), (1, 2), (1, 3), (2, 2), (2, 3))
-    for n, flip in order:
-        pieces = [inside[n, flip]] + ([outside[flip]] if n == 0 else [])
-        update = add_and_scale(update, inverse, pieces, flip, ladder_groups[n][0])
+    order = ((1, 0), (1, 1), (0, 2), (0, 3), (0, 1), (0, 0), (1, 2), (1, 3))
+    for is_wide, flip in order:
+        pieces = [every[flip]] if is_wide else [inside[flip], outside[flip]]
+        update = add_and_scale(update, inverse, pieces, flip, 0 if is_wide else WIDE)
     return update
 
 

time: 492 us -> 448 us (0.911)
  waiting for transfers between devices: 160 us -> 136 us
  Pallas kernels: 149 us -> 130 us
    ppermute x16, waiting for transfers between devices: 27.5 us -> 0.12 us  [line_round(): got[0][step] = lax.ppermute(sends[0], 'blk', plane_perm(1, first, last))]
    ppermute x16, waiting for transfers between devices: 35.2 us -> 61.6 us  [line_round(): lax.ppermute(sends[1], 'blk', plane_perm(-1, PLANES - 1 - last, PLANES -...]
    ppermute x27 -> x28, waiting for transfers between devices: 95.3 us -> 72.4 us  [the longest x4 42.6 us: line_plan(): outside[flip] = lax.ppermute(found[INNER + flip], 'blk', outward_perm(flip))]
    pallas_call x3 -> x1, Pallas kernels: 20.4 us -> 9.86 us  [ladder_terms(): pl.pallas_call(functools.partial(ladder_kernel, table, len(wide), pair_de...]
    pallas_call x12 -> x8, Pallas kernels: 30 us -> 22.9 us  [add_and_scale(): pl.pallas_call(functools.partial(scale_kernel, flip, first, len(pieces)),...]
    pallas_call x9 -> x13, Pallas kernels: 30.8 us -> 37 us  [move(): return list(call(*operands))]
    ppermute x16, starting transfers between devices: 67.9 us -> 73 us  [line_round(): got[0][step] = lax.ppermute(sends[0], 'blk', plane_perm(1, first, last))]
    pallas_call x9, Pallas kernels: 39.8 us -> 34.8 us  [add_pair_sums(): pl.pallas_call(functools.partial(pair_kernel, table, near_too, own_too, p...]
  transfers between devices with their start and end apart: 62 -> 63, of which waited for: 29 -> 26; matrix products, arithmetic and copies ran while one was open for 4% -> 4% of each run, Pallas kernels for 27% -> 25%
where the time goes in v4:
time: 448 us; the launch traced here: 445 us
  starting transfers between devices  139 us (31%)
  waiting for transfers between devices  136 us (30%)
  Pallas kernels  130 us (29%)
  between operations  14.3 us (3%)
  matrix products  11.3 us (3%)
  other arithmetic  7.94 us (2%)
  local copies, waits for them, and re-layouts  6.77 us (2%)
    ppermute x16, starting transfers between devices, line_round(): got[0][step] = lax.ppermute(sends[0], 'blk', plane_perm(1, first, last))  73 us
    ppermute x16, waiting for transfers between devices, line_round(): lax.ppermute(sends[1], 'blk', plane_perm(-1, PLANES - 1 - last, PLANES -...  61.6 us
    ppermute x4, waiting for transfers between devices, line_plan(): outside[flip] = lax.ppermute(found[INNER + flip], 'blk', outward_perm(flip))  42.6 us
    pallas_call x13, Pallas kernels, move(): return list(call(*operands))  37 us
    pallas_call x9, Pallas kernels, add_pair_sums(): pl.pallas_call(functools.partial(pair_kernel, table, near_too, own_too, p...  34.8 us
    pallas_call x13, Pallas kernels, pick(): pl.pallas_call(functools.partial(pick_kernel, tables), out_shape=[jax.Sha...  24.5 us
    pallas_call x8, Pallas kernels, add_and_scale(): pl.pallas_call(functools.partial(scale_kernel, flip, first, len(pieces)),...  22.9 us
    ppermute x6, starting transfers between devices, line_plan(): lax.ppermute(summed, ('rep', 'blk'), [(r * count + i, (r ^ rep) * count +...  22.5 us
  transfers between devices with their start and end apart: 63, of which 26 were waited for; matrix products, arithmetic and copies ran while one was open for 4% of the time, Pallas kernels for 25%

profile of v4, /device:TPU:0, one launch (start us, length us, event | category | flops | bytes accessed | tf_op | source)
XLA Modules:
  0.0 445.2 jit_solution(16890871322409475398)
XLA Ops:
  42.9 5.5 %collective-permute-start.5 = (bf16[24,16,1024]{2,1,0:T(8,128)(2,1)}, bf16[24,16,1024]{2,1,0:T(8,128)(2,1)}, u32[]{:S(2)}, u32[]{:S(2)}) collective-permute-start(bf16[24,16,1024]{2,1,0:T(8,128)(2,1)} %move_own.2.refs_2_.refs_0_.refs_3_.refs_15_), channel_id=1, source_target_pairs={{0,4},{1,5},{2,6},{3,7},{4,8},{5,9},{6,10},{7,11},{8,12},{9,13},{1... | collective-permute-start | bytes 2359304 | tf_op jit(solution)/shard_map/ppermute | solution.py:601
  51.2 14.8 %collective-permute-done.6.refs_4_.refs_2_.refs_0_.refs_16_ = bf16[24,16,1024]{2,1,0:T(8,128)(2,1)S(1)} collective-permute-done((bf16[24,16,1024]{2,1,0:T(8,128)(2,1)}, bf16[24,16,1024]{2,1,0:T(8,128)(2,1)S(1)}, u32[]{:S(2)}, u32[]{:S(2)}) %collective-permute-start.6) | collective-permute-done | bytes 786464 | tf_op jit(solution)/shard_map/ppermute | solution.py:602
  90.9 9.8 %collective-permute-done.12.refs_4_.refs_2_.refs_3_.refs_10_.refs_8_.refs_30_ = bf16[24,16,1024]{2,1,0:T(8,128)(2,1)S(1)} collective-permute-done((bf16[24,16,1024]{2,1,0:T(8,128)(2,1)}, bf16[24,16,1024]{2,1,0:T(8,128)(2,1)S(1)}, u32[]{:S(2)}, u32[]{:S(2)}) %collective-permute-start.12) | collective-permute-done | bytes 786464 | tf_op jit(solution)/shard_map/ppermute | solution.py:602
  105.3 9.7 %collective-permute-done.10.refs_2_ = bf16[12,64,1024]{2,1,0:T(8,128)(2,1)} collective-permute-done((bf16[12,64,1024]{2,1,0:T(8,128)(2,1)}, bf16[12,64,1024]{2,1,0:T(8,128)(2,1)}, u32[]{:S(2)}, u32[]{:S(2)}) %collective-permute-start.10) | collective-permute-done | bytes 1572896 | tf_op jit(solution)/shard_map/ppermute | solution.py:648
  119.9 5.8 %collective-permute-start.21 = (bf16[24,16,1024]{2,1,0:T(8,128)(2,1)}, bf16[24,16,1024]{2,1,0:T(8,128)(2,1)}, u32[]{:S(2)}, u32[]{:S(2)}) collective-permute-start(bf16[24,16,1024]{2,1,0:T(8,128)(2,1)} %get-tuple-element.79.refs_2_.refs_18_.refs_16_.refs_19_.refs_37_), channel_id=1, source_target_pairs={{0,4},{1,5},{2,6},{3,7},{4,8},{5,9},{6,10},{7,11},{8,12},{9,13},{1... | collective-permute-start | bytes 2359304 | tf_op jit(solution)/shard_map/ppermute | solution.py:601
  138.5 5.4 %collective-permute-start.18 = (bf16[24,16,1024]{2,1,0:T(8,128)(2,1)}, bf16[24,16,1024]{2,1,0:T(8,128)(2,1)}, u32[]{:S(2)}, u32[]{:S(2)}) collective-permute-start(bf16[24,16,1024]{2,1,0:T(8,128)(2,1)} %get-tuple-element.80.refs_8_), channel_id=1, source_target_pairs={{0,4},{1,5},{2,6},{3,7},{4,8},{5,9},{6,10},{7,11},{8,12},{9,13},{1... | collective-permute-start | bytes 2359304 | tf_op jit(solution)/shard_map/ppermute | solution.py:601
  148.5 5.4 %collective-permute-start.23 = (bf16[24,16,1024]{2,1,0:T(8,128)(2,1)}, bf16[24,16,1024]{2,1,0:T(8,128)(2,1)}, u32[]{:S(2)}, u32[]{:S(2)}) collective-permute-start(bf16[24,16,1024]{2,1,0:T(8,128)(2,1)} %get-tuple-element.84.refs_2_), channel_id=1, source_target_pairs={{0,4},{1,5},{2,6},{3,7},{4,8},{5,9},{6,10},{7,11},{8,12},{9,13},{1... | collective-permute-start | bytes 2359304 | tf_op jit(solution)/shard_map/ppermute | solution.py:601
  160.0 11.3 %convert_bitcast_fusion.refs_5_.fock_ref = bf16[6,512,1024]{2,1,0:T(8,128)(2,1)} fusion(bf16[6,512,1024]{2,1,0:T(8,128)(2,1)} %refs_0_.21, bf16[1024,1024]{1,0:T(8,128)(2,1)} %all-gather.5.cloned.1.call-done, s32[1024]{0:T(1024)S(1)} %copy-done.22), kind=kOutput, calls=%fused_computation.1 | convolution fusion | flops 6447693824 | bytes 14684160 | tf_op jit(solution)/shard_map/pac,bc->pab/dot_general | solution.py:733
  174.9 5.7 %collective-permute-start.25 = (bf16[24,16,1024]{2,1,0:T(8,128)(2,1)}, bf16[24,16,1024]{2,1,0:T(8,128)(2,1)}, u32[]{:S(2)}, u32[]{:S(2)}) collective-permute-start(bf16[24,16,1024]{2,1,0:T(8,128)(2,1)} %get-tuple-element.87.refs_6_), channel_id=1, source_target_pairs={{0,4},{1,5},{2,6},{3,7},{4,8},{5,9},{6,10},{7,11},{8,12},{9,13},{1... | collective-permute-start | bytes 2359304 | tf_op jit(solution)/shard_map/ppermute | solution.py:601
  187.9 8.7 %collective-permute-done.26.refs_10_.refs_6_.refs_12_.refs_1_ = bf16[24,16,1024]{2,1,0:T(8,128)(2,1)} collective-permute-done((bf16[24,16,1024]{2,1,0:T(8,128)(2,1)}, bf16[24,16,1024]{2,1,0:T(8,128)(2,1)}, u32[]{:S(2)}, u32[]{:S(2)}) %collective-permute-start.26) | collective-permute-done | bytes 786464 | tf_op jit(solution)/shard_map/ppermute | solution.py:602
  202.6 13.3 %collective-permute-start.27 = (bf16[24,16,1024]{2,1,0:T(8,128)(2,1)}, bf16[24,16,1024]{2,1,0:T(8,128)(2,1)}, u32[]{:S(2)}, u32[]{:S(2)}) collective-permute-start(bf16[24,16,1024]{2,1,0:T(8,128)(2,1)} %get-tuple-element.93.refs_7_), channel_id=1, source_target_pairs={{0,4},{1,5},{2,6},{3,7},{4,8},{5,9},{6,10},{7,11},{8,12},{9,13},{1... | collective-permute-start | bytes 2359304 | tf_op jit(solution)/shard_map/ppermute | solution.py:601
  219.5 5.4 %collective-permute-start.34 = (bf16[24,16,1024]{2,1,0:T(8,128)(2,1)}, bf16[24,16,1024]{2,1,0:T(8,128)(2,1)}, u32[]{:S(2)}, u32[]{:S(2)}) collective-permute-start(bf16[24,16,1024]{2,1,0:T(8,128)(2,1)} %get-tuple-element.96.refs_3_), channel_id=1, source_target_pairs={{0,4},{1,5},{2,6},{3,7},{4,8},{5,9},{6,10},{7,11},{8,12},{9,13},{1... | collective-permute-start | bytes 2359304 | tf_op jit(solution)/shard_map/ppermute | solution.py:601
  236.3 6.9 %collective-permute-start.32 = (bf16[24,16,1024]{2,1,0:T(8,128)(2,1)}, bf16[24,16,1024]{2,1,0:T(8,128)(2,1)}, u32[]{:S(2)}, u32[]{:S(2)}) collective-permute-start(bf16[24,16,1024]{2,1,0:T(8,128)(2,1)} %get-tuple-element.98.refs_20_), channel_id=1, source_target_pairs={{0,4},{1,5},{2,6},{3,7},{4,8},{5,9},{6,10},{7,11},{8,12},{9,13},{1... | collective-permute-start | bytes 2359304 | tf_op jit(solution)/shard_map/ppermute | solution.py:601
  243.2 6.2 %pair_sums_0_0.1.refs_6_.refs_21_ = f32[2,96,192]{2,1,0:T(8,128)} custom-call(bf16[24,16,1024]{2,1,0:T(8,128)(2,1)} %collective-permute-done.5.refs_3_.refs_1_.refs_0_.refs_18_, bf16[24,16,1024]{2,1,0:T(8,128)(2,1)} %get-tuple-element.97.refs_7_.refs_1_, bf16[24,16,1024]{2,1,0:T(8,128)(2,1)} %move_own.2.refs_2_.refs_0_.refs_3_.refs_15_, ...), custom_call_target="tpu_custom_call" | custom-call | flops 1509949440 | bytes 7864320 | tf_op jit(solution)/shard_map/pair_sums_0_0/pallas_call | solution.py:247
  253.4 6.2 %pair_sums_0_1.1.refs_6_.refs_21_ = f32[2,96,192]{2,1,0:T(8,128)} custom-call(bf16[24,16,1024]{2,1,0:T(8,128)(2,1)} %move_own.2.refs_2_.refs_0_.refs_3_.refs_15_, bf16[24,16,1024]{2,1,0:T(8,128)(2,1)} %get-tuple-element.97.refs_7_.refs_1_, bf16[24,16,1024]{2,1,0:T(8,128)(2,1)} %copy-done.2, ...), custom_call_target="tpu_custom_call" | custom-call | flops 1509949440 | bytes 7864320 | tf_op jit(solution)/shard_map/pair_sums_0_1/pallas_call | solution.py:247
  259.6 5.9 %collective-permute-done.33.refs_3_.refs_5_.refs_14_.refs_8_.refs_0_.refs_4_.refs_24_ = bf16[24,16,1024]{2,1,0:T(8,128)(2,1)S(1)} collective-permute-done((bf16[24,16,1024]{2,1,0:T(8,128)(2,1)}, bf16[24,16,1024]{2,1,0:T(8,128)(2,1)S(1)}, u32[]{:S(2)}, u32[]{:S(2)}) %collective-permute-start.33) | collective-permute-done | bytes 786464 | tf_op jit(solution)/shard_map/ppermute | solution.py:602
  270.4 6.2 %pair_sums_0_2.1.refs_6_.refs_16_ = f32[2,96,192]{2,1,0:T(8,128)} custom-call(bf16[24,16,1024]{2,1,0:T(8,128)(2,1)} %copy-done.2, bf16[24,16,1024]{2,1,0:T(8,128)(2,1)} %get-tuple-element.97.refs_7_.refs_1_, bf16[24,16,1024]{2,1,0:T(8,128)(2,1)} %collective-permute-done.19.refs_4_.refs_2_, bf16[24,16,1024]{2,1,0:T(8,128)(2,1)} %move_own.2.refs_2_.refs_0_.refs_3_.refs_15_, ...), custom_call_target="tpu_custom_call" | custom-call | flops 1509949440 | bytes 7864320 | tf_op jit(solution)/shard_map/pair_sums_0_2/pallas_call | solution.py:247
  276.6 5.8 %collective-permute-done.39.refs_3_.refs_5_.refs_11_.refs_31_ = bf16[24,16,1024]{2,1,0:T(8,128)(2,1)} collective-permute-done((bf16[24,16,1024]{2,1,0:T(8,128)(2,1)}, bf16[24,16,1024]{2,1,0:T(8,128)(2,1)}, u32[]{:S(2)}, u32[]{:S(2)}) %collective-permute-start.39) | collective-permute-done | bytes 786464 | tf_op jit(solution)/shard_map/ppermute | solution.py:602
  288.3 10.9 %collective-permute-done.36.refs_3_.refs_0_ = bf16[24,16,1024]{2,1,0:T(8,128)(2,1)S(1)} collective-permute-done((bf16[24,16,1024]{2,1,0:T(8,128)(2,1)}, bf16[24,16,1024]{2,1,0:T(8,128)(2,1)S(1)}, u32[]{:S(2)}, u32[]{:S(2)}) %collective-permute-start.36) | collective-permute-done | bytes 786464 | tf_op jit(solution)/shard_map/ppermute | solution.py:602
  331.1 14.2 %collective-permute-start.49 = (f32[96,128]{1,0:T(8,128)S(1)}, f32[96,128]{1,0:T(8,128)S(1)}, u32[]{:S(2)}, u32[]{:S(2)}) collective-permute-start(f32[96,128]{1,0:T(8,128)S(1)} %add_add_fusion.1), channel_id=1, source_target_pairs={{0,8},{1,9},{2,10},{3,11},{4,12},{5,13},{6,14},{7,15},{8,0},{9,1},... | collective-permute-start | bytes 147464 | tf_op jit(solution)/shard_map/ppermute | solution.py:759
  350.0 9.9 %ladder.1 = (bf16[6,48,1024]{2,1,0:T(8,128)(2,1)}, bf16[6,48,1024]{2,1,0:T(8,128)(2,1)}, bf16[6,48,1024]{2,1,0:T(8,128)(2,1)}, bf16[6,48,1024]{2,1,0:T(8,128)(2,...) custom-call(bf16[24,16,1024]{2,1,0:T(8,128)(2,1)} %collective-permut, ...), custom_call_target="tpu_custom_call" | custom-call | flops 6643777536 | bytes 37748736 | tf_op jit(solution)/shard_map/ladder/pallas_call | solution.py:389
  366.1 18.6 %collective-permute-done.53.refs_1_ = bf16[6,48,1024]{2,1,0:T(8,128)(2,1)} collective-permute-done((bf16[6,48,1024]{2,1,0:T(8,128)(2,1)}, bf16[6,48,1024]{2,1,0:T(8,128)(2,1)}, u32[]{:S(2)}, u32[]{:S(2)}) %collective-permute-start.53) | collective-permute-done | bytes 589856 | tf_op jit(solution)/shard_map/ppermute | solution.py:772
  386.3 10.2 %collective-permute-done.55.refs_1_ = bf16[6,48,1024]{2,1,0:T(8,128)(2,1)} collective-permute-done((bf16[6,48,1024]{2,1,0:T(8,128)(2,1)}, bf16[6,48,1024]{2,1,0:T(8,128)(2,1)}, u32[]{:S(2)}, u32[]{:S(2)}) %collective-permute-start.55) | collective-permute-done | bytes 589856 | tf_op jit(solution)/shard_map/ppermute | solution.py:772
  416.6 10.4 %collective-permute-done.58.refs_1_ = bf16[6,48,1024]{2,1,0:T(8,128)(2,1)} collective-permute-done((bf16[6,48,1024]{2,1,0:T(8,128)(2,1)}, bf16[6,48,1024]{2,1,0:T(8,128)(2,1)}, u32[]{:S(2)}, u32[]{:S(2)}) %collective-permute-start.58) | collective-permute-done | bytes 589856 | tf_op jit(solution)/shard_map/ppermute | solution.py:772
  (215 shorter events, 218.9 us)
Async XLA Ops:
  6.5 69.1 %all-gather.3.cloned.1.call-start = ((), (), s32[]{:S(2)}) async-start(), calls=%async_computation | async-start | bytes 1114112 | tf_op jit(solution)/shard_map/all_gather | solution.py:730
  13.3 146.7 %all-gather.5.cloned.1.call-start = ((), (), s32[]{:S(2)}) async-start(), calls=%async_computation.1 | async-start | bytes 3145728 | tf_op jit(solution)/shard_map/all_gather | solution.py:731
  41.1 84.6 %collective-permute-start.17 = (bf16[6,2,128,1024]{3,2,1,0:T(8,128)(2,1)}, bf16[6,2,128,1024]{3,2,1,0:T(8,128)(2,1)}, u32[]{:S(2)}, u32[]{:S(2)}) collective-permute-start(bf16[6,2,128,1024]{3,2,1,0:T(8,128)(2,1)} %move_core_0.1.refs_5_), channel_id=1, source_target_pairs={{0,1},{1,0},{2,3},{3,2},{4,5},{5,4},{6,7},{7,6},{8,9},{9,8},{10,11... | collective-permute-start | bytes 9437192 | tf_op jit(solution)/shard_map/ppermute | solution.py:659
  49.9 33.1 %collective-permute-start.14 = (bf16[24,16,1024]{2,1,0:T(8,128)(2,1)}, bf16[24,16,1024]{2,1,0:T(8,128)(2,1)}, u32[]{:S(2)}, u32[]{:S(2)}) collective-permute-start(bf16[24,16,1024]{2,1,0:T(8,128)(2,1)} %move_own.3.refs_1_.refs_6_.refs_4_.refs_7_.refs_22_), channel_id=1, source_target_pairs={{4,0},{5,1},{6,2},{7,3},{8,4},{9,5},{10,6},{11,7},{12,8},{13,9},{1... | collective-permute-start | bytes 2359304 | tf_op jit(solution)/shard_map/ppermute | solution.py:602
  79.4 35.5 %collective-permute-start.10 = (bf16[12,64,1024]{2,1,0:T(8,128)(2,1)}, bf16[12,64,1024]{2,1,0:T(8,128)(2,1)}, u32[]{:S(2)}, u32[]{:S(2)}) collective-permute-start(bf16[12,64,1024]{2,1,0:T(8,128)(2,1)} %move_across_4.1.refs_4_), channel_id=1, source_target_pairs={{0,2},{1,3},{2,0},{3,1},{4,6},{5,7},{6,4},{7,5},{8,10},{9,11},{10,... | collective-permute-start | bytes 4718600 | tf_op jit(solution)/shard_map/ppermute | solution.py:648
  89.6 38.4 %collective-permute-start.16 = (bf16[24,16,1024]{2,1,0:T(8,128)(2,1)}, bf16[24,16,1024]{2,1,0:T(8,128)(2,1)}, u32[]{:S(2)}, u32[]{:S(2)}) collective-permute-start(bf16[24,16,1024]{2,1,0:T(8,128)(2,1)} %get-tuple-element.78), channel_id=1, source_target_pairs={{4,0},{5,1},{6,2},{7,3},{8,4},{9,5},{10,6},{11,7},{12,8},{13,9},{1... | collective-permute-start | bytes 2359304 | tf_op jit(solution)/shard_map/ppermute | solution.py:602
  137.0 46.1 %collective-permute-start.20 = (bf16[12,48,1024]{2,1,0:T(8,128)(2,1)}, bf16[12,48,1024]{2,1,0:T(8,128)(2,1)}, u32[]{:S(2)}, u32[]{:S(2)}) collective-permute-start(bf16[12,48,1024]{2,1,0:T(8,128)(2,1)} %move_across_5.1.refs_5_), channel_id=1, source_target_pairs={{0,2},{1,3},{2,0},{3,1},{4,6},{5,7},{6,4},{7,5},{8,10},{9,11},{10,... | collective-permute-start | bytes 3538952 | tf_op jit(solution)/shard_map/ppermute | solution.py:648
  138.5 32.8 %collective-permute-start.18 = (bf16[24,16,1024]{2,1,0:T(8,128)(2,1)}, bf16[24,16,1024]{2,1,0:T(8,128)(2,1)}, u32[]{:S(2)}, u32[]{:S(2)}) collective-permute-start(bf16[24,16,1024]{2,1,0:T(8,128)(2,1)} %get-tuple-element.80.refs_8_), channel_id=1, source_target_pairs={{0,4},{1,5},{2,6},{3,7},{4,8},{5,9},{6,10},{7,11},{8,12},{9,13},{1... | collective-permute-start | bytes 2359304 | tf_op jit(solution)/shard_map/ppermute | solution.py:601
  148.5 32.1 %collective-permute-start.23 = (bf16[24,16,1024]{2,1,0:T(8,128)(2,1)}, bf16[24,16,1024]{2,1,0:T(8,128)(2,1)}, u32[]{:S(2)}, u32[]{:S(2)}) collective-permute-start(bf16[24,16,1024]{2,1,0:T(8,128)(2,1)} %get-tuple-element.84.refs_2_), channel_id=1, source_target_pairs={{0,4},{1,5},{2,6},{3,7},{4,8},{5,9},{6,10},{7,11},{8,12},{9,13},{1... | collective-permute-start | bytes 2359304 | tf_op jit(solution)/shard_map/ppermute | solution.py:601
  158.5 66.5 %collective-permute-start.29 = (bf16[12,80,1024]{2,1,0:T(8,128)(2,1)}, bf16[12,80,1024]{2,1,0:T(8,128)(2,1)}, u32[]{:S(2)}, u32[]{:S(2)}) collective-permute-start(bf16[12,80,1024]{2,1,0:T(8,128)(2,1)} %move_across_0.1.refs_6_), channel_id=1, source_target_pairs={{0,2},{1,3},{2,0},{3,1},{4,6},{5,7},{6,4},{7,5},{8,10},{9,11},{10,... | collective-permute-start | bytes 5898248 | tf_op jit(solution)/shard_map/ppermute | solution.py:648
  181.8 34.1 %collective-permute-start.31 = (bf16[24,16,1024]{2,1,0:T(8,128)(2,1)}, bf16[24,16,1024]{2,1,0:T(8,128)(2,1)}, u32[]{:S(2)}, u32[]{:S(2)}) collective-permute-start(bf16[24,16,1024]{2,1,0:T(8,128)(2,1)} %get-tuple-element.95), channel_id=1, source_target_pairs={{4,0},{5,1},{6,2},{7,3},{8,4},{9,5},{10,6},{11,7},{20,16},{21,17},... | collective-permute-start | bytes 2359304 | tf_op jit(solution)/shard_map/ppermute | solution.py:602
  183.1 32.8 %collective-permute-start.30 = (bf16[24,16,1024]{2,1,0:T(8,128)(2,1)}, bf16[24,16,1024]{2,1,0:T(8,128)(2,1)}, u32[]{:S(2)}, u32[]{:S(2)}) collective-permute-start(bf16[24,16,1024]{2,1,0:T(8,128)(2,1)} %get-tuple-element.88.refs_3_), channel_id=1, source_target_pairs={{4,8},{5,9},{6,10},{7,11},{8,12},{9,13},{10,14},{11,15},{20,24},{2... | collective-permute-start | bytes 2359304 | tf_op jit(solution)/shard_map/ppermute | solution.py:601
  201.3 30.4 %collective-permute-start.28 = (bf16[24,16,1024]{2,1,0:T(8,128)(2,1)}, bf16[24,16,1024]{2,1,0:T(8,128)(2,1)S(1)}, u32[]{:S(2)}, u32[]{:S(2)}) collective-permute-start(bf16[24,16,1024]{2,1,0:T(8,128)(2,1)} %get-tuple-element.94), channel_id=1, source_target_pairs={{4,0},{5,1},{6,2},{7,3},{8,4},{9,5},{10,6},{11,7},{12,8},{13,9},{1... | collective-permute-start | bytes 2359304 | tf_op jit(solution)/shard_map/ppermute | solution.py:602
  218.2 31.1 %collective-permute-start.35 = (bf16[24,16,1024]{2,1,0:T(8,128)(2,1)}, bf16[24,16,1024]{2,1,0:T(8,128)(2,1)}, u32[]{:S(2)}, u32[]{:S(2)}) collective-permute-start(bf16[24,16,1024]{2,1,0:T(8,128)(2,1)} %get-tuple-element.104), channel_id=1, source_target_pairs={{4,0},{5,1},{6,2},{7,3},{8,4},{9,5},{10,6},{11,7},{12,8},{13,9},{1... | collective-permute-start | bytes 2359304 | tf_op jit(solution)/shard_map/ppermute | solution.py:602
  219.5 29.8 %collective-permute-start.34 = (bf16[24,16,1024]{2,1,0:T(8,128)(2,1)}, bf16[24,16,1024]{2,1,0:T(8,128)(2,1)}, u32[]{:S(2)}, u32[]{:S(2)}) collective-permute-start(bf16[24,16,1024]{2,1,0:T(8,128)(2,1)} %get-tuple-element.96.refs_3_), channel_id=1, source_target_pairs={{0,4},{1,5},{2,6},{3,7},{4,8},{5,9},{6,10},{7,11},{8,12},{9,13},{1... | collective-permute-start | bytes 2359304 | tf_op jit(solution)/shard_map/ppermute | solution.py:601
  235.0 30.5 %collective-permute-start.33 = (bf16[24,16,1024]{2,1,0:T(8,128)(2,1)}, bf16[24,16,1024]{2,1,0:T(8,128)(2,1)S(1)}, u32[]{:S(2)}, u32[]{:S(2)}) collective-permute-start(bf16[24,16,1024]{2,1,0:T(8,128)(2,1)} %get-tuple-element.99), channel_id=1, source_target_pairs={{4,0},{5,1},{6,2},{7,3},{8,4},{9,5},{10,6},{11,7},{12,8},{13,9},{1... | collective-permute-start | bytes 2359304 | tf_op jit(solution)/shard_map/ppermute | solution.py:602
  250.6 31.9 %collective-permute-start.39 = (bf16[24,16,1024]{2,1,0:T(8,128)(2,1)}, bf16[24,16,1024]{2,1,0:T(8,128)(2,1)}, u32[]{:S(2)}, u32[]{:S(2)}) collective-permute-start(bf16[24,16,1024]{2,1,0:T(8,128)(2,1)} %get-tuple-element.108), channel_id=1, source_target_pairs={{4,0},{5,1},{6,2},{7,3},{8,4},{9,5},{10,6},{11,7},{20,16},{21,17},... | collective-permute-start | bytes 2359304 | tf_op jit(solution)/shard_map/ppermute | solution.py:602
  251.9 30.6 %collective-permute-start.38 = (bf16[24,16,1024]{2,1,0:T(8,128)(2,1)}, bf16[24,16,1024]{2,1,0:T(8,128)(2,1)}, u32[]{:S(2)}, u32[]{:S(2)}) collective-permute-start(bf16[24,16,1024]{2,1,0:T(8,128)(2,1)} %get-tuple-element.105.refs_20_), channel_id=1, source_target_pairs={{4,8},{5,9},{6,10},{7,11},{8,12},{9,13},{10,14},{11,15},{20,24},{2... | collective-permute-start | bytes 2359304 | tf_op jit(solution)/shard_map/ppermute | solution.py:601
  267.5 31.6 %collective-permute-start.36 = (bf16[24,16,1024]{2,1,0:T(8,128)(2,1)}, bf16[24,16,1024]{2,1,0:T(8,128)(2,1)S(1)}, u32[]{:S(2)}, u32[]{:S(2)}) collective-permute-start(bf16[24,16,1024]{2,1,0:T(8,128)(2,1)} %get-tuple-element.106), channel_id=1, source_target_pairs={{4,0},{5,1},{6,2},{7,3},{8,4},{9,5},{10,6},{11,7},{20,16},{21,17},... | collective-permute-start | bytes 2359304 | tf_op jit(solution)/shard_map/ppermute | solution.py:602
  268.8 30.3 %collective-permute-start.37 = (bf16[24,16,1024]{2,1,0:T(8,128)(2,1)}, bf16[24,16,1024]{2,1,0:T(8,128)(2,1)}, u32[]{:S(2)}, u32[]{:S(2)}) collective-permute-start(bf16[24,16,1024]{2,1,0:T(8,128)(2,1)} %get-tuple-element.107.refs_20_), channel_id=1, source_target_pairs={{4,8},{5,9},{6,10},{7,11},{8,12},{9,13},{10,14},{11,15},{20,24},{2... | collective-permute-start | bytes 2359304 | tf_op jit(solution)/shard_map/ppermute | solution.py:601
  359.9 37.9 %collective-permute-start.51 = (bf16[6,80,1024]{2,1,0:T(8,128)(2,1)}, bf16[6,80,1024]{2,1,0:T(8,128)(2,1)}, u32[]{:S(2)}, u32[]{:S(2)}) collective-permute-start(bf16[6,80,1024]{2,1,0:T(8,128)(2,1)} %get-tuple-element.116), channel_id=1, source_target_pairs={{0,1},{1,0},{2,3},{3,2},{4,5},{5,4},{6,7},{7,6},{8,9},{9,8},{10,11... | collective-permute-start | bytes 2949128 | tf_op jit(solution)/shard_map/ppermute | solution.py:775
  363.5 33.0 %collective-permute-start.55 = (bf16[6,48,1024]{2,1,0:T(8,128)(2,1)}, bf16[6,48,1024]{2,1,0:T(8,128)(2,1)}, u32[]{:S(2)}, u32[]{:S(2)}) collective-permute-start(bf16[6,48,1024]{2,1,0:T(8,128)(2,1)} %get-tuple-element.120), channel_id=1, source_target_pairs={{4,3},{5,2},{6,1},{7,0},{8,15},{9,14},{10,13},{11,12},{20,19},{21,... | collective-permute-start | bytes 1769480 | tf_op jit(solution)/shard_map/ppermute | solution.py:772
  364.8 64.8 %collective-permute-start.59 = (bf16[6,80,1024]{2,1,0:T(8,128)(2,1)}, bf16[6,80,1024]{2,1,0:T(8,128)(2,1)}, u32[]{:S(2)}, u32[]{:S(2)}) collective-permute-start(bf16[6,80,1024]{2,1,0:T(8,128)(2,1)} %get-tuple-element.125), channel_id=1, source_target_pairs={{0,2},{1,3},{2,0},{3,1},{4,6},{5,7},{6,4},{7,5},{8,10},{9,11},{10,... | collective-permute-start | bytes 2949128 | tf_op jit(solution)/shard_map/ppermute | solution.py:775
  384.7 50.5 %collective-permute-start.60 = (bf16[6,80,1024]{2,1,0:T(8,128)(2,1)}, bf16[6,80,1024]{2,1,0:T(8,128)(2,1)}, u32[]{:S(2)}, u32[]{:S(2)}) collective-permute-start(bf16[6,80,1024]{2,1,0:T(8,128)(2,1)} %get-tuple-element.126), channel_id=1, source_target_pairs={{0,3},{1,2},{2,1},{3,0},{4,7},{5,6},{6,5},{7,4},{8,11},{9,10},{10,... | collective-permute-start | bytes 2949128 | tf_op jit(solution)/shard_map/ppermute | solution.py:775
  (62 other events, 918.5 us)
Sparse Core Ops, SparseCore 0:
  13.4 41.1 all-gather.2
  80.7 32.8 all-gather.4

commit v5 on v4

--- a/solution.py
+++ b/solution.py
@@ -653,27 +653,39 @@
         found = done_with(move(operands, [full] * (group[1] - group[0]), moves, f"move_own_{group[0]}"))
         found_in.update(zip(range(*group), found))
 
-    def send_core(source, first):
+    def send_core(source, first, after=()):
         shape = (pair_dev, 2, (CHUNKS - first) * CHUNK, width)
-        (core,) = done_with(move(in_turn([source]), [shape], core_moves(0, (first, CHUNKS), 0), f"move_core_{first}"))
+        (core,) = done_with(move(in_turn([source, *after]), [shape], core_moves(0, (first, CHUNKS), 0), f"move_core_{first}"))
         return lax.ppermute(core, "blk", inner_perm(1))
 
     int_groups = ((WIDE, CHUNKS), (0, WIDE))
     sent = done_with(move([amplitudes], [(pair_dev, CHUNK, width)] * len(pieces), pieces, "move_first"))
     sent = [lax.ppermute(part, "blk", inner_perm(flips[n % len(flips)])) for n, part in enumerate(sent)]
-    core = send_core(amplitudes, core_first)
-    for chunk in range(core_first):
+    core = send_core(amplitudes, core_first, sent[2:3])
+    int_core = send_core(integrals, 0)
+
+    def first_chunk(chunk):
         parts = sent[len(flips) * chunk : len(flips) * (chunk + 1)]
         moves = [(0, 0, rows_of(chunk), 0, slice(0, pair_dev))]
         for n, flip in enumerate(flips):
             moves.append((1 + n, None, slice(None), 0, slice(flip * pair_dev, (flip + 1) * pair_dev)))
         (own[chunk],) = done_with(move(in_turn([amplitudes] + parts), [full], moves, "move_own"))
         rounds(chunk)
-        if chunk == 0:
-            across = send_across(amplitudes, core, core_first, groups[0])
-    int_core = send_core(integrals, 0)
+
+    first_chunk(0)
+    packed = done_with(
+        move(
+            in_turn([amplitudes, core] + sent[len(flips) : len(flips) + 2]),
+            [across_shape(group) for group in groups],
+            [one for n, group in enumerate(groups) for one in across_moves(0, 1, core_first, group, pair_dev, n)],
+            "move_across",
+        )
+    )
+    acrosses = [lax.ppermute(part, "blk", inner_perm(2)) for part in packed]
+    first_chunk(1)
+    across = acrosses[0]
     assemble(amplitudes, core, across, core_first, groups[0], own, arrived(0))
-    across = send_across(amplitudes, core, core_first, groups[1])
+    across = acrosses[1]
     rounds(2, after=beside)
     rounds(3)
     assemble(amplitudes, core, across, core_first, groups[1], own, arrived(2))

time: 448 us -> 440 us (0.982)
  waiting for transfers between devices: 136 us -> 123 us
  starting transfers between devices: 139 us -> 145 us
    ppermute x4 -> x2, waiting for transfers between devices: 9.66 us -> 0.01 us  [send_across(): return lax.ppermute(across, 'blk', inner_perm(2))]
    ppermute x16, waiting for transfers between devices: 61.6 us -> 53.8 us  [line_round(): lax.ppermute(sends[1], 'blk', plane_perm(-1, PLANES - 1 - last, PLANES -...]
    ppermute x0 -> x2, waiting for transfers between devices: none -> 5.19 us  [line_exchanges(): acrosses = [lax.ppermute(part, 'blk', inner_perm(2)) for part in packed]]
    pallas_call x13 -> x12, Pallas kernels: 37 us -> 35.3 us  [move(): return list(call(*operands))]
where the time goes in v5:
time: 440 us; the launch traced here: 437 us
  starting transfers between devices  145 us (33%)
  Pallas kernels  128 us (29%)
  waiting for transfers between devices  123 us (28%)
  between operations  14.3 us (3%)
  matrix products  11.3 us (3%)
  other arithmetic  7.93 us (2%)
  local copies, waits for them, and re-layouts  7.5 us (2%)
    ppermute x16, starting transfers between devices, line_round(): got[0][step] = lax.ppermute(sends[0], 'blk', plane_perm(1, first, last))  75.6 us
    ppermute x16, waiting for transfers between devices, line_round(): lax.ppermute(sends[1], 'blk', plane_perm(-1, PLANES - 1 - last, PLANES -...  53.8 us
    ppermute x4, waiting for transfers between devices, line_plan(): outside[flip] = lax.ppermute(found[INNER + flip], 'blk', outward_perm(flip))  41.9 us
    pallas_call x12, Pallas kernels, move(): return list(call(*operands))  35.3 us
    pallas_call x9, Pallas kernels, add_pair_sums(): pl.pallas_call(functools.partial(pair_kernel, table, near_too, own_too, p...  34.8 us
    pallas_call x13, Pallas kernels, pick(): pl.pallas_call(functools.partial(pick_kernel, tables), out_shape=[jax.Sha...  24.5 us
    ppermute x6, starting transfers between devices, line_plan(): lax.ppermute(summed, ('rep', 'blk'), [(r * count + i, (r ^ rep) * count +...  24 us
    pallas_call x8, Pallas kernels, add_and_scale(): pl.pallas_call(functools.partial(scale_kernel, flip, first, len(pieces)),...  22.9 us
  transfers between devices with their start and end apart: 63, of which 26 were waited for; matrix products, arithmetic and copies ran while one was open for 4% of the time, Pallas kernels for 25%

profile of v5, /device:TPU:0, one launch (start us, length us, event | category | flops | bytes accessed | tf_op | source)
XLA Modules:
  0.0 437.3 jit_solution(8759493715169286130)
XLA Ops:
  52.8 9.7 %collective-permute-done.9.refs_4_.refs_2_.refs_0_.refs_16_ = bf16[24,16,1024]{2,1,0:T(8,128)(2,1)S(1)} collective-permute-done((bf16[24,16,1024]{2,1,0:T(8,128)(2,1)}, bf16[24,16,1024]{2,1,0:T(8,128)(2,1)S(1)}, u32[]{:S(2)}, u32[]{:S(2)}) %collective-permute-start.9) | collective-permute-done | bytes 786464 | tf_op jit(solution)/shard_map/ppermute | solution.py:602
  87.9 8.4 %collective-permute-done.12.refs_4_.refs_2_.refs_3_.refs_10_.refs_8_.refs_30_ = bf16[24,16,1024]{2,1,0:T(8,128)(2,1)S(1)} collective-permute-done((bf16[24,16,1024]{2,1,0:T(8,128)(2,1)}, bf16[24,16,1024]{2,1,0:T(8,128)(2,1)S(1)}, u32[]{:S(2)}, u32[]{:S(2)}) %collective-permute-start.12) | collective-permute-done | bytes 786464 | tf_op jit(solution)/shard_map/ppermute | solution.py:602
  112.4 5.8 %collective-permute-start.21 = (bf16[24,16,1024]{2,1,0:T(8,128)(2,1)}, bf16[24,16,1024]{2,1,0:T(8,128)(2,1)}, u32[]{:S(2)}, u32[]{:S(2)}) collective-permute-start(bf16[24,16,1024]{2,1,0:T(8,128)(2,1)} %get-tuple-element.83.refs_2_.refs_18_.refs_16_.refs_19_.refs_37_), channel_id=1, source_target_pairs={{0,4},{1,5},{2,6},{3,7},{4,8},{5,9},{6,10},{7,11},{8,12},{9,13},{1... | collective-permute-start | bytes 2359304 | tf_op jit(solution)/shard_map/ppermute | solution.py:601
  124.1 5.3 %subtract_divide_fusion.refs_5_.inverse_ref = f32[6,512,1024]{2,1,0:T(8,128)} fusion(f32[1024]{0:T(1024)S(1)} %copy-done.16, f32[6,512]{1,0:T(8,128)S(1)} %broadcast_subtract_fusion), kind=kLoop, calls=%fused_computation | loop fusion | flops 6291456 | bytes 12599296 | tf_op jit(solution)/shard_map/div | solution.py:757
  131.0 5.5 %collective-permute-start.18 = (bf16[24,16,1024]{2,1,0:T(8,128)(2,1)}, bf16[24,16,1024]{2,1,0:T(8,128)(2,1)}, u32[]{:S(2)}, u32[]{:S(2)}) collective-permute-start(bf16[24,16,1024]{2,1,0:T(8,128)(2,1)} %get-tuple-element.84.refs_8_), channel_id=1, source_target_pairs={{0,4},{1,5},{2,6},{3,7},{4,8},{5,9},{6,10},{7,11},{8,12},{9,13},{1... | collective-permute-start | bytes 2359304 | tf_op jit(solution)/shard_map/ppermute | solution.py:601
  141.1 5.4 %collective-permute-start.23 = (bf16[24,16,1024]{2,1,0:T(8,128)(2,1)}, bf16[24,16,1024]{2,1,0:T(8,128)(2,1)}, u32[]{:S(2)}, u32[]{:S(2)}) collective-permute-start(bf16[24,16,1024]{2,1,0:T(8,128)(2,1)} %get-tuple-element.88.refs_2_), channel_id=1, source_target_pairs={{0,4},{1,5},{2,6},{3,7},{4,8},{5,9},{6,10},{7,11},{8,12},{9,13},{1... | collective-permute-start | bytes 2359304 | tf_op jit(solution)/shard_map/ppermute | solution.py:601
  152.5 11.3 %convert_bitcast_fusion.refs_5_.fock_ref = bf16[6,512,1024]{2,1,0:T(8,128)(2,1)} fusion(bf16[6,512,1024]{2,1,0:T(8,128)(2,1)} %refs_0_.19, bf16[1024,1024]{1,0:T(8,128)(2,1)} %all-gather.5.cloned.1.call-done, s32[1024]{0:T(1024)S(1)} %copy-done.22), kind=kOutput, calls=%fused_computation.1 | convolution fusion | flops 6447693824 | bytes 14684160 | tf_op jit(solution)/shard_map/pac,bc->pab/dot_general | solution.py:745
  167.5 5.7 %collective-permute-start.25 = (bf16[24,16,1024]{2,1,0:T(8,128)(2,1)}, bf16[24,16,1024]{2,1,0:T(8,128)(2,1)}, u32[]{:S(2)}, u32[]{:S(2)}) collective-permute-start(bf16[24,16,1024]{2,1,0:T(8,128)(2,1)} %get-tuple-element.91.refs_6_), channel_id=1, source_target_pairs={{0,4},{1,5},{2,6},{3,7},{4,8},{5,9},{6,10},{7,11},{8,12},{9,13},{1... | collective-permute-start | bytes 2359304 | tf_op jit(solution)/shard_map/ppermute | solution.py:601
  180.4 7.8 %collective-permute-done.26.refs_10_.refs_6_.refs_12_.refs_1_ = bf16[24,16,1024]{2,1,0:T(8,128)(2,1)} collective-permute-done((bf16[24,16,1024]{2,1,0:T(8,128)(2,1)}, bf16[24,16,1024]{2,1,0:T(8,128)(2,1)}, u32[]{:S(2)}, u32[]{:S(2)}) %collective-permute-start.26) | collective-permute-done | bytes 786464 | tf_op jit(solution)/shard_map/ppermute | solution.py:602
  194.3 13.7 %collective-permute-start.27 = (bf16[24,16,1024]{2,1,0:T(8,128)(2,1)}, bf16[24,16,1024]{2,1,0:T(8,128)(2,1)}, u32[]{:S(2)}, u32[]{:S(2)}) collective-permute-start(bf16[24,16,1024]{2,1,0:T(8,128)(2,1)} %get-tuple-element.97.refs_7_), channel_id=1, source_target_pairs={{0,4},{1,5},{2,6},{3,7},{4,8},{5,9},{6,10},{7,11},{8,12},{9,13},{1... | collective-permute-start | bytes 2359304 | tf_op jit(solution)/shard_map/ppermute | solution.py:601
  211.6 5.4 %collective-permute-start.34 = (bf16[24,16,1024]{2,1,0:T(8,128)(2,1)}, bf16[24,16,1024]{2,1,0:T(8,128)(2,1)}, u32[]{:S(2)}, u32[]{:S(2)}) collective-permute-start(bf16[24,16,1024]{2,1,0:T(8,128)(2,1)} %get-tuple-element.100.refs_3_), channel_id=1, source_target_pairs={{0,4},{1,5},{2,6},{3,7},{4,8},{5,9},{6,10},{7,11},{8,12},{9,13},{1... | collective-permute-start | bytes 2359304 | tf_op jit(solution)/shard_map/ppermute | solution.py:601
  228.3 6.9 %collective-permute-start.32 = (bf16[24,16,1024]{2,1,0:T(8,128)(2,1)}, bf16[24,16,1024]{2,1,0:T(8,128)(2,1)}, u32[]{:S(2)}, u32[]{:S(2)}) collective-permute-start(bf16[24,16,1024]{2,1,0:T(8,128)(2,1)} %get-tuple-element.102.refs_20_), channel_id=1, source_target_pairs={{0,4},{1,5},{2,6},{3,7},{4,8},{5,9},{6,10},{7,11},{8,12},{9,13},{1... | collective-permute-start | bytes 2359304 | tf_op jit(solution)/shard_map/ppermute | solution.py:601
  235.2 6.2 %pair_sums_0_0.1.refs_6_.refs_21_ = f32[2,96,192]{2,1,0:T(8,128)} custom-call(bf16[24,16,1024]{2,1,0:T(8,128)(2,1)} %collective-permute-done.8.refs_3_.refs_1_.refs_0_.refs_18_, bf16[24,16,1024]{2,1,0:T(8,128)(2,1)} %get-tuple-element.101.refs_7_.refs_1_, bf16[24,16,1024]{2,1,0:T(8,128)(2,1)} %move_own.2.refs_4_.refs_2_.refs_0_.refs_3_.refs_15_, ...), custom_call_target="tpu_custom_call" | custom-call | flops 1509949440 | bytes 7864320 | tf_op jit(solution)/shard_map/pair_sums_0_0/pallas_call | solution.py:247
  245.4 6.2 %pair_sums_0_1.1.refs_6_.refs_21_ = f32[2,96,192]{2,1,0:T(8,128)} custom-call(bf16[24,16,1024]{2,1,0:T(8,128)(2,1)} %move_own.2.refs_4_.refs_2_.refs_0_.refs_3_.refs_15_, bf16[24,16,1024]{2,1,0:T(8,128)(2,1)} %get-tuple-element.101.refs_7_.refs_1_, bf16[24,16,1024]{2,1,0:T(8,128)(2,1)} %copy-done.2, ...), custom_call_target="tpu_custom_call" | custom-call | flops 1509949440 | bytes 7864320 | tf_op jit(solution)/shard_map/pair_sums_0_1/pallas_call | solution.py:247
  251.6 5.9 %collective-permute-done.33.refs_3_.refs_5_.refs_14_.refs_8_.refs_0_.refs_4_.refs_24_ = bf16[24,16,1024]{2,1,0:T(8,128)(2,1)S(1)} collective-permute-done((bf16[24,16,1024]{2,1,0:T(8,128)(2,1)}, bf16[24,16,1024]{2,1,0:T(8,128)(2,1)S(1)}, u32[]{:S(2)}, u32[]{:S(2)}) %collective-permute-start.33) | collective-permute-done | bytes 786464 | tf_op jit(solution)/shard_map/ppermute | solution.py:602
  262.5 6.2 %pair_sums_0_2.1.refs_6_.refs_16_ = f32[2,96,192]{2,1,0:T(8,128)} custom-call(bf16[24,16,1024]{2,1,0:T(8,128)(2,1)} %copy-done.2, bf16[24,16,1024]{2,1,0:T(8,128)(2,1)} %get-tuple-element.101.refs_7_.refs_1_, bf16[24,16,1024]{2,1,0:T(8,128)(2,1)} %collective-permute-done.19.refs_4_.refs_2_, ...), custom_call_target="tpu_custom_call" | custom-call | flops 1509949440 | bytes 7864320 | tf_op jit(solution)/shard_map/pair_sums_0_2/pallas_call | solution.py:247
  268.7 5.8 %collective-permute-done.39.refs_3_.refs_5_.refs_11_.refs_31_ = bf16[24,16,1024]{2,1,0:T(8,128)(2,1)} collective-permute-done((bf16[24,16,1024]{2,1,0:T(8,128)(2,1)}, bf16[24,16,1024]{2,1,0:T(8,128)(2,1)}, u32[]{:S(2)}, u32[]{:S(2)}) %collective-permute-start.39) | collective-permute-done | bytes 786464 | tf_op jit(solution)/shard_map/ppermute | solution.py:602
  280.4 8.8 %collective-permute-done.36.refs_3_.refs_0_ = bf16[24,16,1024]{2,1,0:T(8,128)(2,1)S(1)} collective-permute-done((bf16[24,16,1024]{2,1,0:T(8,128)(2,1)}, bf16[24,16,1024]{2,1,0:T(8,128)(2,1)S(1)}, u32[]{:S(2)}, u32[]{:S(2)}) %collective-permute-start.36) | collective-permute-done | bytes 786464 | tf_op jit(solution)/shard_map/ppermute | solution.py:602
  316.9 5.4 %collective-permute-start.50 = (f32[96,128]{1,0:T(8,128)S(1)}, f32[96,128]{1,0:T(8,128)S(1)}, u32[]{:S(2)}, u32[]{:S(2)}) collective-permute-start(f32[96,128]{1,0:T(8,128)S(1)} %add_add_fusion.1), channel_id=1, source_target_pairs={{0,12},{1,13},{2,14},{3,15},{4,8},{5,9},{6,10},{7,11},{8,4},{9,5},... | collective-permute-start | bytes 147464 | tf_op jit(solution)/shard_map/ppermute | solution.py:771
  322.2 15.2 %collective-permute-start.49 = (f32[96,128]{1,0:T(8,128)S(1)}, f32[96,128]{1,0:T(8,128)S(1)}, u32[]{:S(2)}, u32[]{:S(2)}) collective-permute-start(f32[96,128]{1,0:T(8,128)S(1)} %add_add_fusion.1), channel_id=1, source_target_pairs={{0,8},{1,9},{2,10},{3,11},{4,12},{5,13},{6,14},{7,15},{8,0},{9,1},... | collective-permute-start | bytes 147464 | tf_op jit(solution)/shard_map/ppermute | solution.py:771
  342.1 9.8 %ladder.1 = (bf16[6,48,1024]{2,1,0:T(8,128)(2,1)}, bf16[6,48,1024]{2,1,0:T(8,128)(2,1)}, bf16[6,48,1024]{2,1,0:T(8,128)(2,1)}, bf16[6,48,1024]{2,1,0:T(8,128)(2,...) custom-call(bf16[24,16,1024]{2,1,0:T(8,128)(2,1)} %collective-permut, ...), custom_call_target="tpu_custom_call" | custom-call | flops 6643777536 | bytes 37748736 | tf_op jit(solution)/shard_map/ladder/pallas_call | solution.py:389
  357.9 18.0 %collective-permute-done.53.refs_1_ = bf16[6,48,1024]{2,1,0:T(8,128)(2,1)} collective-permute-done((bf16[6,48,1024]{2,1,0:T(8,128)(2,1)}, bf16[6,48,1024]{2,1,0:T(8,128)(2,1)}, u32[]{:S(2)}, u32[]{:S(2)}) %collective-permute-start.53) | collective-permute-done | bytes 589856 | tf_op jit(solution)/shard_map/ppermute | solution.py:784
  377.5 10.2 %collective-permute-done.55.refs_1_ = bf16[6,48,1024]{2,1,0:T(8,128)(2,1)} collective-permute-done((bf16[6,48,1024]{2,1,0:T(8,128)(2,1)}, bf16[6,48,1024]{2,1,0:T(8,128)(2,1)}, u32[]{:S(2)}, u32[]{:S(2)}) %collective-permute-start.55) | collective-permute-done | bytes 589856 | tf_op jit(solution)/shard_map/ppermute | solution.py:784
  407.8 10.4 %collective-permute-done.58.refs_1_ = bf16[6,48,1024]{2,1,0:T(8,128)(2,1)} collective-permute-done((bf16[6,48,1024]{2,1,0:T(8,128)(2,1)}, bf16[6,48,1024]{2,1,0:T(8,128)(2,1)}, u32[]{:S(2)}, u32[]{:S(2)}) %collective-permute-start.58) | collective-permute-done | bytes 589856 | tf_op jit(solution)/shard_map/ppermute | solution.py:784
  (214 shorter events, 224.1 us)
Async XLA Ops:
  6.5 63.4 %all-gather.3.cloned.1.call-start = ((), (), s32[]{:S(2)}) async-start(), calls=%async_computation | async-start | bytes 1114112 | tf_op jit(solution)/shard_map/all_gather | solution.py:742
  15.6 136.9 %all-gather.5.cloned.1.call-start = ((), (), s32[]{:S(2)}) async-start(), calls=%async_computation.1 | async-start | bytes 3145728 | tf_op jit(solution)/shard_map/all_gather | solution.py:743
  19.2 98.9 %collective-permute-start.17 = (bf16[6,2,128,1024]{3,2,1,0:T(8,128)(2,1)}, bf16[6,2,128,1024]{3,2,1,0:T(8,128)(2,1)}, u32[]{:S(2)}, u32[]{:S(2)}) collective-permute-start(bf16[6,2,128,1024]{3,2,1,0:T(8,128)(2,1)} %move_core_0.1.refs_4_), channel_id=1, source_target_pairs={{0,1},{1,0},{2,3},{3,2},{4,5},{5,4},{6,7},{7,6},{8,9},{9,8},{10,11... | collective-permute-start | bytes 9437192 | tf_op jit(solution)/shard_map/ppermute | solution.py:659
  37.3 30.0 %collective-permute-start.8 = (bf16[24,16,1024]{2,1,0:T(8,128)(2,1)}, bf16[24,16,1024]{2,1,0:T(8,128)(2,1)}, u32[]{:S(2)}, u32[]{:S(2)}) collective-permute-start(bf16[24,16,1024]{2,1,0:T(8,128)(2,1)} %move_own.2.refs_4_.refs_2_.refs_0_.refs_3_.refs_15_), channel_id=1, source_target_pairs={{0,4},{1,5},{2,6},{3,7},{4,8},{5,9},{6,10},{7,11},{8,12},{9,13},{1... | collective-permute-start | bytes 2359304 | tf_op jit(solution)/shard_map/ppermute | solution.py:601
  73.7 33.7 %collective-permute-start.6 = (bf16[12,64,1024]{2,1,0:T(8,128)(2,1)}, bf16[12,64,1024]{2,1,0:T(8,128)(2,1)}, u32[]{:S(2)}, u32[]{:S(2)}) collective-permute-start(bf16[12,64,1024]{2,1,0:T(8,128)(2,1)} %get-tuple-element.73), channel_id=1, source_target_pairs={{0,2},{1,3},{2,0},{3,1},{4,6},{5,7},{6,4},{7,5},{8,10},{9,11},{10,... | collective-permute-start | bytes 4718600 | tf_op jit(solution)/shard_map/ppermute | solution.py:684
  86.6 33.9 %collective-permute-start.16 = (bf16[24,16,1024]{2,1,0:T(8,128)(2,1)}, bf16[24,16,1024]{2,1,0:T(8,128)(2,1)}, u32[]{:S(2)}, u32[]{:S(2)}) collective-permute-start(bf16[24,16,1024]{2,1,0:T(8,128)(2,1)} %get-tuple-element.82), channel_id=1, source_target_pairs={{4,0},{5,1},{6,2},{7,3},{8,4},{9,5},{10,6},{11,7},{12,8},{13,9},{1... | collective-permute-start | bytes 2359304 | tf_op jit(solution)/shard_map/ppermute | solution.py:602
  129.5 46.1 %collective-permute-start.20 = (bf16[12,48,1024]{2,1,0:T(8,128)(2,1)}, bf16[12,48,1024]{2,1,0:T(8,128)(2,1)}, u32[]{:S(2)}, u32[]{:S(2)}) collective-permute-start(bf16[12,48,1024]{2,1,0:T(8,128)(2,1)} %move_across_5.1.refs_5_), channel_id=1, source_target_pairs={{0,2},{1,3},{2,0},{3,1},{4,6},{5,7},{6,4},{7,5},{8,10},{9,11},{10,... | collective-permute-start | bytes 3538952 | tf_op jit(solution)/shard_map/ppermute | solution.py:648
  131.0 32.8 %collective-permute-start.18 = (bf16[24,16,1024]{2,1,0:T(8,128)(2,1)}, bf16[24,16,1024]{2,1,0:T(8,128)(2,1)}, u32[]{:S(2)}, u32[]{:S(2)}) collective-permute-start(bf16[24,16,1024]{2,1,0:T(8,128)(2,1)} %get-tuple-element.84.refs_8_), channel_id=1, source_target_pairs={{0,4},{1,5},{2,6},{3,7},{4,8},{5,9},{6,10},{7,11},{8,12},{9,13},{1... | collective-permute-start | bytes 2359304 | tf_op jit(solution)/shard_map/ppermute | solution.py:601
  141.1 32.1 %collective-permute-start.23 = (bf16[24,16,1024]{2,1,0:T(8,128)(2,1)}, bf16[24,16,1024]{2,1,0:T(8,128)(2,1)}, u32[]{:S(2)}, u32[]{:S(2)}) collective-permute-start(bf16[24,16,1024]{2,1,0:T(8,128)(2,1)} %get-tuple-element.88.refs_2_), channel_id=1, source_target_pairs={{0,4},{1,5},{2,6},{3,7},{4,8},{5,9},{6,10},{7,11},{8,12},{9,13},{1... | collective-permute-start | bytes 2359304 | tf_op jit(solution)/shard_map/ppermute | solution.py:601
  151.0 66.0 %collective-permute-start.29 = (bf16[12,80,1024]{2,1,0:T(8,128)(2,1)}, bf16[12,80,1024]{2,1,0:T(8,128)(2,1)}, u32[]{:S(2)}, u32[]{:S(2)}) collective-permute-start(bf16[12,80,1024]{2,1,0:T(8,128)(2,1)} %move_across_0.1.refs_6_), channel_id=1, source_target_pairs={{0,2},{1,3},{2,0},{3,1},{4,6},{5,7},{6,4},{7,5},{8,10},{9,11},{10,... | collective-permute-start | bytes 5898248 | tf_op jit(solution)/shard_map/ppermute | solution.py:648
  174.3 33.7 %collective-permute-start.31 = (bf16[24,16,1024]{2,1,0:T(8,128)(2,1)}, bf16[24,16,1024]{2,1,0:T(8,128)(2,1)}, u32[]{:S(2)}, u32[]{:S(2)}) collective-permute-start(bf16[24,16,1024]{2,1,0:T(8,128)(2,1)} %get-tuple-element.99), channel_id=1, source_target_pairs={{4,0},{5,1},{6,2},{7,3},{8,4},{9,5},{10,6},{11,7},{20,16},{21,17},... | collective-permute-start | bytes 2359304 | tf_op jit(solution)/shard_map/ppermute | solution.py:602
  175.6 32.4 %collective-permute-start.30 = (bf16[24,16,1024]{2,1,0:T(8,128)(2,1)}, bf16[24,16,1024]{2,1,0:T(8,128)(2,1)}, u32[]{:S(2)}, u32[]{:S(2)}) collective-permute-start(bf16[24,16,1024]{2,1,0:T(8,128)(2,1)} %get-tuple-element.92.refs_3_), channel_id=1, source_target_pairs={{4,8},{5,9},{6,10},{7,11},{8,12},{9,13},{10,14},{11,15},{20,24},{2... | collective-permute-start | bytes 2359304 | tf_op jit(solution)/shard_map/ppermute | solution.py:601
  193.0 30.8 %collective-permute-start.28 = (bf16[24,16,1024]{2,1,0:T(8,128)(2,1)}, bf16[24,16,1024]{2,1,0:T(8,128)(2,1)S(1)}, u32[]{:S(2)}, u32[]{:S(2)}) collective-permute-start(bf16[24,16,1024]{2,1,0:T(8,128)(2,1)} %get-tuple-element.98), channel_id=1, source_target_pairs={{4,0},{5,1},{6,2},{7,3},{8,4},{9,5},{10,6},{11,7},{12,8},{13,9},{1... | collective-permute-start | bytes 2359304 | tf_op jit(solution)/shard_map/ppermute | solution.py:602
  194.3 29.5 %collective-permute-start.27 = (bf16[24,16,1024]{2,1,0:T(8,128)(2,1)}, bf16[24,16,1024]{2,1,0:T(8,128)(2,1)}, u32[]{:S(2)}, u32[]{:S(2)}) collective-permute-start(bf16[24,16,1024]{2,1,0:T(8,128)(2,1)} %get-tuple-element.97.refs_7_), channel_id=1, source_target_pairs={{0,4},{1,5},{2,6},{3,7},{4,8},{5,9},{6,10},{7,11},{8,12},{9,13},{1... | collective-permute-start | bytes 2359304 | tf_op jit(solution)/shard_map/ppermute | solution.py:601
  210.3 31.1 %collective-permute-start.35 = (bf16[24,16,1024]{2,1,0:T(8,128)(2,1)}, bf16[24,16,1024]{2,1,0:T(8,128)(2,1)}, u32[]{:S(2)}, u32[]{:S(2)}) collective-permute-start(bf16[24,16,1024]{2,1,0:T(8,128)(2,1)} %get-tuple-element.108), channel_id=1, source_target_pairs={{4,0},{5,1},{6,2},{7,3},{8,4},{9,5},{10,6},{11,7},{12,8},{13,9},{1... | collective-permute-start | bytes 2359304 | tf_op jit(solution)/shard_map/ppermute | solution.py:602
  211.6 29.8 %collective-permute-start.34 = (bf16[24,16,1024]{2,1,0:T(8,128)(2,1)}, bf16[24,16,1024]{2,1,0:T(8,128)(2,1)}, u32[]{:S(2)}, u32[]{:S(2)}) collective-permute-start(bf16[24,16,1024]{2,1,0:T(8,128)(2,1)} %get-tuple-element.100.refs_3_), channel_id=1, source_target_pairs={{0,4},{1,5},{2,6},{3,7},{4,8},{5,9},{6,10},{7,11},{8,12},{9,13},{1... | collective-permute-start | bytes 2359304 | tf_op jit(solution)/shard_map/ppermute | solution.py:601
  227.0 30.5 %collective-permute-start.33 = (bf16[24,16,1024]{2,1,0:T(8,128)(2,1)}, bf16[24,16,1024]{2,1,0:T(8,128)(2,1)S(1)}, u32[]{:S(2)}, u32[]{:S(2)}) collective-permute-start(bf16[24,16,1024]{2,1,0:T(8,128)(2,1)} %get-tuple-element.103), channel_id=1, source_target_pairs={{4,0},{5,1},{6,2},{7,3},{8,4},{9,5},{10,6},{11,7},{12,8},{13,9},{1... | collective-permute-start | bytes 2359304 | tf_op jit(solution)/shard_map/ppermute | solution.py:602
  242.6 31.9 %collective-permute-start.39 = (bf16[24,16,1024]{2,1,0:T(8,128)(2,1)}, bf16[24,16,1024]{2,1,0:T(8,128)(2,1)}, u32[]{:S(2)}, u32[]{:S(2)}) collective-permute-start(bf16[24,16,1024]{2,1,0:T(8,128)(2,1)} %get-tuple-element.112), channel_id=1, source_target_pairs={{4,0},{5,1},{6,2},{7,3},{8,4},{9,5},{10,6},{11,7},{20,16},{21,17},... | collective-permute-start | bytes 2359304 | tf_op jit(solution)/shard_map/ppermute | solution.py:602
  243.9 30.6 %collective-permute-start.38 = (bf16[24,16,1024]{2,1,0:T(8,128)(2,1)}, bf16[24,16,1024]{2,1,0:T(8,128)(2,1)}, u32[]{:S(2)}, u32[]{:S(2)}) collective-permute-start(bf16[24,16,1024]{2,1,0:T(8,128)(2,1)} %get-tuple-element.109.refs_20_), channel_id=1, source_target_pairs={{4,8},{5,9},{6,10},{7,11},{8,12},{9,13},{10,14},{11,15},{20,24},{2... | collective-permute-start | bytes 2359304 | tf_op jit(solution)/shard_map/ppermute | solution.py:601
  259.6 29.6 %collective-permute-start.36 = (bf16[24,16,1024]{2,1,0:T(8,128)(2,1)}, bf16[24,16,1024]{2,1,0:T(8,128)(2,1)S(1)}, u32[]{:S(2)}, u32[]{:S(2)}) collective-permute-start(bf16[24,16,1024]{2,1,0:T(8,128)(2,1)} %get-tuple-element.110), channel_id=1, source_target_pairs={{4,0},{5,1},{6,2},{7,3},{8,4},{9,5},{10,6},{11,7},{20,16},{21,17},... | collective-permute-start | bytes 2359304 | tf_op jit(solution)/shard_map/ppermute | solution.py:602
  352.0 37.0 %collective-permute-start.51 = (bf16[6,80,1024]{2,1,0:T(8,128)(2,1)}, bf16[6,80,1024]{2,1,0:T(8,128)(2,1)}, u32[]{:S(2)}, u32[]{:S(2)}) collective-permute-start(bf16[6,80,1024]{2,1,0:T(8,128)(2,1)} %get-tuple-element.120), channel_id=1, source_target_pairs={{0,1},{1,0},{2,3},{3,2},{4,5},{5,4},{6,7},{7,6},{8,9},{9,8},{10,11... | collective-permute-start | bytes 2949128 | tf_op jit(solution)/shard_map/ppermute | solution.py:787
  355.6 32.2 %collective-permute-start.55 = (bf16[6,48,1024]{2,1,0:T(8,128)(2,1)}, bf16[6,48,1024]{2,1,0:T(8,128)(2,1)}, u32[]{:S(2)}, u32[]{:S(2)}) collective-permute-start(bf16[6,48,1024]{2,1,0:T(8,128)(2,1)} %get-tuple-element.124), channel_id=1, source_target_pairs={{4,3},{5,2},{6,1},{7,0},{8,15},{9,14},{10,13},{11,12},{20,19},{21,... | collective-permute-start | bytes 1769480 | tf_op jit(solution)/shard_map/ppermute | solution.py:784
  356.9 63.9 %collective-permute-start.59 = (bf16[6,80,1024]{2,1,0:T(8,128)(2,1)}, bf16[6,80,1024]{2,1,0:T(8,128)(2,1)}, u32[]{:S(2)}, u32[]{:S(2)}) collective-permute-start(bf16[6,80,1024]{2,1,0:T(8,128)(2,1)} %get-tuple-element.129), channel_id=1, source_target_pairs={{0,2},{1,3},{2,0},{3,1},{4,6},{5,7},{6,4},{7,5},{8,10},{9,11},{10,... | collective-permute-start | bytes 2949128 | tf_op jit(solution)/shard_map/ppermute | solution.py:787
  375.9 51.4 %collective-permute-start.60 = (bf16[6,80,1024]{2,1,0:T(8,128)(2,1)}, bf16[6,80,1024]{2,1,0:T(8,128)(2,1)}, u32[]{:S(2)}, u32[]{:S(2)}) collective-permute-start(bf16[6,80,1024]{2,1,0:T(8,128)(2,1)} %get-tuple-element.130), channel_id=1, source_target_pairs={{0,3},{1,2},{2,1},{3,0},{4,7},{5,6},{6,5},{7,4},{8,11},{9,10},{10,... | collective-permute-start | bytes 2949128 | tf_op jit(solution)/shard_map/ppermute | solution.py:787
  (62 other events, 946.0 us)
Sparse Core Ops, SparseCore 0:
  15.7 41.3 all-gather.2
  75.4 32.8 all-gather.4
